TPU v7x, 32 devices: a whole 2x2x4 slice. The times are simulated.
32 devices in a mesh: gx: 8 (over z, x), gy: 4 (over y, core).
Axes of the slice: x: 2, y: 2, z: 4, core: 2. Of those that a mesh axis runs over, the one named last changes fastest.
Arguments:
- density: float32 [4, 32, 64, 128], P(None, 'gx', 'gy'), may hold values from 0 to 12, as said below
- rate_table: float32 [4, 9], replicated, may hold values from 0 to 80, as said below
Outputs:
- propagated: float32 [4, 32, 64, 128], P(None, 'gx', 'gy')
- step_entries: float32 [4, 5], replicated
Inputs may be any that keep to these rules, and one draw needn't show every extreme that they name: `density`: every entry is positive. `rate_table`: all entries positive; entry r of a row is the constant cr of the steps.
All inputs are finite; a program needn't handle non-finite values.
Results may differ from a plain program's by a relative error of at most 0.0006.
Values sent between devices are 32-bit elements; how exact they have to be, the bound alone decides.
No kernel may reach another device: no remote copies, remote signals or barrier semaphores. Data moves between devices by JAX's collectives and lax.ppermute only.
A program may use at most 64 MiB of HBM per device.

v0:
```python
import functools

import jax
import jax.numpy as jnp
from jax import lax
from jax.experimental import pallas as pl
from jax.experimental.pallas import tpu as pltpu
from jax.sharding import PartitionSpec as P

tau_step = 0.01
taylor_terms = 16
squarings = 4
HIGHEST = lax.Precision.HIGHEST
REACH = 4
HALF = 2
GAP = 8


def images_kernel(
    lattice,
    place,
    rates,
    field,
    even_x,
    odd_x,
    even_y,
    odd_y,
    even_corners,
    odd_corners,
    image_one,
    image_two,
    message,
    wide,
    wide_image,
    parts,
):
    members, rows, cols, depth = field.shape
    span = cols + 2 * GAP
    first_i, first_j = place[0], place[1]
    count_i, count_j = lattice

    ends_i, ends_j = first_i + rows < count_i, first_j + cols < count_j

    def sides(even, odd, is_even, lower_inside, higher_inside):
        lower, higher = jnp.where(is_even, odd, even), jnp.where(is_even, even, odd)
        return jnp.where(lower_inside, lower, 0.0), jnp.where(higher_inside, higher, 0.0)

    wide[:, REACH : REACH + rows, GAP : GAP + cols] = field[...]
    above, below = sides(even_x[...], odd_x[...], place[2] == 0, first_i > 0, ends_i)
    wide[:, :REACH, GAP : GAP + cols] = above
    wide[:, REACH + rows :, GAP : GAP + cols] = below
    left, right = sides(even_y[...], odd_y[...], place[3] == 0, first_j > 0, ends_j)
    wide[:, REACH : REACH + rows, GAP - 2 : GAP] = left
    wide[:, REACH : REACH + rows, GAP + cols : GAP + cols + 2] = right
    upper, lower = sides(even_corners[...], odd_corners[...], place[2] == 0, first_i > 0, ends_i)
    for corners, at in ((upper, REACH - HALF), (lower, REACH + rows)):
        wide[:, at : at + HALF, GAP - 1 : GAP] = jnp.where(first_j > 0, corners[:, :, :1], 0.0)
        wide[:, at : at + HALF, GAP + cols : GAP + cols + 1] = jnp.where(ends_j, corners[:, :, 1:], 0.0)

    lane = lax.broadcasted_iota(jnp.int32, (1, depth), 1)
    amount_k = lane.astype(jnp.float32)
    above_k = jnp.where(lane < depth - 1, amount_k + 1.0, 0.0)
    inner_k = jnp.where(lane > 0, 1.0, 0.0)
    sublane = lax.broadcasted_iota(jnp.int32, (span, 1), 0)
    amount_j = (first_j - GAP + sublane).astype(jnp.float32)

    for member in range(members):
        c = [rates[member, r] for r in range(9)]
        ratio_j = amount_j / jnp.full((span, 1), c[7])
        ratio_k = amount_k / jnp.full((1, depth), c[8])
        make_u = jnp.broadcast_to(c[0] / (1.0 + ratio_j * ratio_j), (span, depth))
        make_v = c[2] / (1.0 + ratio_k * ratio_k)
        lose_v = jnp.broadcast_to(c[3] * (amount_j + 1.0), (span, depth))
        rest = make_u + make_v + (c[3] * amount_j + (c[5] + c[6]) * amount_k)

        def apply(read, row, start, size):
            i = (first_i + row).astype(jnp.float32)
            cut = slice(GAP + start, GAP + start + size)
            centre = read(row, start, size)
            value = make_u[cut] * read(row - 1, start, size)
            value = value + (c[1] * (i + 1.0)) * read(row + 1, start, size)
            value = value + make_v * read(row, start - 1, size)
            value = value + lose_v[cut] * read(row, start + 1, size)
            pair = (0.5 * c[4] * (i + 2.0) * (i + 1.0)) * read(row + 2, start, size)
            value = value + inner_k * pltpu.roll(pair, 1, 1)
            split = c[5] * read(row - 2, start, size) + c[6] * centre
            value = value + above_k * pltpu.roll(split, depth - 1, 1)
            out = rest[cut] + (c[1] * i + 0.5 * c[4] * i * (i - 1.0))
            return value - out * centre

        def read_field(row, start, size):
            return wide[member, row + REACH, pl.ds(GAP + start, size), :]

        def read_image(row, start, size):
            return wide_image[member, row + HALF, pl.ds(GAP + start, size), :]

        for row in range(-HALF, rows + HALF):
            inside = (first_i + row >= 0) & (first_i + row < count_i)
            value = apply(read_field, row, 0, cols)
            if row < 0 or row >= rows:
                value = jnp.where(inside, value, 0.0)
            else:
                image_one[member, row] = value
            wide_image[member, row + HALF, GAP : GAP + cols] = value
            if 0 <= row < rows:
                value = apply(read_field, row, -1, 1)
                wide_image[member, row + HALF, GAP - 1 : GAP] = jnp.where(first_j > 0, value, 0.0)
                value = apply(read_field, row, cols, 1)
                wide_image[member, row + HALF, GAP + cols : GAP + cols + 1] = jnp.where(
                    first_j + cols < count_j, value, 0.0
                )

        products = [jnp.zeros((cols, depth), jnp.float32) for _ in range(6)]
        for row in range(rows):
            zero = field[member, row]
            one = image_one[member, row]
            two = apply(read_image, row, 0, cols)
            image_two[member, row] = two
            terms = (zero * zero, zero * one, zero * two, one * one, one * two, two * two)
            products = [total + term for total, term in zip(products, terms)]
        for index, total in enumerate(products):
            parts[8 * index + member : 8 * index + member + 1, :] = jnp.sum(total, axis=0, keepdims=True)

    for index in range(6):
        parts[8 * index + members : 8 * index + 8, :] = jnp.zeros((8 - members, depth), jnp.float32)
    parts[48:, :] = jnp.zeros((parts.shape[0] - 48, depth), jnp.float32)
    ones = jnp.ones(message.shape[:1] + (depth,), jnp.float32)
    message[...] = lax.dot_general(
        ones, parts[...], (((1,), (1,)), ((), ())), precision=HIGHEST, preferred_element_type=jnp.float32
    )


def first_column(h00, s01, h11):
    scale = tau_step / 2.0**squarings
    a, b, d = scale * h00, scale * s01, scale * h11
    c = scale
    zero, one = jnp.zeros_like(a), jnp.ones_like(a)
    p00, p01, p10, p11, q0, q1 = one, zero, zero, one, zero, zero
    for term in range(taylor_terms, 0, -1):
        inverse = 1.0 / term
        p00, p01, p10, p11, q0, q1 = (
            1.0 + (a * p00 + b * p10) * inverse,
            (a * p01 + b * p11) * inverse,
            (c * p00 + d * p10) * inverse,
            1.0 + (c * p01 + d * p11) * inverse,
            p10 * (c * inverse),
            p11 * (c * inverse),
        )
    for _ in range(squarings):
        p00, p01, p10, p11, q0, q1 = (
            p00 * p00 + p01 * p10,
            p00 * p01 + p01 * p11,
            p10 * p00 + p11 * p10,
            p10 * p01 + p11 * p11,
            q0 * p00 + q1 * p10 + q0,
            q0 * p01 + q1 * p11 + q1,
        )
    return p00, p10, q0


def combine_kernel(gathered, field, image_one, image_two, propagated, entries):
    members, rows, cols, depth = field.shape
    ones = jnp.ones((gathered.shape[0], 128), jnp.float32)
    sums = lax.dot_general(
        gathered[...], ones, (((0,), (0,)), ((), ())), precision=HIGHEST, preferred_element_type=jnp.float32
    )
    g00, g01, g02, g11, g12, g22 = [sums[8 * index : 8 * index + 8] for index in range(6)]
    tiny = jnp.finfo(jnp.float32).tiny
    h00 = g01 / g00
    square_10 = jnp.maximum(g11 / g00 - h00 * h00, tiny)
    s01 = (g02 - h00 * g01) / g00
    h11 = ((g12 - h00 * g02) - h00 * (g11 - h00 * g01)) / (g00 * square_10)
    norm_2 = ((g22 - h00 * g12) - h00 * (g12 - h00 * g11)) / (g00 * square_10)
    h10 = jnp.sqrt(square_10)
    h01 = s01 / h10
    h21 = jnp.sqrt(jnp.maximum(norm_2 - h01 * h01 - h11 * h11, 0.0))
    e0, e1, e2 = first_column(h00, s01, h11)
    a2 = e2
    a1 = e1 - e2 * (h00 + h11)
    a0 = e0 - e1 * h00 - e2 * (s01 - h11 * h00)
    lane = lax.broadcasted_iota(jnp.int32, h00.shape, 1)
    table = h21
    for index, entry in enumerate((h00, h10, h01, h11)):
        table = jnp.where(lane == index, entry, table)
    entries[...] = (tau_step * table)[: entries.shape[0], : entries.shape[1]]
    for member in range(members):
        b0, b1, b2 = [jnp.broadcast_to(a[member : member + 1], (cols, depth)) for a in (a0, a1, a2)]
        for row in range(rows):
            propagated[member, row] = (
                b0 * field[member, row] + b1 * image_one[member, row] + b2 * image_two[member, row]
            )


def shards(density, rate_table):
    members, rows, cols, depth = density.shape
    size_x, size_y = lax.axis_size("gx"), lax.axis_size("gy")
    devices = size_x * size_y
    index_x, index_y = lax.axis_index("gx"), lax.axis_index("gy")
    parity_x, parity_y = index_x % 2, index_y % 2
    place = jnp.stack([index_x * rows, index_y * cols, parity_x, parity_y]).astype(jnp.int32)

    def swap(axis, size, first, value):
        def partner(x, y):
            at = x if axis == "gx" else y
            other = at + 1 if (at - first) % 2 == 0 else at - 1
            if not 0 <= other < size:
                return (x, y ^ 1) if axis == "gx" else (x ^ 1, y)
            return (other, y) if axis == "gx" else (x, other)

        pairs = [
            (x * size_y + y, partner(x, y)[0] * size_y + partner(x, y)[1])
            for x in range(size_x)
            for y in range(size_y)
        ]
        return lax.ppermute(value, ("gx", "gy"), pairs)

    assert size_x % 2 == 0 and size_y % 2 == 0

    def swaps(axis, size, parity, initial, last):
        if initial is last:
            return swap(axis, size, 0, last), swap(axis, size, 1, last)
        is_even = parity == 0
        return (
            swap(axis, size, 0, jnp.where(is_even, last, initial)),
            swap(axis, size, 1, jnp.where(is_even, initial, last)),
        )

    if rows == REACH:
        even_x, odd_x = swaps("gx", size_x, parity_x, density, density)
    else:
        even_x, odd_x = swaps("gx", size_x, parity_x, density[:, :REACH], density[:, rows - REACH :])

    even_y, odd_y = swaps("gy", size_y, parity_y, density[:, :, :2], density[:, :, cols - 2 :])

    def corners(first):
        even, odd = even_y[:, first : first + HALF], odd_y[:, first : first + HALF]
        left = jnp.where(parity_y == 0, odd, even)[:, :, 1:]
        right = jnp.where(parity_y == 0, even, odd)[:, :, :1]
        return jnp.concatenate([left, right], axis=2)

    even_corners, odd_corners = swaps("gx", size_x, parity_x, corners(0), corners(rows - HALF))

    vmem = pl.BlockSpec(memory_space=pltpu.VMEM)
    smem = pl.BlockSpec(memory_space=pltpu.SMEM)
    block = jax.ShapeDtypeStruct(density.shape, jnp.float32)
    image_one, image_two, message = pl.pallas_call(
        functools.partial(images_kernel, (size_x * rows, size_y * cols)),
        out_shape=[block, block, jax.ShapeDtypeStruct((devices, 128), jnp.float32)],
        in_specs=[smem, smem] + [vmem] * 7,
        out_specs=[vmem, vmem, vmem],
        scratch_shapes=[
            pltpu.VMEM((members, rows + 2 * REACH, cols + 2 * GAP, depth), jnp.float32),
            pltpu.VMEM((members, rows + 2 * HALF, cols + 2 * GAP, depth), jnp.float32),
            pltpu.VMEM((128, depth), jnp.float32),
        ],
        compiler_params=pltpu.CompilerParams(vmem_limit_bytes=8 * 2**20),
        name="images",
    )(place, rate_table, density, even_x, odd_x, even_y, odd_y, even_corners, odd_corners)

    gathered = lax.all_to_all(message, ("gx", "gy"), 0, 0, tiled=True)

    return pl.pallas_call(
        combine_kernel,
        out_shape=[block, jax.ShapeDtypeStruct((members, 5), jnp.float32)],
        in_specs=[vmem] * 4,
        out_specs=[vmem, vmem],
        compiler_params=pltpu.CompilerParams(vmem_limit_bytes=8 * 2**20),
        name="combine",
    )(gathered, density, image_one, image_two)


def solution(mesh):
    in_specs = (P(None, "gx", "gy", None), P())
    out_specs = (P(None, "gx", "gy", None), P())
    return jax.shard_map(shards, mesh=mesh, in_specs=in_specs, out_specs=out_specs, check_vma=False)
```

profile of v0, /device:TPU:0, one launch (start us, length us, event | category | flops | bytes accessed | tf_op | source)
XLA Modules:
  0.0 27.7 jit_solution(2970764837857243671)
XLA Ops:
  0.6 0.0 copy-start
  0.7 0.9 %broadcast_select_fusion = (f32[4,4,2,128]{3,2,1,0:T(2,128)S(1)}, f32[4,4,2,128]{3,2,1,0:T(2,128)S(1)}) fusion(pred[]{:T(512)S(6)} %eq.7, f32[4,4,16,128]{3,2,1,0:T(8,128)} %field.3), kind=kLoop, calls=%fused_computation | loop fusion | flops 8192 | bytes 65537 | tf_op jit(solution)/shard_map/jit(_where)/select_n | solution.py:225
  1.6 3.0 %collective-permute-start.3 = (f32[4,4,2,128]{3,2,1,0:T(2,128)S(1)}, f32[4,4,2,128]{3,2,1,0:T(2,128)S(1)}, u32[]{:S(2)}, u32[]{:S(2)}) collective-permute-start(f32[4,4,2,128]{3,2,1,0:T(2,128)S(1)} %get-tuple-element.8), channel_id=1, source_target_pairs={{0,4},{1,2},{2,1},{3,7},{4,0},{5,6},{6,5},{7,3},{8,12},{9,10},{10,... | collective-permute-start | bytes 49160 | tf_op jit(solution)/shard_map/ppermute | solution.py:215
  4.6 0.1 collective-permute-start.1
  4.7 2.9 %collective-permute-start = (f32[4,4,16,128]{3,2,1,0:T(8,128)}, f32[4,4,16,128]{3,2,1,0:T(8,128)S(1)}, u32[]{:S(2)}, u32[]{:S(2)}) collective-permute-start(f32[4,4,16,128]{3,2,1,0:T(8,128)} %field.3), channel_id=1, source_target_pairs={{0,4},{1,5},{2,6},{3,7},{4,0},{5,1},{6,2},{7,3},{8,12},{9,13},{10,... | collective-permute-start | bytes 393224 | tf_op jit(solution)/shard_map/ppermute | solution.py:215
  7.6 0.0 collective-permute-start.2
  7.6 0.0 collective-permute-done.3.odd_y
  7.6 1.2 %collective-permute-done.2.even_y = f32[4,4,2,128]{3,2,1,0:T(2,128)S(1)} collective-permute-done((f32[4,4,2,128]{3,2,1,0:T(2,128)S(1)}, f32[4,4,2,128]{3,2,1,0:T(2,128)S(1)}, u32[]{:S(2)}, u32[]{:S(2)}) %collective-permute-start.2) | collective-permute-done | bytes 16416 | tf_op jit(solution)/shard_map/ppermute | solution.py:215
  8.9 0.2 collective-permute-start.5
  9.1 2.9 %collective-permute-start.4 = (f32[4,2,2,128]{3,2,1,0:T(2,128)S(1)}, f32[4,2,2,128]{3,2,1,0:T(2,128)S(1)}, u32[]{:S(2)}, u32[]{:S(2)}) collective-permute-start(f32[4,2,2,128]{3,2,1,0:T(2,128)S(1)} %get-tuple-element.11), channel_id=1, source_target_pairs={{0,4},{1,5},{2,6},{3,7},{4,0},{5,1},{6,2},{7,3},{8,12},{9,13},{10,... | collective-permute-start | bytes 24584 | tf_op jit(solution)/shard_map/ppermute | solution.py:215
  12.0 0.0 copy-start.1
  12.0 0.1 pad_add_fusion.place
  12.1 0.0 collective-permute-done.5.odd_corners
  12.1 1.5 %collective-permute-done.4.even_corners = f32[4,2,2,128]{3,2,1,0:T(2,128)S(1)} collective-permute-done((f32[4,2,2,128]{3,2,1,0:T(2,128)S(1)}, f32[4,2,2,128]{3,2,1,0:T(2,128)S(1)}, u32[]{:S(2)}, u32[]{:S(2)}) %collective-permute-start.4) | collective-permute-done | bytes 8224 | tf_op jit(solution)/shard_map/ppermute | solution.py:215
  13.6 0.0 collective-permute-done.1.odd_x
  13.6 0.0 collective-permute-done.even_x
  13.6 0.0 copy-done
  13.6 0.0 copy-done.1
  13.6 1.3 %images.1 = (f32[4,4,16,128]{3,2,1,0:T(8,128)S(1)}, f32[4,4,16,128]{3,2,1,0:T(8,128)S(1)}, f32[32,128]{1,0:T(8,128)S(1)}) custom-call(s32[4]{0:T(128)S(1)} %pad_add_fusion.place, f32[4,9]{1,0:T(4,128)S(1)} %copy-done.1, f32[4,4,16,128]{3,2,1,0:T(8,128)S(1)} %copy-done, f32[4,4,16,128]{3,2,1,0:T(8,128)S(1)} %collective-permute-done.even_x, ...), custom_call_target="tpu_custom_call" | custom-call | tf_op jit(solution)/shard_map/images/pallas_call | solution.py:246
  15.0 11.7 %all_to_all.11 = f32[32,1,128]{2,1,0:T(1,128)S(1)} all-to-all(f32[32,1,128]{2,1,0:T(1,128)S(1)} %bitcast.9), channel_id=1, replica_groups=mesh['gx'=8,'gy'=4] {'gx','gy'}, dimensions={0} | all-to-all | bytes 32768 | tf_op jit(solution)/shard_map/all_to_all | solution.py:260
  26.7 1.0 %combine.1 = (f32[4,4,16,128]{3,2,1,0:T(8,128)}, f32[4,5]{1,0:T(4,128)}) custom-call(f32[32,128]{1,0:T(8,128)S(1)} %bitcast.8, f32[4,4,16,128]{3,2,1,0:T(8,128)S(1)} %copy-done, f32[4,4,16,128]{3,2,1,0:T(8,128)S(1)} %get-tuple-element.6.image_one, f32[4,4,16,128]{3,2,1,0:T(8,128)S(1)} %get-tuple-element.7.image_two), custom_call_target="tpu_custom_call" | custom-call | tf_op jit(solution)/shard_map/combine/pallas_call | solution.py:262
  (4 shorter events, 0.0 us)
Async XLA Ops:
  0.6 13.0 %copy-start = (f32[4,4,16,128]{3,2,1,0:T(8,128)S(1)}, f32[4,4,16,128]{3,2,1,0:T(8,128)}, u32[]{:S(2)}) copy-start(f32[4,4,16,128]{3,2,1,0:T(8,128)} %field.3) | copy-start | bytes 393220
  1.6 6.0 %collective-permute-start.3 = (f32[4,4,2,128]{3,2,1,0:T(2,128)S(1)}, f32[4,4,2,128]{3,2,1,0:T(2,128)S(1)}, u32[]{:S(2)}, u32[]{:S(2)}) collective-permute-start(f32[4,4,2,128]{3,2,1,0:T(2,128)S(1)} %get-tuple-element.8), channel_id=1, source_target_pairs={{0,4},{1,2},{2,1},{3,7},{4,0},{5,6},{6,5},{7,3},{8,12},{9,10},{10,... | collective-permute-start | bytes 49160 | tf_op jit(solution)/shard_map/ppermute | solution.py:215
  4.6 9.0 %collective-permute-start.1 = (f32[4,4,16,128]{3,2,1,0:T(8,128)}, f32[4,4,16,128]{3,2,1,0:T(8,128)S(1)}, u32[]{:S(2)}, u32[]{:S(2)}) collective-permute-start(f32[4,4,16,128]{3,2,1,0:T(8,128)} %field.3), channel_id=1, source_target_pairs={{0,1},{1,0},{2,3},{3,2},{4,8},{5,9},{6,10},{7,11},{8,4},{9,5},{10,... | collective-permute-start | bytes 393224 | tf_op jit(solution)/shard_map/ppermute | solution.py:215
  4.7 8.9 %collective-permute-start = (f32[4,4,16,128]{3,2,1,0:T(8,128)}, f32[4,4,16,128]{3,2,1,0:T(8,128)S(1)}, u32[]{:S(2)}, u32[]{:S(2)}) collective-permute-start(f32[4,4,16,128]{3,2,1,0:T(8,128)} %field.3), channel_id=1, source_target_pairs={{0,4},{1,5},{2,6},{3,7},{4,0},{5,1},{6,2},{7,3},{8,12},{9,13},{10,... | collective-permute-start | bytes 393224 | tf_op jit(solution)/shard_map/ppermute | solution.py:215
  7.6 1.2 %collective-permute-start.2 = (f32[4,4,2,128]{3,2,1,0:T(2,128)S(1)}, f32[4,4,2,128]{3,2,1,0:T(2,128)S(1)}, u32[]{:S(2)}, u32[]{:S(2)}) collective-permute-start(f32[4,4,2,128]{3,2,1,0:T(2,128)S(1)} %get-tuple-element.9), channel_id=1, source_target_pairs={{0,1},{1,0},{2,3},{3,2},{4,5},{5,4},{6,7},{7,6},{8,9},{9,8},{10,11... | collective-permute-start | bytes 49160 | tf_op jit(solution)/shard_map/ppermute | solution.py:215
  8.9 3.2 %collective-permute-start.5 = (f32[4,2,2,128]{3,2,1,0:T(2,128)S(1)}, f32[4,2,2,128]{3,2,1,0:T(2,128)S(1)}, u32[]{:S(2)}, u32[]{:S(2)}) collective-permute-start(f32[4,2,2,128]{3,2,1,0:T(2,128)S(1)} %get-tuple-element.10), channel_id=1, source_target_pairs={{0,1},{1,0},{2,3},{3,2},{4,8},{5,9},{6,10},{7,11},{8,4},{9,5},{10,... | collective-permute-start | bytes 24584 | tf_op jit(solution)/shard_map/ppermute | solution.py:215
  9.1 4.5 %collective-permute-start.4 = (f32[4,2,2,128]{3,2,1,0:T(2,128)S(1)}, f32[4,2,2,128]{3,2,1,0:T(2,128)S(1)}, u32[]{:S(2)}, u32[]{:S(2)}) collective-permute-start(f32[4,2,2,128]{3,2,1,0:T(2,128)S(1)} %get-tuple-element.11), channel_id=1, source_target_pairs={{0,4},{1,5},{2,6},{3,7},{4,0},{5,1},{6,2},{7,3},{8,12},{9,13},{10,... | collective-permute-start | bytes 24584 | tf_op jit(solution)/shard_map/ppermute | solution.py:215
  12.0 1.6 %copy-start.1 = (f32[4,9]{1,0:T(4,128)S(1)}, f32[4,9]{1,0:T(4,128)}, u32[]{:S(2)}) copy-start(f32[4,9]{1,0:T(4,128)} %rates.1) | copy-start | bytes 436
where the time goes:
time: 27.9 us; the launch traced here: 27.7 us
  blocking collectives  11.7 us (42%)
  starting transfers between devices  9.15 us (33%)
  waiting for transfers between devices  2.73 us (10%)
  Pallas kernels  2.38 us (9%)
  other arithmetic  1.04 us (4%)
  between operations  0.69 us (2%)
    all_to_all x1, blocking collectives, shards(): gathered = lax.all_to_all(message, ('gx', 'gy'), 0, 0, tiled=True)  11.7 us
    ppermute x6, starting transfers between devices, swap(): return lax.ppermute(value, ('gx', 'gy'), pairs)  9.15 us
    ppermute x6, waiting for transfers between devices, swap(): return lax.ppermute(value, ('gx', 'gy'), pairs)  2.73 us
    pallas_call x1, Pallas kernels, shards(): pl.pallas_call(functools.partial(images_kernel, (size_x * rows, size_y *...  1.35 us
    pallas_call x1, Pallas kernels, shards(): pl.pallas_call(combine_kernel, out_shape=[block, jax.ShapeDtypeStruct((me...  1.03 us
    select_n x2, other arithmetic, swaps(): jnp.where(is_even, initial, last)  0.94 us
  transfers between devices with their start and end apart: 6, of which 2 were waited for; matrix products, arithmetic and copies ran while one was open for 0% of the time, Pallas kernels for 0%

commit v1 on v0

--- a/solution.py
+++ b/solution.py
@@ -232,6 +232,8 @@
 
     even_y, odd_y = swaps("gy", size_y, parity_y, density[:, :, :2], density[:, :, cols - 2 :])
 
+    even_x, even_y, odd_y = lax.optimization_barrier((even_x, even_y, odd_y))
+
     def corners(first):
         even, odd = even_y[:, first : first + HALF], odd_y[:, first : first + HALF]
         left = jnp.where(parity_y == 0, odd, even)[:, :, 1:]

time: 27.9 us -> 27.5 us (0.986)
  starting transfers between devices: 9.15 us -> 7.8 us
  waiting for transfers between devices: 2.73 us -> 3.65 us
    ppermute x6, starting transfers between devices: 9.15 us -> 7.8 us  [swap(): return lax.ppermute(value, ('gx', 'gy'), pairs)]
    ppermute x6, waiting for transfers between devices: 2.73 us -> 3.65 us  [swap(): return lax.ppermute(value, ('gx', 'gy'), pairs)]
  transfers between devices with their start and end apart: 6 -> 6, of which waited for: 2 -> 2; matrix products, arithmetic and copies ran while one was open for 0% -> 4% of each run, Pallas kernels for 0% -> 0%
where the time goes in v1:
time: 27.5 us; the launch traced here: 27.4 us
  blocking collectives  11.8 us (43%)
  starting transfers between devices  7.8 us (28%)
  waiting for transfers between devices  3.65 us (13%)
  Pallas kernels  2.37 us (9%)
  other arithmetic  1.08 us (4%)
  between operations  0.68 us (2%)
    all_to_all x1, blocking collectives, shards(): gathered = lax.all_to_all(message, ('gx', 'gy'), 0, 0, tiled=True)  11.8 us
    ppermute x6, starting transfers between devices, swap(): return lax.ppermute(value, ('gx', 'gy'), pairs)  7.8 us
    ppermute x6, waiting for transfers between devices, swap(): return lax.ppermute(value, ('gx', 'gy'), pairs)  3.65 us
    pallas_call x1, Pallas kernels, shards(): pl.pallas_call(functools.partial(images_kernel, (size_x * rows, size_y *...  1.34 us
    pallas_call x1, Pallas kernels, shards(): pl.pallas_call(combine_kernel, out_shape=[block, jax.ShapeDtypeStruct((me...  1.03 us
    select_n x2, other arithmetic, swaps(): jnp.where(is_even, initial, last)  0.98 us
  transfers between devices with their start and end apart: 6, of which 2 were waited for; matrix products, arithmetic and copies ran while one was open for 4% of the time, Pallas kernels for 0%

profile of v1, /device:TPU:0, one launch (start us, length us, event | category | flops | bytes accessed | tf_op | source)
XLA Modules:
  0.0 27.4 jit_solution(2106987432896227626)
XLA Ops:
  0.6 3.0 %collective-permute-start = (f32[4,4,16,128]{3,2,1,0:T(8,128)}, f32[4,4,16,128]{3,2,1,0:T(8,128)S(1)}, u32[]{:S(2)}, u32[]{:S(2)}) collective-permute-start(f32[4,4,16,128]{3,2,1,0:T(8,128)} %field.3), channel_id=1, source_target_pairs={{0,4},{1,5},{2,6},{3,7},{4,0},{5,1},{6,2},{7,3},{8,12},{9,13},{10,... | collective-permute-start | bytes 393224 | tf_op jit(solution)/shard_map/ppermute | solution.py:215
  3.6 0.0 copy-start
  3.6 1.0 %broadcast_select_fusion = (f32[4,4,2,128]{3,2,1,0:T(2,128)S(1)}, f32[4,4,2,128]{3,2,1,0:T(2,128)S(1)}) fusion(pred[]{:T(512)S(6)} %eq.7, f32[4,4,16,128]{3,2,1,0:T(8,128)} %field.3), kind=kLoop, calls=%fused_computation | loop fusion | flops 8192 | bytes 65537 | tf_op jit(solution)/shard_map/jit(_where)/select_n | solution.py:225
  4.6 0.1 collective-permute-start.2
  4.7 1.6 %collective-permute-start.1 = (f32[4,4,2,128]{3,2,1,0:T(2,128)S(1)}, f32[4,4,2,128]{3,2,1,0:T(2,128)S(1)}, u32[]{:S(2)}, u32[]{:S(2)}) collective-permute-start(f32[4,4,2,128]{3,2,1,0:T(2,128)S(1)} %get-tuple-element.15), channel_id=1, source_target_pairs={{0,1},{1,0},{2,3},{3,2},{4,5},{5,4},{6,7},{7,6},{8,9},{9,8},{10,11... | collective-permute-start | bytes 49160 | tf_op jit(solution)/shard_map/ppermute | solution.py:215
  6.3 0.0 collective-permute-start.3
  6.3 2.1 %collective-permute-done.2.odd_y = f32[4,4,2,128]{3,2,1,0:T(2,128)S(1)} collective-permute-done((f32[4,4,2,128]{3,2,1,0:T(2,128)S(1)}, f32[4,4,2,128]{3,2,1,0:T(2,128)S(1)}, u32[]{:S(2)}, u32[]{:S(2)}) %collective-permute-start.2) | collective-permute-done | bytes 16416 | tf_op jit(solution)/shard_map/ppermute | solution.py:215
  8.4 0.0 collective-permute-done.1.even_y
  8.4 0.0 collective-permute-done.even_x
  8.5 0.1 collective-permute-start.5
  8.6 3.0 %collective-permute-start.4 = (f32[4,2,2,128]{3,2,1,0:T(2,128)S(1)}, f32[4,2,2,128]{3,2,1,0:T(2,128)S(1)}, u32[]{:S(2)}, u32[]{:S(2)}) collective-permute-start(f32[4,2,2,128]{3,2,1,0:T(2,128)S(1)} %get-tuple-element.17), channel_id=1, source_target_pairs={{0,4},{1,5},{2,6},{3,7},{4,0},{5,1},{6,2},{7,3},{8,12},{9,13},{10,... | collective-permute-start | bytes 24584 | tf_op jit(solution)/shard_map/ppermute | solution.py:215
  11.6 0.0 copy-start.1
  11.6 0.1 pad_add_fusion.place
  11.7 0.0 collective-permute-done.3.odd_x
  11.7 0.0 collective-permute-done.5.odd_corners
  11.7 1.5 %collective-permute-done.4.even_corners = f32[4,2,2,128]{3,2,1,0:T(2,128)S(1)} collective-permute-done((f32[4,2,2,128]{3,2,1,0:T(2,128)S(1)}, f32[4,2,2,128]{3,2,1,0:T(2,128)S(1)}, u32[]{:S(2)}, u32[]{:S(2)}) %collective-permute-start.4) | collective-permute-done | bytes 8224 | tf_op jit(solution)/shard_map/ppermute | solution.py:215
  13.2 0.0 copy-done
  13.2 0.0 copy-done.1
  13.2 1.3 %images.1 = (f32[4,4,16,128]{3,2,1,0:T(8,128)S(1)}, f32[4,4,16,128]{3,2,1,0:T(8,128)S(1)}, f32[32,128]{1,0:T(8,128)S(1)}) custom-call(s32[4]{0:T(128)S(1)} %pad_add_fusion.place, f32[4,9]{1,0:T(4,128)S(1)} %copy-done.1, f32[4,4,16,128]{3,2,1,0:T(8,128)S(1)} %copy-done, f32[4,4,16,128]{3,2,1,0:T(8,128)S(1)} %collective-permute-done.even_x, ...), custom_call_target="tpu_custom_call" | custom-call | tf_op jit(solution)/shard_map/images/pallas_call | solution.py:248
  14.6 11.8 %all_to_all.11 = f32[32,1,128]{2,1,0:T(1,128)S(1)} all-to-all(f32[32,1,128]{2,1,0:T(1,128)S(1)} %bitcast.9), channel_id=1, replica_groups=mesh['gx'=8,'gy'=4] {'gx','gy'}, dimensions={0} | all-to-all | bytes 32768 | tf_op jit(solution)/shard_map/all_to_all | solution.py:262
  26.3 1.0 %combine.1 = (f32[4,4,16,128]{3,2,1,0:T(8,128)}, f32[4,5]{1,0:T(4,128)}) custom-call(f32[32,128]{1,0:T(8,128)S(1)} %bitcast.8, f32[4,4,16,128]{3,2,1,0:T(8,128)S(1)} %copy-done, f32[4,4,16,128]{3,2,1,0:T(8,128)S(1)} %get-tuple-element.12.image_one, f32[4,4,16,128]{3,2,1,0:T(8,128)S(1)} %get-tuple-element.13.image_two), custom_call_target="tpu_custom_call" | custom-call | tf_op jit(solution)/shard_map/combine/pallas_call | solution.py:264
  (4 shorter events, 0.1 us)
Async XLA Ops:
  0.6 7.8 %collective-permute-start = (f32[4,4,16,128]{3,2,1,0:T(8,128)}, f32[4,4,16,128]{3,2,1,0:T(8,128)S(1)}, u32[]{:S(2)}, u32[]{:S(2)}) collective-permute-start(f32[4,4,16,128]{3,2,1,0:T(8,128)} %field.3), channel_id=1, source_target_pairs={{0,4},{1,5},{2,6},{3,7},{4,0},{5,1},{6,2},{7,3},{8,12},{9,13},{10,... | collective-permute-start | bytes 393224 | tf_op jit(solution)/shard_map/ppermute | solution.py:215
  3.6 9.6 %copy-start = (f32[4,4,16,128]{3,2,1,0:T(8,128)S(1)}, f32[4,4,16,128]{3,2,1,0:T(8,128)}, u32[]{:S(2)}) copy-start(f32[4,4,16,128]{3,2,1,0:T(8,128)} %field.3) | copy-start | bytes 393220
  4.6 3.8 %collective-permute-start.2 = (f32[4,4,2,128]{3,2,1,0:T(2,128)S(1)}, f32[4,4,2,128]{3,2,1,0:T(2,128)S(1)}, u32[]{:S(2)}, u32[]{:S(2)}) collective-permute-start(f32[4,4,2,128]{3,2,1,0:T(2,128)S(1)} %get-tuple-element.14), channel_id=1, source_target_pairs={{0,4},{1,2},{2,1},{3,7},{4,0},{5,6},{6,5},{7,3},{8,12},{9,10},{10,... | collective-permute-start | bytes 49160 | tf_op jit(solution)/shard_map/ppermute | solution.py:215
  4.7 3.7 %collective-permute-start.1 = (f32[4,4,2,128]{3,2,1,0:T(2,128)S(1)}, f32[4,4,2,128]{3,2,1,0:T(2,128)S(1)}, u32[]{:S(2)}, u32[]{:S(2)}) collective-permute-start(f32[4,4,2,128]{3,2,1,0:T(2,128)S(1)} %get-tuple-element.15), channel_id=1, source_target_pairs={{0,1},{1,0},{2,3},{3,2},{4,5},{5,4},{6,7},{7,6},{8,9},{9,8},{10,11... | collective-permute-start | bytes 49160 | tf_op jit(solution)/shard_map/ppermute | solution.py:215
  6.3 5.4 %collective-permute-start.3 = (f32[4,4,16,128]{3,2,1,0:T(8,128)}, f32[4,4,16,128]{3,2,1,0:T(8,128)S(1)}, u32[]{:S(2)}, u32[]{:S(2)}) collective-permute-start(f32[4,4,16,128]{3,2,1,0:T(8,128)} %field.3), channel_id=1, source_target_pairs={{0,1},{1,0},{2,3},{3,2},{4,8},{5,9},{6,10},{7,11},{8,4},{9,5},{10,... | collective-permute-start | bytes 393224 | tf_op jit(solution)/shard_map/ppermute | solution.py:215
  8.5 3.2 %collective-permute-start.5 = (f32[4,2,2,128]{3,2,1,0:T(2,128)S(1)}, f32[4,2,2,128]{3,2,1,0:T(2,128)S(1)}, u32[]{:S(2)}, u32[]{:S(2)}) collective-permute-start(f32[4,2,2,128]{3,2,1,0:T(2,128)S(1)} %get-tuple-element.16), channel_id=1, source_target_pairs={{0,1},{1,0},{2,3},{3,2},{4,8},{5,9},{6,10},{7,11},{8,4},{9,5},{10,... | collective-permute-start | bytes 24584 | tf_op jit(solution)/shard_map/ppermute | solution.py:215
  8.6 4.7 %collective-permute-start.4 = (f32[4,2,2,128]{3,2,1,0:T(2,128)S(1)}, f32[4,2,2,128]{3,2,1,0:T(2,128)S(1)}, u32[]{:S(2)}, u32[]{:S(2)}) collective-permute-start(f32[4,2,2,128]{3,2,1,0:T(2,128)S(1)} %get-tuple-element.17), channel_id=1, source_target_pairs={{0,4},{1,5},{2,6},{3,7},{4,0},{5,1},{6,2},{7,3},{8,12},{9,13},{10,... | collective-permute-start | bytes 24584 | tf_op jit(solution)/shard_map/ppermute | solution.py:215
  11.6 1.6 %copy-start.1 = (f32[4,9]{1,0:T(4,128)S(1)}, f32[4,9]{1,0:T(4,128)}, u32[]{:S(2)}) copy-start(f32[4,9]{1,0:T(4,128)} %rates.1) | copy-start | bytes 436

commit v2 on v1

--- a/solution.py
+++ b/solution.py
@@ -10,15 +10,18 @@
 tau_step = 0.01
 taylor_terms = 16
 squarings = 4
-HIGHEST = lax.Precision.HIGHEST
 REACH = 4
 HALF = 2
 GAP = 8
 
 
+def own_lane(first):
+    row = lax.broadcasted_iota(jnp.int32, (8, 128), 0)
+    return lax.broadcasted_iota(jnp.int32, (8, 128), 1) == first + row
+
+
 def images_kernel(
     lattice,
-    place,
     rates,
     field,
     even_x,
@@ -36,7 +39,9 @@
 ):
     members, rows, cols, depth = field.shape
     span = cols + 2 * GAP
-    first_i, first_j = place[0], place[1]
+    index_i, index_j = lax.axis_index("gx"), lax.axis_index("gy")
+    first_i, first_j = index_i * rows, index_j * cols
+    even_i, even_j = index_i % 2 == 0, index_j % 2 == 0
     count_i, count_j = lattice
 
     ends_i, ends_j = first_i + rows < count_i, first_j + cols < count_j
@@ -46,13 +51,13 @@
         return jnp.where(lower_inside, lower, 0.0), jnp.where(higher_inside, higher, 0.0)
 
     wide[:, REACH : REACH + rows, GAP : GAP + cols] = field[...]
-    above, below = sides(even_x[...], odd_x[...], place[2] == 0, first_i > 0, ends_i)
+    above, below = sides(even_x[...], odd_x[...], even_i, first_i > 0, ends_i)
     wide[:, :REACH, GAP : GAP + cols] = above
     wide[:, REACH + rows :, GAP : GAP + cols] = below
-    left, right = sides(even_y[...], odd_y[...], place[3] == 0, first_j > 0, ends_j)
+    left, right = sides(even_y[...], odd_y[...], even_j, first_j > 0, ends_j)
     wide[:, REACH : REACH + rows, GAP - 2 : GAP] = left
     wide[:, REACH : REACH + rows, GAP + cols : GAP + cols + 2] = right
-    upper, lower = sides(even_corners[...], odd_corners[...], place[2] == 0, first_i > 0, ends_i)
+    upper, lower = sides(even_corners[...], odd_corners[...], even_i, first_i > 0, ends_i)
     for corners, at in ((upper, REACH - HALF), (lower, REACH + rows)):
         wide[:, at : at + HALF, GAP - 1 : GAP] = jnp.where(first_j > 0, corners[:, :, :1], 0.0)
         wide[:, at : at + HALF, GAP + cols : GAP + cols + 1] = jnp.where(ends_j, corners[:, :, 1:], 0.0)
@@ -65,12 +70,12 @@
     amount_j = (first_j - GAP + sublane).astype(jnp.float32)
 
     for member in range(members):
-        c = [rates[member, r] for r in range(9)]
-        ratio_j = amount_j / jnp.full((span, 1), c[7])
-        ratio_k = amount_k / jnp.full((1, depth), c[8])
-        make_u = jnp.broadcast_to(c[0] / (1.0 + ratio_j * ratio_j), (span, depth))
+        c = [jnp.broadcast_to(rates[member : member + 1, r : r + 1], (1, depth)) for r in range(9)]
+        ratio_j = amount_j / c[7]
+        ratio_k = amount_k / c[8]
+        make_u = c[0] / (1.0 + ratio_j * ratio_j)
         make_v = c[2] / (1.0 + ratio_k * ratio_k)
-        lose_v = jnp.broadcast_to(c[3] * (amount_j + 1.0), (span, depth))
+        lose_v = c[3] * (amount_j + 1.0)
         rest = make_u + make_v + (c[3] * amount_j + (c[5] + c[6]) * amount_k)
 
         def apply(read, row, start, size):
@@ -123,11 +128,11 @@
 
     for index in range(6):
         parts[8 * index + members : 8 * index + 8, :] = jnp.zeros((8 - members, depth), jnp.float32)
-    parts[48:, :] = jnp.zeros((parts.shape[0] - 48, depth), jnp.float32)
-    ones = jnp.ones(message.shape[:1] + (depth,), jnp.float32)
-    message[...] = lax.dot_general(
-        ones, parts[...], (((1,), (1,)), ((), ())), precision=HIGHEST, preferred_element_type=jnp.float32
-    )
+    row = jnp.zeros((8, depth), jnp.float32)
+    for index in range(6):
+        total = jnp.sum(parts[8 * index : 8 * index + 8], axis=1, keepdims=True)
+        row = row + jnp.where(own_lane(8 * index), total, 0.0)
+    message[...] = jnp.broadcast_to(jnp.sum(row, axis=0, keepdims=True), message.shape)
 
 
 def first_column(h00, s01, h11):
@@ -160,11 +165,11 @@
 
 def combine_kernel(gathered, field, image_one, image_two, propagated, entries):
     members, rows, cols, depth = field.shape
-    ones = jnp.ones((gathered.shape[0], 128), jnp.float32)
-    sums = lax.dot_general(
-        gathered[...], ones, (((0,), (0,)), ((), ())), precision=HIGHEST, preferred_element_type=jnp.float32
-    )
-    g00, g01, g02, g11, g12, g22 = [sums[8 * index : 8 * index + 8] for index in range(6)]
+    sums = jnp.broadcast_to(jnp.sum(gathered[...], axis=0, keepdims=True), (8, 128))
+    g00, g01, g02, g11, g12, g22 = [
+        jnp.broadcast_to(jnp.sum(jnp.where(own_lane(8 * index), sums, 0.0), axis=1, keepdims=True), (8, 128))
+        for index in range(6)
+    ]
     tiny = jnp.finfo(jnp.float32).tiny
     h00 = g01 / g00
     square_10 = jnp.maximum(g11 / g00 - h00 * h00, tiny)
@@ -195,9 +200,7 @@
     members, rows, cols, depth = density.shape
     size_x, size_y = lax.axis_size("gx"), lax.axis_size("gy")
     devices = size_x * size_y
-    index_x, index_y = lax.axis_index("gx"), lax.axis_index("gy")
-    parity_x, parity_y = index_x % 2, index_y % 2
-    place = jnp.stack([index_x * rows, index_y * cols, parity_x, parity_y]).astype(jnp.int32)
+    parity_x, parity_y = lax.axis_index("gx") % 2, lax.axis_index("gy") % 2
 
     def swap(axis, size, first, value):
         def partner(x, y):
@@ -243,21 +246,20 @@
     even_corners, odd_corners = swaps("gx", size_x, parity_x, corners(0), corners(rows - HALF))
 
     vmem = pl.BlockSpec(memory_space=pltpu.VMEM)
-    smem = pl.BlockSpec(memory_space=pltpu.SMEM)
     block = jax.ShapeDtypeStruct(density.shape, jnp.float32)
     image_one, image_two, message = pl.pallas_call(
         functools.partial(images_kernel, (size_x * rows, size_y * cols)),
         out_shape=[block, block, jax.ShapeDtypeStruct((devices, 128), jnp.float32)],
-        in_specs=[smem, smem] + [vmem] * 7,
+        in_specs=[vmem] * 8,
         out_specs=[vmem, vmem, vmem],
         scratch_shapes=[
             pltpu.VMEM((members, rows + 2 * REACH, cols + 2 * GAP, depth), jnp.float32),
             pltpu.VMEM((members, rows + 2 * HALF, cols + 2 * GAP, depth), jnp.float32),
-            pltpu.VMEM((128, depth), jnp.float32),
+            pltpu.VMEM((48, depth), jnp.float32),
         ],
         compiler_params=pltpu.CompilerParams(vmem_limit_bytes=8 * 2**20),
         name="images",
-    )(place, rate_table, density, even_x, odd_x, even_y, odd_y, even_corners, odd_corners)
+    )(rate_table, density, even_x, odd_x, even_y, odd_y, even_corners, odd_corners)
 
     gathered = lax.all_to_all(message, ("gx", "gy"), 0, 0, tiled=True)
 

time: 27.5 us -> 26.8 us (0.975)
  Pallas kernels: 2.37 us -> 1.67 us
    pallas_call x1, Pallas kernels: 1.34 us -> 0.8 us  [shards(): pl.pallas_call(functools.partial(images_kernel, (size_x * rows, size_y *...]
where the time goes in v2:
time: 26.8 us; the launch traced here: 26.7 us
  blocking collectives  11.7 us (44%)
  starting transfers between devices  7.8 us (29%)
  waiting for transfers between devices  3.73 us (14%)
  Pallas kernels  1.67 us (6%)
  other arithmetic  1 us (4%)
  between operations  0.69 us (3%)
    all_to_all x1, blocking collectives, shards(): gathered = lax.all_to_all(message, ('gx', 'gy'), 0, 0, tiled=True)  11.7 us
    ppermute x6, starting transfers between devices, swap(): return lax.ppermute(value, ('gx', 'gy'), pairs)  7.8 us
    ppermute x6, waiting for transfers between devices, swap(): return lax.ppermute(value, ('gx', 'gy'), pairs)  3.73 us
    select_n x2, other arithmetic, swaps(): jnp.where(is_even, initial, last)  0.98 us
    pallas_call x1, Pallas kernels, shards(): pl.pallas_call(combine_kernel, out_shape=[block, jax.ShapeDtypeStruct((me...  0.87 us
    pallas_call x1, Pallas kernels, shards(): pl.pallas_call(functools.partial(images_kernel, (size_x * rows, size_y *...  0.8 us
  transfers between devices with their start and end apart: 6, of which 2 were waited for; matrix products, arithmetic and copies ran while one was open for 4% of the time, Pallas kernels for 0%

profile of v2, /device:TPU:0, one launch (start us, length us, event | category | flops | bytes accessed | tf_op | source)
XLA Modules:
  0.0 26.7 jit_solution(2853969168432535484)
XLA Ops:
  0.6 3.0 %collective-permute-start = (f32[4,4,16,128]{3,2,1,0:T(8,128)}, f32[4,4,16,128]{3,2,1,0:T(8,128)S(1)}, u32[]{:S(2)}, u32[]{:S(2)}) collective-permute-start(f32[4,4,16,128]{3,2,1,0:T(8,128)} %field.3), channel_id=1, source_target_pairs={{0,4},{1,5},{2,6},{3,7},{4,0},{5,1},{6,2},{7,3},{8,12},{9,13},{10,... | collective-permute-start | bytes 393224 | tf_op jit(solution)/shard_map/ppermute | solution.py:218
  3.6 0.0 copy-start
  3.6 1.0 %broadcast_select_fusion = (f32[4,4,2,128]{3,2,1,0:T(2,128)S(1)}, f32[4,4,2,128]{3,2,1,0:T(2,128)S(1)}) fusion(pred[]{:T(512)S(6)} %eq.7, f32[4,4,16,128]{3,2,1,0:T(8,128)} %field.3), kind=kLoop, calls=%fused_computation | loop fusion | flops 8192 | bytes 65537 | tf_op jit(solution)/shard_map/jit(_where)/select_n | solution.py:228
  4.6 0.1 collective-permute-start.2
  4.7 1.6 %collective-permute-start.1 = (f32[4,4,2,128]{3,2,1,0:T(2,128)S(1)}, f32[4,4,2,128]{3,2,1,0:T(2,128)S(1)}, u32[]{:S(2)}, u32[]{:S(2)}) collective-permute-start(f32[4,4,2,128]{3,2,1,0:T(2,128)S(1)} %get-tuple-element.15), channel_id=1, source_target_pairs={{0,1},{1,0},{2,3},{3,2},{4,5},{5,4},{6,7},{7,6},{8,9},{9,8},{10,11... | collective-permute-start | bytes 49160 | tf_op jit(solution)/shard_map/ppermute | solution.py:218
  6.3 0.0 collective-permute-start.3
  6.3 2.1 %collective-permute-done.2.odd_y = f32[4,4,2,128]{3,2,1,0:T(2,128)S(1)} collective-permute-done((f32[4,4,2,128]{3,2,1,0:T(2,128)S(1)}, f32[4,4,2,128]{3,2,1,0:T(2,128)S(1)}, u32[]{:S(2)}, u32[]{:S(2)}) %collective-permute-start.2) | collective-permute-done | bytes 16416 | tf_op jit(solution)/shard_map/ppermute | solution.py:218
  8.4 0.0 collective-permute-done.1.even_y
  8.4 0.0 collective-permute-done.even_x
  8.5 0.0 copy-start.1
  8.5 0.1 collective-permute-start.5
  8.6 3.0 %collective-permute-start.4 = (f32[4,2,2,128]{3,2,1,0:T(2,128)S(1)}, f32[4,2,2,128]{3,2,1,0:T(2,128)S(1)}, u32[]{:S(2)}, u32[]{:S(2)}) collective-permute-start(f32[4,2,2,128]{3,2,1,0:T(2,128)S(1)} %get-tuple-element.17), channel_id=1, source_target_pairs={{0,4},{1,5},{2,6},{3,7},{4,0},{5,1},{6,2},{7,3},{8,12},{9,13},{10,... | collective-permute-start | bytes 24584 | tf_op jit(solution)/shard_map/ppermute | solution.py:218
  11.6 0.0 collective-permute-done.3.odd_x
  11.6 0.0 collective-permute-done.5.odd_corners
  11.6 1.6 %collective-permute-done.4.even_corners = f32[4,2,2,128]{3,2,1,0:T(2,128)S(1)} collective-permute-done((f32[4,2,2,128]{3,2,1,0:T(2,128)S(1)}, f32[4,2,2,128]{3,2,1,0:T(2,128)S(1)}, u32[]{:S(2)}, u32[]{:S(2)}) %collective-permute-start.4) | collective-permute-done | bytes 8224 | tf_op jit(solution)/shard_map/ppermute | solution.py:218
  13.2 0.0 copy-done
  13.2 0.0 copy-done.1
  13.2 0.8 %images.1 = (f32[4,4,16,128]{3,2,1,0:T(8,128)S(1)}, f32[4,4,16,128]{3,2,1,0:T(8,128)S(1)}, f32[32,128]{1,0:T(8,128)S(1)}) custom-call(f32[4,9]{1,0:T(4,128)S(1)} %copy-done.1, f32[4,4,16,128]{3,2,1,0:T(8,128)S(1)} %copy-done, f32[4,4,16,128]{3,2,1,0:T(8,128)S(1)} %collective-permute-done.even_x, f32[4,4,16,128]{3,2,1,0:T(8,128)S(1)} %collective-permute-done.3.odd_x, ...), custom_call_target="tpu_custom_call" | custom-call | tf_op jit(solution)/shard_map/images/pallas_call | solution.py:250
  14.0 11.7 %all_to_all.11 = f32[32,1,128]{2,1,0:T(1,128)S(1)} all-to-all(f32[32,1,128]{2,1,0:T(1,128)S(1)} %bitcast.5), channel_id=1, replica_groups=mesh['gx'=8,'gy'=4] {'gx','gy'}, dimensions={0} | all-to-all | bytes 32768 | tf_op jit(solution)/shard_map/all_to_all | solution.py:264
  25.8 0.9 %combine.1 = (f32[4,4,16,128]{3,2,1,0:T(8,128)}, f32[4,5]{1,0:T(4,128)}) custom-call(f32[32,128]{1,0:T(8,128)S(1)} %bitcast.4, f32[4,4,16,128]{3,2,1,0:T(8,128)S(1)} %copy-done, f32[4,4,16,128]{3,2,1,0:T(8,128)S(1)} %get-tuple-element.12.image_one, f32[4,4,16,128]{3,2,1,0:T(8,128)S(1)} %get-tuple-element.13.image_two), custom_call_target="tpu_custom_call" | custom-call | tf_op jit(solution)/shard_map/combine/pallas_call | solution.py:266
  (4 shorter events, 0.1 us)
Async XLA Ops:
  0.6 7.8 %collective-permute-start = (f32[4,4,16,128]{3,2,1,0:T(8,128)}, f32[4,4,16,128]{3,2,1,0:T(8,128)S(1)}, u32[]{:S(2)}, u32[]{:S(2)}) collective-permute-start(f32[4,4,16,128]{3,2,1,0:T(8,128)} %field.3), channel_id=1, source_target_pairs={{0,4},{1,5},{2,6},{3,7},{4,0},{5,1},{6,2},{7,3},{8,12},{9,13},{10,... | collective-permute-start | bytes 393224 | tf_op jit(solution)/shard_map/ppermute | solution.py:218
  3.6 9.6 %copy-start = (f32[4,4,16,128]{3,2,1,0:T(8,128)S(1)}, f32[4,4,16,128]{3,2,1,0:T(8,128)}, u32[]{:S(2)}) copy-start(f32[4,4,16,128]{3,2,1,0:T(8,128)} %field.3) | copy-start | bytes 393220
  4.6 3.8 %collective-permute-start.2 = (f32[4,4,2,128]{3,2,1,0:T(2,128)S(1)}, f32[4,4,2,128]{3,2,1,0:T(2,128)S(1)}, u32[]{:S(2)}, u32[]{:S(2)}) collective-permute-start(f32[4,4,2,128]{3,2,1,0:T(2,128)S(1)} %get-tuple-element.14), channel_id=1, source_target_pairs={{0,4},{1,2},{2,1},{3,7},{4,0},{5,6},{6,5},{7,3},{8,12},{9,10},{10,... | collective-permute-start | bytes 49160 | tf_op jit(solution)/shard_map/ppermute | solution.py:218
  4.7 3.7 %collective-permute-start.1 = (f32[4,4,2,128]{3,2,1,0:T(2,128)S(1)}, f32[4,4,2,128]{3,2,1,0:T(2,128)S(1)}, u32[]{:S(2)}, u32[]{:S(2)}) collective-permute-start(f32[4,4,2,128]{3,2,1,0:T(2,128)S(1)} %get-tuple-element.15), channel_id=1, source_target_pairs={{0,1},{1,0},{2,3},{3,2},{4,5},{5,4},{6,7},{7,6},{8,9},{9,8},{10,11... | collective-permute-start | bytes 49160 | tf_op jit(solution)/shard_map/ppermute | solution.py:218
  6.3 5.3 %collective-permute-start.3 = (f32[4,4,16,128]{3,2,1,0:T(8,128)}, f32[4,4,16,128]{3,2,1,0:T(8,128)S(1)}, u32[]{:S(2)}, u32[]{:S(2)}) collective-permute-start(f32[4,4,16,128]{3,2,1,0:T(8,128)} %field.3), channel_id=1, source_target_pairs={{0,1},{1,0},{2,3},{3,2},{4,8},{5,9},{6,10},{7,11},{8,4},{9,5},{10,... | collective-permute-start | bytes 393224 | tf_op jit(solution)/shard_map/ppermute | solution.py:218
  8.5 4.8 %copy-start.1 = (f32[4,9]{1,0:T(4,128)S(1)}, f32[4,9]{1,0:T(4,128)}, u32[]{:S(2)}) copy-start(f32[4,9]{1,0:T(4,128)} %rates.1) | copy-start | bytes 436
  8.5 3.1 %collective-permute-start.5 = (f32[4,2,2,128]{3,2,1,0:T(2,128)S(1)}, f32[4,2,2,128]{3,2,1,0:T(2,128)S(1)}, u32[]{:S(2)}, u32[]{:S(2)}) collective-permute-start(f32[4,2,2,128]{3,2,1,0:T(2,128)S(1)} %get-tuple-element.16), channel_id=1, source_target_pairs={{0,1},{1,0},{2,3},{3,2},{4,8},{5,9},{6,10},{7,11},{8,4},{9,5},{10,... | collective-permute-start | bytes 24584 | tf_op jit(solution)/shard_map/ppermute | solution.py:218
  8.6 4.7 %collective-permute-start.4 = (f32[4,2,2,128]{3,2,1,0:T(2,128)S(1)}, f32[4,2,2,128]{3,2,1,0:T(2,128)S(1)}, u32[]{:S(2)}, u32[]{:S(2)}) collective-permute-start(f32[4,2,2,128]{3,2,1,0:T(2,128)S(1)} %get-tuple-element.17), channel_id=1, source_target_pairs={{0,4},{1,5},{2,6},{3,7},{4,0},{5,1},{6,2},{7,3},{8,12},{9,13},{10,... | collective-permute-start | bytes 24584 | tf_op jit(solution)/shard_map/ppermute | solution.py:218

commit v3 on v2

--- a/solution.py
+++ b/solution.py
@@ -203,11 +203,13 @@
     parity_x, parity_y = lax.axis_index("gx") % 2, lax.axis_index("gy") % 2
 
     def swap(axis, size, first, value):
+        spare = 2 if size_x % 4 == 0 else 1
+
         def partner(x, y):
             at = x if axis == "gx" else y
             other = at + 1 if (at - first) % 2 == 0 else at - 1
             if not 0 <= other < size:
-                return (x, y ^ 1) if axis == "gx" else (x ^ 1, y)
+                return (x, y ^ 1) if axis == "gx" else (x ^ spare, y)
             return (other, y) if axis == "gx" else (x, other)
 
         pairs = [

time: 26.8 us -> 26.8 us (level)
  starting transfers between devices: 7.8 us -> 8.25 us
  waiting for transfers between devices: 3.73 us -> 3.28 us
    ppermute x6, starting transfers between devices: 7.8 us -> 8.25 us  [swap(): return lax.ppermute(value, ('gx', 'gy'), pairs)]
    ppermute x6, waiting for transfers between devices: 3.73 us -> 3.28 us  [swap(): return lax.ppermute(value, ('gx', 'gy'), pairs)]
where the time goes in v3:
time: 26.8 us; the launch traced here: 26.7 us
  blocking collectives  11.7 us (44%)
  starting transfers between devices  8.25 us (31%)
  waiting for transfers between devices  3.28 us (12%)
  Pallas kernels  1.67 us (6%)
  other arithmetic  1 us (4%)
  between operations  0.68 us (3%)
    all_to_all x1, blocking collectives, shards(): gathered = lax.all_to_all(message, ('gx', 'gy'), 0, 0, tiled=True)  11.7 us
    ppermute x6, starting transfers between devices, swap(): return lax.ppermute(value, ('gx', 'gy'), pairs)  8.25 us
    ppermute x6, waiting for transfers between devices, swap(): return lax.ppermute(value, ('gx', 'gy'), pairs)  3.28 us
    select_n x2, other arithmetic, swaps(): jnp.where(is_even, initial, last)  0.98 us
    pallas_call x1, Pallas kernels, shards(): pl.pallas_call(combine_kernel, out_shape=[block, jax.ShapeDtypeStruct((me...  0.87 us
    pallas_call x1, Pallas kernels, shards(): pl.pallas_call(functools.partial(images_kernel, (size_x * rows, size_y *...  0.8 us
  transfers between devices with their start and end apart: 6, of which 2 were waited for; matrix products, arithmetic and copies ran while one was open for 4% of the time, Pallas kernels for 0%

profile of v3, /device:TPU:0, one launch (start us, length us, event | category | flops | bytes accessed | tf_op | source)
XLA Modules:
  0.0 26.7 jit_solution(518922934125271484)
XLA Ops:
  0.6 3.0 %collective-permute-start = (f32[4,4,16,128]{3,2,1,0:T(8,128)}, f32[4,4,16,128]{3,2,1,0:T(8,128)S(1)}, u32[]{:S(2)}, u32[]{:S(2)}) collective-permute-start(f32[4,4,16,128]{3,2,1,0:T(8,128)} %field.3), channel_id=1, source_target_pairs={{0,4},{1,5},{2,6},{3,7},{4,0},{5,1},{6,2},{7,3},{8,12},{9,13},{10,... | collective-permute-start | bytes 393224 | tf_op jit(solution)/shard_map/ppermute | solution.py:220
  3.6 0.0 copy-start
  3.6 1.0 %broadcast_select_fusion = (f32[4,4,2,128]{3,2,1,0:T(2,128)S(1)}, f32[4,4,2,128]{3,2,1,0:T(2,128)S(1)}) fusion(pred[]{:T(512)S(6)} %eq.7, f32[4,4,16,128]{3,2,1,0:T(8,128)} %field.3), kind=kLoop, calls=%fused_computation | loop fusion | flops 8192 | bytes 65537 | tf_op jit(solution)/shard_map/jit(_where)/select_n | solution.py:230
  4.6 1.6 %collective-permute-start.2 = (f32[4,4,2,128]{3,2,1,0:T(2,128)S(1)}, f32[4,4,2,128]{3,2,1,0:T(2,128)S(1)}, u32[]{:S(2)}, u32[]{:S(2)}) collective-permute-start(f32[4,4,2,128]{3,2,1,0:T(2,128)S(1)} %get-tuple-element.14), channel_id=1, source_target_pairs={{0,8},{1,2},{2,1},{3,11},{4,12},{5,6},{6,5},{7,15},{8,0},{9,10},{1... | collective-permute-start | bytes 49160 | tf_op jit(solution)/shard_map/ppermute | solution.py:220
  6.2 0.1 collective-permute-start.1
  6.3 0.5 %collective-permute-start.3 = (f32[4,4,16,128]{3,2,1,0:T(8,128)}, f32[4,4,16,128]{3,2,1,0:T(8,128)S(1)}, u32[]{:S(2)}, u32[]{:S(2)}) collective-permute-start(f32[4,4,16,128]{3,2,1,0:T(8,128)} %field.3), channel_id=1, source_target_pairs={{0,1},{1,0},{2,3},{3,2},{4,8},{5,9},{6,10},{7,11},{8,4},{9,5},{10,... | collective-permute-start | bytes 393224 | tf_op jit(solution)/shard_map/ppermute | solution.py:220
  6.7 1.7 %collective-permute-done.2.odd_y = f32[4,4,2,128]{3,2,1,0:T(2,128)S(1)} collective-permute-done((f32[4,4,2,128]{3,2,1,0:T(2,128)S(1)}, f32[4,4,2,128]{3,2,1,0:T(2,128)S(1)}, u32[]{:S(2)}, u32[]{:S(2)}) %collective-permute-start.2) | collective-permute-done | bytes 16416 | tf_op jit(solution)/shard_map/ppermute | solution.py:220
  8.4 0.0 collective-permute-done.1.even_y
  8.4 0.0 collective-permute-done.even_x
  8.5 0.0 copy-start.1
  8.5 0.1 collective-permute-start.5
  8.6 3.0 %collective-permute-start.4 = (f32[4,2,2,128]{3,2,1,0:T(2,128)S(1)}, f32[4,2,2,128]{3,2,1,0:T(2,128)S(1)}, u32[]{:S(2)}, u32[]{:S(2)}) collective-permute-start(f32[4,2,2,128]{3,2,1,0:T(2,128)S(1)} %get-tuple-element.17), channel_id=1, source_target_pairs={{0,4},{1,5},{2,6},{3,7},{4,0},{5,1},{6,2},{7,3},{8,12},{9,13},{10,... | collective-permute-start | bytes 24584 | tf_op jit(solution)/shard_map/ppermute | solution.py:220
  11.6 0.0 collective-permute-done.3.odd_x
  11.6 0.0 collective-permute-done.5.odd_corners
  11.6 1.6 %collective-permute-done.4.even_corners = f32[4,2,2,128]{3,2,1,0:T(2,128)S(1)} collective-permute-done((f32[4,2,2,128]{3,2,1,0:T(2,128)S(1)}, f32[4,2,2,128]{3,2,1,0:T(2,128)S(1)}, u32[]{:S(2)}, u32[]{:S(2)}) %collective-permute-start.4) | collective-permute-done | bytes 8224 | tf_op jit(solution)/shard_map/ppermute | solution.py:220
  13.2 0.0 copy-done
  13.2 0.0 copy-done.1
  13.2 0.8 %images.1 = (f32[4,4,16,128]{3,2,1,0:T(8,128)S(1)}, f32[4,4,16,128]{3,2,1,0:T(8,128)S(1)}, f32[32,128]{1,0:T(8,128)S(1)}) custom-call(f32[4,9]{1,0:T(4,128)S(1)} %copy-done.1, f32[4,4,16,128]{3,2,1,0:T(8,128)S(1)} %copy-done, f32[4,4,16,128]{3,2,1,0:T(8,128)S(1)} %collective-permute-done.even_x, f32[4,4,16,128]{3,2,1,0:T(8,128)S(1)} %collective-permute-done.3.odd_x, ...), custom_call_target="tpu_custom_call" | custom-call | tf_op jit(solution)/shard_map/images/pallas_call | solution.py:252
  14.0 11.7 %all_to_all.11 = f32[32,1,128]{2,1,0:T(1,128)S(1)} all-to-all(f32[32,1,128]{2,1,0:T(1,128)S(1)} %bitcast.5), channel_id=1, replica_groups=mesh['gx'=8,'gy'=4] {'gx','gy'}, dimensions={0} | all-to-all | bytes 32768 | tf_op jit(solution)/shard_map/all_to_all | solution.py:266
  25.8 0.9 %combine.1 = (f32[4,4,16,128]{3,2,1,0:T(8,128)}, f32[4,5]{1,0:T(4,128)}) custom-call(f32[32,128]{1,0:T(8,128)S(1)} %bitcast.4, f32[4,4,16,128]{3,2,1,0:T(8,128)S(1)} %copy-done, f32[4,4,16,128]{3,2,1,0:T(8,128)S(1)} %get-tuple-element.12.image_one, f32[4,4,16,128]{3,2,1,0:T(8,128)S(1)} %get-tuple-element.13.image_two), custom_call_target="tpu_custom_call" | custom-call | tf_op jit(solution)/shard_map/combine/pallas_call | solution.py:268
  (4 shorter events, 0.1 us)
Async XLA Ops:
  0.6 7.8 %collective-permute-start = (f32[4,4,16,128]{3,2,1,0:T(8,128)}, f32[4,4,16,128]{3,2,1,0:T(8,128)S(1)}, u32[]{:S(2)}, u32[]{:S(2)}) collective-permute-start(f32[4,4,16,128]{3,2,1,0:T(8,128)} %field.3), channel_id=1, source_target_pairs={{0,4},{1,5},{2,6},{3,7},{4,0},{5,1},{6,2},{7,3},{8,12},{9,13},{10,... | collective-permute-start | bytes 393224 | tf_op jit(solution)/shard_map/ppermute | solution.py:220
  3.6 9.6 %copy-start = (f32[4,4,16,128]{3,2,1,0:T(8,128)S(1)}, f32[4,4,16,128]{3,2,1,0:T(8,128)}, u32[]{:S(2)}) copy-start(f32[4,4,16,128]{3,2,1,0:T(8,128)} %field.3) | copy-start | bytes 393220
  4.6 3.8 %collective-permute-start.2 = (f32[4,4,2,128]{3,2,1,0:T(2,128)S(1)}, f32[4,4,2,128]{3,2,1,0:T(2,128)S(1)}, u32[]{:S(2)}, u32[]{:S(2)}) collective-permute-start(f32[4,4,2,128]{3,2,1,0:T(2,128)S(1)} %get-tuple-element.14), channel_id=1, source_target_pairs={{0,8},{1,2},{2,1},{3,11},{4,12},{5,6},{6,5},{7,15},{8,0},{9,10},{1... | collective-permute-start | bytes 49160 | tf_op jit(solution)/shard_map/ppermute | solution.py:220
  6.2 2.2 %collective-permute-start.1 = (f32[4,4,2,128]{3,2,1,0:T(2,128)S(1)}, f32[4,4,2,128]{3,2,1,0:T(2,128)S(1)}, u32[]{:S(2)}, u32[]{:S(2)}) collective-permute-start(f32[4,4,2,128]{3,2,1,0:T(2,128)S(1)} %get-tuple-element.15), channel_id=1, source_target_pairs={{0,1},{1,0},{2,3},{3,2},{4,5},{5,4},{6,7},{7,6},{8,9},{9,8},{10,11... | collective-permute-start | bytes 49160 | tf_op jit(solution)/shard_map/ppermute | solution.py:220
  6.3 5.3 %collective-permute-start.3 = (f32[4,4,16,128]{3,2,1,0:T(8,128)}, f32[4,4,16,128]{3,2,1,0:T(8,128)S(1)}, u32[]{:S(2)}, u32[]{:S(2)}) collective-permute-start(f32[4,4,16,128]{3,2,1,0:T(8,128)} %field.3), channel_id=1, source_target_pairs={{0,1},{1,0},{2,3},{3,2},{4,8},{5,9},{6,10},{7,11},{8,4},{9,5},{10,... | collective-permute-start | bytes 393224 | tf_op jit(solution)/shard_map/ppermute | solution.py:220
  8.5 4.8 %copy-start.1 = (f32[4,9]{1,0:T(4,128)S(1)}, f32[4,9]{1,0:T(4,128)}, u32[]{:S(2)}) copy-start(f32[4,9]{1,0:T(4,128)} %rates.1) | copy-start | bytes 436
  8.5 3.1 %collective-permute-start.5 = (f32[4,2,2,128]{3,2,1,0:T(2,128)S(1)}, f32[4,2,2,128]{3,2,1,0:T(2,128)S(1)}, u32[]{:S(2)}, u32[]{:S(2)}) collective-permute-start(f32[4,2,2,128]{3,2,1,0:T(2,128)S(1)} %get-tuple-element.16), channel_id=1, source_target_pairs={{0,1},{1,0},{2,3},{3,2},{4,8},{5,9},{6,10},{7,11},{8,4},{9,5},{10,... | collective-permute-start | bytes 24584 | tf_op jit(solution)/shard_map/ppermute | solution.py:220
  8.6 4.7 %collective-permute-start.4 = (f32[4,2,2,128]{3,2,1,0:T(2,128)S(1)}, f32[4,2,2,128]{3,2,1,0:T(2,128)S(1)}, u32[]{:S(2)}, u32[]{:S(2)}) collective-permute-start(f32[4,2,2,128]{3,2,1,0:T(2,128)S(1)} %get-tuple-element.17), channel_id=1, source_target_pairs={{0,4},{1,5},{2,6},{3,7},{4,0},{5,1},{6,2},{7,3},{8,12},{9,13},{10,... | collective-permute-start | bytes 24584 | tf_op jit(solution)/shard_map/ppermute | solution.py:220

commit v4 on v2

--- a/solution.py
+++ b/solution.py
@@ -28,8 +28,6 @@
     odd_x,
     even_y,
     odd_y,
-    even_corners,
-    odd_corners,
     image_one,
     image_two,
     message,
@@ -55,12 +53,11 @@
     wide[:, :REACH, GAP : GAP + cols] = above
     wide[:, REACH + rows :, GAP : GAP + cols] = below
     left, right = sides(even_y[...], odd_y[...], even_j, first_j > 0, ends_j)
-    wide[:, REACH : REACH + rows, GAP - 2 : GAP] = left
-    wide[:, REACH : REACH + rows, GAP + cols : GAP + cols + 2] = right
-    upper, lower = sides(even_corners[...], odd_corners[...], even_i, first_i > 0, ends_i)
-    for corners, at in ((upper, REACH - HALF), (lower, REACH + rows)):
-        wide[:, at : at + HALF, GAP - 1 : GAP] = jnp.where(first_j > 0, corners[:, :, :1], 0.0)
-        wide[:, at : at + HALF, GAP + cols : GAP + cols + 1] = jnp.where(ends_j, corners[:, :, 1:], 0.0)
+    end = REACH + rows
+    for columns, at in ((left, GAP - 2), (right, GAP + cols)):
+        wide[:, HALF:REACH, at : at + 2] = jnp.where(first_i > 0, columns[:, :HALF], 0.0)
+        wide[:, REACH:end, at : at + 2] = columns[:, HALF : HALF + rows]
+        wide[:, end : end + HALF, at : at + 2] = jnp.where(ends_i, columns[:, HALF + rows :], 0.0)
 
     lane = lax.broadcasted_iota(jnp.int32, (1, depth), 1)
     amount_k = lane.astype(jnp.float32)
@@ -233,24 +230,24 @@
     else:
         even_x, odd_x = swaps("gx", size_x, parity_x, density[:, :REACH], density[:, rows - REACH :])
 
-    even_y, odd_y = swaps("gy", size_y, parity_y, density[:, :, :2], density[:, :, cols - 2 :])
-
-    even_x, even_y, odd_y = lax.optimization_barrier((even_x, even_y, odd_y))
-
-    def corners(first):
-        even, odd = even_y[:, first : first + HALF], odd_y[:, first : first + HALF]
-        left = jnp.where(parity_y == 0, odd, even)[:, :, 1:]
-        right = jnp.where(parity_y == 0, even, odd)[:, :, :1]
-        return jnp.concatenate([left, right], axis=2)
-
-    even_corners, odd_corners = swaps("gx", size_x, parity_x, corners(0), corners(rows - HALF))
+    low, high = density[:, :, :2], density[:, :, cols - 2 :]
+    sides = jnp.concatenate([low, high], axis=2)
+    even_near, odd_near = swaps("gx", size_x, parity_x, sides[:, :HALF], sides[:, rows - HALF :])
+    even_x, even_near, odd_near = lax.optimization_barrier((even_x, even_near, odd_near))
+    above = jnp.where(parity_x == 0, odd_near, even_near)
+    below = jnp.where(parity_x == 0, even_near, odd_near)
+
+    def edge(own, cut):
+        return jnp.concatenate([above[:, :, cut], own, below[:, :, cut]], axis=1)
+
+    even_y, odd_y = swaps("gy", size_y, parity_y, edge(low, slice(0, 2)), edge(high, slice(2, 4)))
 
     vmem = pl.BlockSpec(memory_space=pltpu.VMEM)
     block = jax.ShapeDtypeStruct(density.shape, jnp.float32)
     image_one, image_two, message = pl.pallas_call(
         functools.partial(images_kernel, (size_x * rows, size_y * cols)),
         out_shape=[block, block, jax.ShapeDtypeStruct((devices, 128), jnp.float32)],
-        in_specs=[vmem] * 8,
+        in_specs=[vmem] * 6,
         out_specs=[vmem, vmem, vmem],
         scratch_shapes=[
             pltpu.VMEM((members, rows + 2 * REACH, cols + 2 * GAP, depth), jnp.float32),
@@ -259,7 +256,7 @@
         ],
         compiler_params=pltpu.CompilerParams(vmem_limit_bytes=8 * 2**20),
         name="images",
-    )(rate_table, density, even_x, odd_x, even_y, odd_y, even_corners, odd_corners)
+    )(rate_table, density, even_x, odd_x, even_y, odd_y)
 
     gathered = lax.all_to_all(message, ("gx", "gy"), 0, 0, tiled=True)
 

time: 26.8 us -> 27.7 us (1.034)
  starting transfers between devices: 7.8 us -> 8.92 us
  other arithmetic: 1 us -> 0.06 us
  local copies, waits for them, and re-layouts: 0.02 us -> 0.91 us
    ppermute x6, starting transfers between devices: 7.8 us -> 8.92 us  [swap(): return lax.ppermute(value, ('gx', 'gy'), pairs)]
    select_n x2, other arithmetic: 0.98 us -> 0.05 us  [swaps(): jnp.where(is_even, initial, last)]
    slice x2, local copies, waits for them, and re-layouts: 0.01 us -> 0.9 us  [the longest x1 0.89 us: shards(): low, high = (density[:, :, :2], density[:, :, cols - 2:])]
  transfers between devices with their start and end apart: 6 -> 6, of which waited for: 2 -> 2; matrix products, arithmetic and copies ran while one was open for 4% -> 3% of each run, Pallas kernels for 0% -> 0%
where the time goes in v4:
time: 27.7 us; the launch traced here: 27.5 us
  blocking collectives  11.6 us (42%)
  starting transfers between devices  8.92 us (32%)
  waiting for transfers between devices  3.6 us (13%)
  Pallas kernels  1.68 us (6%)
  local copies, waits for them, and re-layouts  0.91 us (3%)
  between operations  0.71 us (3%)
    all_to_all x1, blocking collectives, shards(): gathered = lax.all_to_all(message, ('gx', 'gy'), 0, 0, tiled=True)  11.6 us
    ppermute x6, starting transfers between devices, swap(): return lax.ppermute(value, ('gx', 'gy'), pairs)  8.92 us
    ppermute x6, waiting for transfers between devices, swap(): return lax.ppermute(value, ('gx', 'gy'), pairs)  3.6 us
    slice x1, local copies, waits for them, and re-layouts, shards(): low, high = (density[:, :, :2], density[:, :, cols - 2:])  0.89 us
    pallas_call x1, Pallas kernels, shards(): pl.pallas_call(combine_kernel, out_shape=[block, jax.ShapeDtypeStruct((me...  0.87 us
    pallas_call x1, Pallas kernels, shards(): pl.pallas_call(functools.partial(images_kernel, (size_x * rows, size_y *...  0.81 us
  transfers between devices with their start and end apart: 6, of which 2 were waited for; matrix products, arithmetic and copies ran while one was open for 3% of the time, Pallas kernels for 0%

profile of v4, /device:TPU:0, one launch (start us, length us, event | category | flops | bytes accessed | tf_op | source)
XLA Modules:
  0.0 27.5 jit_solution(16015024239485350292)
XLA Ops:
  0.6 0.0 copy-start
  0.6 3.0 %collective-permute-start = (f32[4,4,16,128]{3,2,1,0:T(8,128)}, f32[4,4,16,128]{3,2,1,0:T(8,128)S(1)}, u32[]{:S(2)}, u32[]{:S(2)}) collective-permute-start(f32[4,4,16,128]{3,2,1,0:T(8,128)} %field.3), channel_id=1, source_target_pairs={{0,4},{1,5},{2,6},{3,7},{4,0},{5,1},{6,2},{7,3},{8,12},{9,13},{10,... | collective-permute-start | bytes 393224 | tf_op jit(solution)/shard_map/ppermute | solution.py:215
  3.6 0.9 %fusion.1 = (f32[4,4,2,128]{3,2,1,0:T(2,128)S(1)}, f32[4,4,2,128]{3,2,1,0:T(2,128)S(1)}) fusion(f32[4,4,16,128]{3,2,1,0:T(8,128)} %field.3), kind=kLoop, calls=%fused_computation.12 | loop fusion | bytes 65536 | tf_op jit(solution)/shard_map/slice | solution.py:233
  4.6 0.1 collective-permute-start.2
  4.7 3.0 %collective-permute-start.1 = (f32[4,2,4,128]{3,2,1,0:T(4,128)S(1)}, f32[4,2,4,128]{3,2,1,0:T(4,128)S(1)}, u32[]{:S(2)}, u32[]{:S(2)}) collective-permute-start(f32[4,2,4,128]{3,2,1,0:T(4,128)S(1)} %get-tuple-element.21), channel_id=1, source_target_pairs={{0,4},{1,5},{2,6},{3,7},{4,0},{5,1},{6,2},{7,3},{8,12},{9,13},{10,... | collective-permute-start | bytes 49160 | tf_op jit(solution)/shard_map/ppermute | solution.py:215
  7.7 0.0 copy-done
  7.7 0.0 collective-permute-start.3
  7.7 0.0 collective-permute-done.2
  7.7 1.7 %collective-permute-done.1 = f32[4,2,4,128]{3,2,1,0:T(4,128)S(1)} collective-permute-done((f32[4,2,4,128]{3,2,1,0:T(4,128)S(1)}, f32[4,2,4,128]{3,2,1,0:T(4,128)S(1)}, u32[]{:S(2)}, u32[]{:S(2)}) %collective-permute-start.1) | collective-permute-done | bytes 16416 | tf_op jit(solution)/shard_map/ppermute | solution.py:215
  9.4 0.0 collective-permute-done.even_x
  9.5 0.0 copy-start.1
  9.5 2.8 %collective-permute-start.5 = (f32[4,8,2,128]{3,2,1,0:T(2,128)S(1)}, f32[4,8,2,128]{3,2,1,0:T(2,128)S(1)}, u32[]{:S(2)}, u32[]{:S(2)}) collective-permute-start(f32[4,8,2,128]{3,2,1,0:T(2,128)S(1)} %get-tuple-element.16), channel_id=1, source_target_pairs={{0,4},{1,2},{2,1},{3,7},{4,0},{5,6},{6,5},{7,3},{8,12},{9,10},{10,... | collective-permute-start | bytes 98312 | tf_op jit(solution)/shard_map/ppermute | solution.py:215
  12.3 0.0 collective-permute-start.4
  12.3 0.0 collective-permute-done.3.odd_x
  12.3 1.9 %collective-permute-done.5.odd_y = f32[4,8,2,128]{3,2,1,0:T(2,128)S(1)} collective-permute-done((f32[4,8,2,128]{3,2,1,0:T(2,128)S(1)}, f32[4,8,2,128]{3,2,1,0:T(2,128)S(1)}, u32[]{:S(2)}, u32[]{:S(2)}) %collective-permute-start.5) | collective-permute-done | bytes 32800 | tf_op jit(solution)/shard_map/ppermute | solution.py:215
  14.2 0.0 collective-permute-done.4.even_y
  14.2 0.0 copy-done.1
  14.2 0.8 %images.1 = (f32[4,4,16,128]{3,2,1,0:T(8,128)S(1)}, f32[4,4,16,128]{3,2,1,0:T(8,128)S(1)}, f32[32,128]{1,0:T(8,128)S(1)}) custom-call(f32[4,9]{1,0:T(4,128)S(1)} %copy-done.1, f32[4,4,16,128]{3,2,1,0:T(8,128)S(1)} %copy-done, f32[4,4,16,128]{3,2,1,0:T(8,128)S(1)} %collective-permute-done.even_x, f32[4,4,16,128]{3,2,1,0:T(8,128)S(1)} %collective-permute-done.3.odd_x, ...), custom_call_target="tpu_custom_call" | custom-call | tf_op jit(solution)/shard_map/images/pallas_call | solution.py:247
  15.0 11.6 %all_to_all.11 = f32[32,1,128]{2,1,0:T(1,128)S(1)} all-to-all(f32[32,1,128]{2,1,0:T(1,128)S(1)} %bitcast.9), channel_id=1, replica_groups=mesh['gx'=8,'gy'=4] {'gx','gy'}, dimensions={0} | all-to-all | bytes 32768 | tf_op jit(solution)/shard_map/all_to_all | solution.py:261
  26.6 0.9 %combine.1 = (f32[4,4,16,128]{3,2,1,0:T(8,128)}, f32[4,5]{1,0:T(4,128)}) custom-call(f32[32,128]{1,0:T(8,128)S(1)} %bitcast.8, f32[4,4,16,128]{3,2,1,0:T(8,128)S(1)} %copy-done, f32[4,4,16,128]{3,2,1,0:T(8,128)S(1)} %get-tuple-element.12.image_one, f32[4,4,16,128]{3,2,1,0:T(8,128)S(1)} %get-tuple-element.13.image_two), custom_call_target="tpu_custom_call" | custom-call | tf_op jit(solution)/shard_map/combine/pallas_call | solution.py:263
  (4 shorter events, 0.1 us)
Async XLA Ops:
  0.6 7.1 %copy-start = (f32[4,4,16,128]{3,2,1,0:T(8,128)S(1)}, f32[4,4,16,128]{3,2,1,0:T(8,128)}, u32[]{:S(2)}) copy-start(f32[4,4,16,128]{3,2,1,0:T(8,128)} %field.3) | copy-start | bytes 393220
  0.6 8.8 %collective-permute-start = (f32[4,4,16,128]{3,2,1,0:T(8,128)}, f32[4,4,16,128]{3,2,1,0:T(8,128)S(1)}, u32[]{:S(2)}, u32[]{:S(2)}) collective-permute-start(f32[4,4,16,128]{3,2,1,0:T(8,128)} %field.3), channel_id=1, source_target_pairs={{0,4},{1,5},{2,6},{3,7},{4,0},{5,1},{6,2},{7,3},{8,12},{9,13},{10,... | collective-permute-start | bytes 393224 | tf_op jit(solution)/shard_map/ppermute | solution.py:215
  4.6 3.1 %collective-permute-start.2 = (f32[4,2,4,128]{3,2,1,0:T(4,128)S(1)}, f32[4,2,4,128]{3,2,1,0:T(4,128)S(1)}, u32[]{:S(2)}, u32[]{:S(2)}) collective-permute-start(f32[4,2,4,128]{3,2,1,0:T(4,128)S(1)} %get-tuple-element.20), channel_id=1, source_target_pairs={{0,1},{1,0},{2,3},{3,2},{4,8},{5,9},{6,10},{7,11},{8,4},{9,5},{10,... | collective-permute-start | bytes 49160 | tf_op jit(solution)/shard_map/ppermute | solution.py:215
  4.7 4.7 %collective-permute-start.1 = (f32[4,2,4,128]{3,2,1,0:T(4,128)S(1)}, f32[4,2,4,128]{3,2,1,0:T(4,128)S(1)}, u32[]{:S(2)}, u32[]{:S(2)}) collective-permute-start(f32[4,2,4,128]{3,2,1,0:T(4,128)S(1)} %get-tuple-element.21), channel_id=1, source_target_pairs={{0,4},{1,5},{2,6},{3,7},{4,0},{5,1},{6,2},{7,3},{8,12},{9,13},{10,... | collective-permute-start | bytes 49160 | tf_op jit(solution)/shard_map/ppermute | solution.py:215
  7.7 4.6 %collective-permute-start.3 = (f32[4,4,16,128]{3,2,1,0:T(8,128)S(1)}, f32[4,4,16,128]{3,2,1,0:T(8,128)S(1)}, u32[]{:S(2)}, u32[]{:S(2)}) collective-permute-start(f32[4,4,16,128]{3,2,1,0:T(8,128)S(1)} %copy-done), channel_id=1, source_target_pairs={{0,1},{1,0},{2,3},{3,2},{4,8},{5,9},{6,10},{7,11},{8,4},{9,5},{10,... | collective-permute-start | bytes 393224 | tf_op jit(solution)/shard_map/ppermute | solution.py:215
  9.5 4.7 %copy-start.1 = (f32[4,9]{1,0:T(4,128)S(1)}, f32[4,9]{1,0:T(4,128)}, u32[]{:S(2)}) copy-start(f32[4,9]{1,0:T(4,128)} %rates.1) | copy-start | bytes 436
  9.5 4.7 %collective-permute-start.5 = (f32[4,8,2,128]{3,2,1,0:T(2,128)S(1)}, f32[4,8,2,128]{3,2,1,0:T(2,128)S(1)}, u32[]{:S(2)}, u32[]{:S(2)}) collective-permute-start(f32[4,8,2,128]{3,2,1,0:T(2,128)S(1)} %get-tuple-element.16), channel_id=1, source_target_pairs={{0,4},{1,2},{2,1},{3,7},{4,0},{5,6},{6,5},{7,3},{8,12},{9,10},{10,... | collective-permute-start | bytes 98312 | tf_op jit(solution)/shard_map/ppermute | solution.py:215
  12.3 1.9 %collective-permute-start.4 = (f32[4,8,2,128]{3,2,1,0:T(2,128)S(1)}, f32[4,8,2,128]{3,2,1,0:T(2,128)S(1)}, u32[]{:S(2)}, u32[]{:S(2)}) collective-permute-start(f32[4,8,2,128]{3,2,1,0:T(2,128)S(1)} %get-tuple-element.17), channel_id=1, source_target_pairs={{0,1},{1,0},{2,3},{3,2},{4,5},{5,4},{6,7},{7,6},{8,9},{9,8},{10,11... | collective-permute-start | bytes 98312 | tf_op jit(solution)/shard_map/ppermute | solution.py:215

commit v5 on v2

--- a/solution.py
+++ b/solution.py
@@ -1,4 +1,5 @@
 import functools
+import math
 
 import jax
 import jax.numpy as jnp
@@ -13,6 +14,17 @@
 REACH = 4
 HALF = 2
 GAP = 8
+
+
+def edges_kernel(field, for_odd, for_even, block, arrived):
+    copy = pltpu.make_async_copy(field, block, arrived)
+    copy.start()
+    is_even = lax.axis_index("gy") % 2 == 0
+    cols = block.shape[2]
+    copy.wait()
+    low, high = block[:, :, :2], block[:, :, cols - 2 :]
+    for_even[...] = jnp.where(is_even, high, low)
+    for_odd[...] = jnp.where(is_even, low, high)
 
 
 def own_lane(first):
@@ -50,17 +62,25 @@
         lower, higher = jnp.where(is_even, odd, even), jnp.where(is_even, even, odd)
         return jnp.where(lower_inside, lower, 0.0), jnp.where(higher_inside, higher, 0.0)
 
-    wide[:, REACH : REACH + rows, GAP : GAP + cols] = field[...]
+    def place(row, start, values):
+        for at in range(values.shape[1]):
+            first = (row + REACH + at) * span + GAP + start
+            wide[:, first : first + values.shape[2]] = values[:, at]
+
+    def column(ref, member, row, at):
+        return ref[member, pl.ds(row * span + at, rows, stride=span), :]
+
+    place(0, 0, field[...])
     above, below = sides(even_x[...], odd_x[...], even_i, first_i > 0, ends_i)
-    wide[:, :REACH, GAP : GAP + cols] = above
-    wide[:, REACH + rows :, GAP : GAP + cols] = below
+    place(-REACH, 0, above)
+    place(rows, 0, below)
     left, right = sides(even_y[...], odd_y[...], even_j, first_j > 0, ends_j)
-    wide[:, REACH : REACH + rows, GAP - 2 : GAP] = left
-    wide[:, REACH : REACH + rows, GAP + cols : GAP + cols + 2] = right
+    place(0, -2, left)
+    place(0, cols, right)
     upper, lower = sides(even_corners[...], odd_corners[...], even_i, first_i > 0, ends_i)
-    for corners, at in ((upper, REACH - HALF), (lower, REACH + rows)):
-        wide[:, at : at + HALF, GAP - 1 : GAP] = jnp.where(first_j > 0, corners[:, :, :1], 0.0)
-        wide[:, at : at + HALF, GAP + cols : GAP + cols + 1] = jnp.where(ends_j, corners[:, :, 1:], 0.0)
+    for corners, row in ((upper, -HALF), (lower, rows)):
+        place(row, -1, jnp.where(first_j > 0, corners[:, :, :1], 0.0))
+        place(row, cols, jnp.where(ends_j, corners[:, :, 1:], 0.0))
 
     lane = lax.broadcasted_iota(jnp.int32, (1, depth), 1)
     amount_k = lane.astype(jnp.float32)
@@ -78,26 +98,27 @@
         lose_v = c[3] * (amount_j + 1.0)
         rest = make_u + make_v + (c[3] * amount_j + (c[5] + c[6]) * amount_k)
 
-        def apply(read, row, start, size):
-            i = (first_i + row).astype(jnp.float32)
+        def apply(read, row, start, size, i=None):
+            if i is None:
+                i = (first_i + row).astype(jnp.float32)
             cut = slice(GAP + start, GAP + start + size)
             centre = read(row, start, size)
             value = make_u[cut] * read(row - 1, start, size)
             value = value + (c[1] * (i + 1.0)) * read(row + 1, start, size)
             value = value + make_v * read(row, start - 1, size)
             value = value + lose_v[cut] * read(row, start + 1, size)
-            pair = (0.5 * c[4] * (i + 2.0) * (i + 1.0)) * read(row + 2, start, size)
-            value = value + inner_k * pltpu.roll(pair, 1, 1)
+            pair = pltpu.roll(read(row + 2, start, size), 1, 1)
+            value = value + (inner_k * (0.5 * c[4] * (i + 2.0) * (i + 1.0))) * pair
             split = c[5] * read(row - 2, start, size) + c[6] * centre
             value = value + above_k * pltpu.roll(split, depth - 1, 1)
             out = rest[cut] + (c[1] * i + 0.5 * c[4] * i * (i - 1.0))
             return value - out * centre
 
         def read_field(row, start, size):
-            return wide[member, row + REACH, pl.ds(GAP + start, size), :]
+            return wide[member, pl.ds((row + REACH) * span + GAP + start, size), :]
 
         def read_image(row, start, size):
-            return wide_image[member, row + HALF, pl.ds(GAP + start, size), :]
+            return wide_image[member, pl.ds((row + HALF) * span + GAP + start, size), :]
 
         for row in range(-HALF, rows + HALF):
             inside = (first_i + row >= 0) & (first_i + row < count_i)
@@ -106,14 +127,15 @@
                 value = jnp.where(inside, value, 0.0)
             else:
                 image_one[member, row] = value
-            wide_image[member, row + HALF, GAP : GAP + cols] = value
-            if 0 <= row < rows:
-                value = apply(read_field, row, -1, 1)
-                wide_image[member, row + HALF, GAP - 1 : GAP] = jnp.where(first_j > 0, value, 0.0)
-                value = apply(read_field, row, cols, 1)
-                wide_image[member, row + HALF, GAP + cols : GAP + cols + 1] = jnp.where(
-                    first_j + cols < count_j, value, 0.0
-                )
+            wide_image[member, pl.ds((row + HALF) * span + GAP, cols), :] = value
+
+        def read_side(row, start, size):
+            return column(wide, member, row + REACH, GAP + start)
+
+        i = (first_i + lax.broadcasted_iota(jnp.int32, (rows, depth), 0)).astype(jnp.float32)
+        for start, inside in ((-1, first_j > 0), (cols, ends_j)):
+            value = jnp.where(inside, apply(read_side, 0, start, 1, i), 0.0)
+            wide_image[member, pl.ds(HALF * span + GAP + start, rows, stride=span), :] = value
 
         products = [jnp.zeros((cols, depth), jnp.float32) for _ in range(6)]
         for row in range(rows):
@@ -135,22 +157,31 @@
     message[...] = jnp.broadcast_to(jnp.sum(row, axis=0, keepdims=True), message.shape)
 
 
+def product(left, right):
+    a, b, c, d = left
+    e, f, g, h = right
+    return a * e + b * g, a * f + b * h, c * e + d * g, c * f + d * h
+
+
 def first_column(h00, s01, h11):
     scale = tau_step / 2.0**squarings
-    a, b, d = scale * h00, scale * s01, scale * h11
-    c = scale
-    zero, one = jnp.zeros_like(a), jnp.ones_like(a)
-    p00, p01, p10, p11, q0, q1 = one, zero, zero, one, zero, zero
-    for term in range(taylor_terms, 0, -1):
-        inverse = 1.0 / term
-        p00, p01, p10, p11, q0, q1 = (
-            1.0 + (a * p00 + b * p10) * inverse,
-            (a * p01 + b * p11) * inverse,
-            (c * p00 + d * p10) * inverse,
-            1.0 + (c * p01 + d * p11) * inverse,
-            p10 * (c * inverse),
-            p11 * (c * inverse),
-        )
+    one = jnp.ones_like(h00)
+    z1 = (scale * h00, scale * s01, scale * one, scale * h11)
+    z2 = product(z1, z1)
+    z3, z4 = product(z2, z1), product(z2, z2)
+    weights = [1.0 / math.factorial(k + 1) for k in range(taylor_terms)]
+
+    def block(first):
+        w0, w1, w2, w3 = weights[first : first + 4]
+        terms = [w1 * p + w2 * q + w3 * r for p, q, r in zip(z1, z2, z3)]
+        return terms[0] + w0, terms[1], terms[2], terms[3] + w0
+
+    phi = block(taylor_terms - 4)
+    for first in range(taylor_terms - 8, -1, -4):
+        phi = tuple(p + q for p, q in zip(product(z4, phi), block(first)))
+    p00, p01, p10, p11 = product(z1, phi)
+    p00, p11 = 1.0 + p00, 1.0 + p11
+    q0, q1 = scale * phi[2], scale * phi[3]
     for _ in range(squarings):
         p00, p01, p10, p11, q0, q1 = (
             p00 * p00 + p01 * p10,
@@ -200,6 +231,7 @@
     members, rows, cols, depth = density.shape
     size_x, size_y = lax.axis_size("gx"), lax.axis_size("gy")
     devices = size_x * size_y
+    vmem = pl.BlockSpec(memory_space=pltpu.VMEM)
     parity_x, parity_y = lax.axis_index("gx") % 2, lax.axis_index("gy") % 2
 
     def swap(axis, size, first, value):
@@ -233,9 +265,21 @@
     else:
         even_x, odd_x = swaps("gx", size_x, parity_x, density[:, :REACH], density[:, rows - REACH :])
 
-    even_y, odd_y = swaps("gy", size_y, parity_y, density[:, :, :2], density[:, :, cols - 2 :])
-
-    even_x, even_y, odd_y = lax.optimization_barrier((even_x, even_y, odd_y))
+    edge = jax.ShapeDtypeStruct((members, rows, 2, depth), jnp.float32)
+    block = jax.ShapeDtypeStruct(density.shape, jnp.float32)
+    for_odd, for_even, field = pl.pallas_call(
+        edges_kernel,
+        out_shape=[edge, edge, block],
+        in_specs=[pl.BlockSpec(memory_space=pl.ANY)],
+        out_specs=[vmem] * 3,
+        scratch_shapes=[pltpu.SemaphoreType.DMA],
+        compiler_params=pltpu.CompilerParams(vmem_limit_bytes=4 * 2**20),
+        name="edges",
+    )(density)
+    odd_y = swap("gy", size_y, 1, for_odd)
+    even_y = swap("gy", size_y, 0, for_even)
+
+    even_x, odd_y, even_y = lax.optimization_barrier((even_x, odd_y, even_y))
 
     def corners(first):
         even, odd = even_y[:, first : first + HALF], odd_y[:, first : first + HALF]
@@ -245,21 +289,19 @@
 
     even_corners, odd_corners = swaps("gx", size_x, parity_x, corners(0), corners(rows - HALF))
 
-    vmem = pl.BlockSpec(memory_space=pltpu.VMEM)
-    block = jax.ShapeDtypeStruct(density.shape, jnp.float32)
     image_one, image_two, message = pl.pallas_call(
         functools.partial(images_kernel, (size_x * rows, size_y * cols)),
         out_shape=[block, block, jax.ShapeDtypeStruct((devices, 128), jnp.float32)],
         in_specs=[vmem] * 8,
         out_specs=[vmem, vmem, vmem],
         scratch_shapes=[
-            pltpu.VMEM((members, rows + 2 * REACH, cols + 2 * GAP, depth), jnp.float32),
-            pltpu.VMEM((members, rows + 2 * HALF, cols + 2 * GAP, depth), jnp.float32),
+            pltpu.VMEM((members, (rows + 2 * REACH) * (cols + 2 * GAP), depth), jnp.float32),
+            pltpu.VMEM((members, (rows + 2 * HALF) * (cols + 2 * GAP), depth), jnp.float32),
             pltpu.VMEM((48, depth), jnp.float32),
         ],
         compiler_params=pltpu.CompilerParams(vmem_limit_bytes=8 * 2**20),
         name="images",
-    )(rate_table, density, even_x, odd_x, even_y, odd_y, even_corners, odd_corners)
+    )(rate_table, field, even_x, odd_x, even_y, odd_y, even_corners, odd_corners)
 
     gathered = lax.all_to_all(message, ("gx", "gy"), 0, 0, tiled=True)
 
@@ -270,7 +312,7 @@
         out_specs=[vmem, vmem],
         compiler_params=pltpu.CompilerParams(vmem_limit_bytes=8 * 2**20),
         name="combine",
-    )(gathered, density, image_one, image_two)
+    )(gathered, field, image_one, image_two)
 
 
 def solution(mesh):

time: 26.8 us -> 26.7 us (level)
  other arithmetic: 1 us -> 0.05 us
  Pallas kernels: 1.67 us -> 2.55 us
    select_n x2 -> x1, other arithmetic: 0.98 us -> 0.02 us  [swaps(): jnp.where(is_even, initial, last)]
    pallas_call x0 -> x1, Pallas kernels: none -> 0.96 us  [shards(): pl.pallas_call(edges_kernel, out_shape=[edge, edge, block], in_specs=[pl....]
  transfers between devices with their start and end apart: 6 -> 6, of which waited for: 2 -> 2; matrix products, arithmetic and copies ran while one was open for 4% -> 0% of each run, Pallas kernels for 0% -> 4%
where the time goes in v5:
time: 26.7 us; the launch traced here: 26.6 us
  blocking collectives  11.7 us (44%)
  starting transfers between devices  7.8 us (29%)
  waiting for transfers between devices  3.73 us (14%)
  Pallas kernels  2.55 us (10%)
  between operations  0.69 us (3%)
    all_to_all x1, blocking collectives, shards(): gathered = lax.all_to_all(message, ('gx', 'gy'), 0, 0, tiled=True)  11.7 us
    ppermute x6, starting transfers between devices, swap(): return lax.ppermute(value, ('gx', 'gy'), pairs)  7.8 us
    ppermute x6, waiting for transfers between devices, swap(): return lax.ppermute(value, ('gx', 'gy'), pairs)  3.73 us
    pallas_call x1, Pallas kernels, shards(): pl.pallas_call(edges_kernel, out_shape=[edge, edge, block], in_specs=[pl....  0.96 us
    pallas_call x1, Pallas kernels, shards(): pl.pallas_call(combine_kernel, out_shape=[block, jax.ShapeDtypeStruct((me...  0.83 us
    pallas_call x1, Pallas kernels, shards(): pl.pallas_call(functools.partial(images_kernel, (size_x * rows, size_y *...  0.76 us
  transfers between devices with their start and end apart: 6, of which 2 were waited for; matrix products, arithmetic and copies ran while one was open for 0% of the time, Pallas kernels for 4%

profile of v5, /device:TPU:0, one launch (start us, length us, event | category | flops | bytes accessed | tf_op | source)
XLA Modules:
  0.0 26.6 jit_solution(9940996259254639554)
XLA Ops:
  0.6 3.0 %collective-permute-start = (f32[4,4,16,128]{3,2,1,0:T(8,128)}, f32[4,4,16,128]{3,2,1,0:T(8,128)S(1)}, u32[]{:S(2)}, u32[]{:S(2)}) collective-permute-start(f32[4,4,16,128]{3,2,1,0:T(8,128)} %field.1), channel_id=1, source_target_pairs={{0,4},{1,5},{2,6},{3,7},{4,0},{5,1},{6,2},{7,3},{8,12},{9,13},{10,... | collective-permute-start | bytes 393224 | tf_op jit(solution)/shard_map/ppermute | solution.py:250
  3.6 1.0 %edges.1 = (f32[4,4,2,128]{3,2,1,0:T(2,128)S(1)}, f32[4,4,2,128]{3,2,1,0:T(2,128)S(1)}, f32[4,4,16,128]{3,2,1,0:T(8,128)S(1)}) custom-call(f32[4,4,16,128]{3,2,1,0:T(8,128)} %field.1), custom_call_target="tpu_custom_call" | custom-call | tf_op jit(solution)/shard_map/edges/pallas_call | solution.py:270
  4.6 0.1 collective-permute-start.1
  4.7 1.6 %collective-permute-start.2 = (f32[4,4,2,128]{3,2,1,0:T(2,128)S(1)}, f32[4,4,2,128]{3,2,1,0:T(2,128)S(1)}, u32[]{:S(2)}, u32[]{:S(2)}) collective-permute-start(f32[4,4,2,128]{3,2,1,0:T(2,128)S(1)} %get-tuple-element.13), channel_id=1, source_target_pairs={{0,1},{1,0},{2,3},{3,2},{4,5},{5,4},{6,7},{7,6},{8,9},{9,8},{10,11... | collective-permute-start | bytes 49160 | tf_op jit(solution)/shard_map/ppermute | solution.py:250
  6.3 0.0 collective-permute-start.3
  6.3 2.1 %collective-permute-done.1.odd_y = f32[4,4,2,128]{3,2,1,0:T(2,128)S(1)} collective-permute-done((f32[4,4,2,128]{3,2,1,0:T(2,128)S(1)}, f32[4,4,2,128]{3,2,1,0:T(2,128)S(1)}, u32[]{:S(2)}, u32[]{:S(2)}) %collective-permute-start.1) | collective-permute-done | bytes 16416 | tf_op jit(solution)/shard_map/ppermute | solution.py:250
  8.4 0.0 collective-permute-done.2.even_y
  8.4 0.0 collective-permute-done.even_x
  8.5 0.0 copy-start
  8.5 0.1 collective-permute-start.5
  8.6 3.0 %collective-permute-start.4 = (f32[4,2,2,128]{3,2,1,0:T(2,128)S(1)}, f32[4,2,2,128]{3,2,1,0:T(2,128)S(1)}, u32[]{:S(2)}, u32[]{:S(2)}) collective-permute-start(f32[4,2,2,128]{3,2,1,0:T(2,128)S(1)} %get-tuple-element.21), channel_id=1, source_target_pairs={{0,4},{1,5},{2,6},{3,7},{4,0},{5,1},{6,2},{7,3},{8,12},{9,13},{10,... | collective-permute-start | bytes 24584 | tf_op jit(solution)/shard_map/ppermute | solution.py:250
  11.6 0.0 collective-permute-done.3.odd_x
  11.6 0.0 collective-permute-done.5.odd_corners
  11.6 1.6 %collective-permute-done.4.even_corners = f32[4,2,2,128]{3,2,1,0:T(2,128)S(1)} collective-permute-done((f32[4,2,2,128]{3,2,1,0:T(2,128)S(1)}, f32[4,2,2,128]{3,2,1,0:T(2,128)S(1)}, u32[]{:S(2)}, u32[]{:S(2)}) %collective-permute-start.4) | collective-permute-done | bytes 8224 | tf_op jit(solution)/shard_map/ppermute | solution.py:250
  13.2 0.0 copy-done
  13.2 0.8 %images.1 = (f32[4,4,16,128]{3,2,1,0:T(8,128)S(1)}, f32[4,4,16,128]{3,2,1,0:T(8,128)S(1)}, f32[32,128]{1,0:T(8,128)S(1)}) custom-call(f32[4,9]{1,0:T(4,128)S(1)} %copy-done, f32[4,4,16,128]{3,2,1,0:T(8,128)S(1)} %get-tuple-element.11.field, f32[4,4,16,128]{3,2,1,0:T(8,128)S(1)} %collective-permute-done.even_x, ...), custom_call_target="tpu_custom_call" | custom-call | tf_op jit(solution)/shard_map/images/pallas_call | solution.py:292
  14.0 11.7 %all_to_all.11 = f32[32,1,128]{2,1,0:T(1,128)S(1)} all-to-all(f32[32,1,128]{2,1,0:T(1,128)S(1)} %bitcast.5), channel_id=1, replica_groups=mesh['gx'=8,'gy'=4] {'gx','gy'}, dimensions={0} | all-to-all | bytes 32768 | tf_op jit(solution)/shard_map/all_to_all | solution.py:306
  25.7 0.8 %combine.1 = (f32[4,4,16,128]{3,2,1,0:T(8,128)}, f32[4,5]{1,0:T(4,128)}) custom-call(f32[32,128]{1,0:T(8,128)S(1)} %bitcast.4, f32[4,4,16,128]{3,2,1,0:T(8,128)S(1)} %get-tuple-element.11.field, f32[4,4,16,128]{3,2,1,0:T(8,128)S(1)} %get-tuple-element.18.image_one, f32[4,4,16,128]{3,2,1,0:T(8,128)S(1)} %get-tuple-element.19.image_two), custom_call_target="tpu_custom_call" | custom-call | tf_op jit(solution)/shard_map/combine/pallas_call | solution.py:308
  (4 shorter events, 0.1 us)
Async XLA Ops:
  0.6 7.8 %collective-permute-start = (f32[4,4,16,128]{3,2,1,0:T(8,128)}, f32[4,4,16,128]{3,2,1,0:T(8,128)S(1)}, u32[]{:S(2)}, u32[]{:S(2)}) collective-permute-start(f32[4,4,16,128]{3,2,1,0:T(8,128)} %field.1), channel_id=1, source_target_pairs={{0,4},{1,5},{2,6},{3,7},{4,0},{5,1},{6,2},{7,3},{8,12},{9,13},{10,... | collective-permute-start | bytes 393224 | tf_op jit(solution)/shard_map/ppermute | solution.py:250
  4.6 3.8 %collective-permute-start.1 = (f32[4,4,2,128]{3,2,1,0:T(2,128)S(1)}, f32[4,4,2,128]{3,2,1,0:T(2,128)S(1)}, u32[]{:S(2)}, u32[]{:S(2)}) collective-permute-start(f32[4,4,2,128]{3,2,1,0:T(2,128)S(1)} %get-tuple-element.12), channel_id=1, source_target_pairs={{0,4},{1,2},{2,1},{3,7},{4,0},{5,6},{6,5},{7,3},{8,12},{9,10},{10,... | collective-permute-start | bytes 49160 | tf_op jit(solution)/shard_map/ppermute | solution.py:250
  4.7 3.7 %collective-permute-start.2 = (f32[4,4,2,128]{3,2,1,0:T(2,128)S(1)}, f32[4,4,2,128]{3,2,1,0:T(2,128)S(1)}, u32[]{:S(2)}, u32[]{:S(2)}) collective-permute-start(f32[4,4,2,128]{3,2,1,0:T(2,128)S(1)} %get-tuple-element.13), channel_id=1, source_target_pairs={{0,1},{1,0},{2,3},{3,2},{4,5},{5,4},{6,7},{7,6},{8,9},{9,8},{10,11... | collective-permute-start | bytes 49160 | tf_op jit(solution)/shard_map/ppermute | solution.py:250
  6.3 5.3 %collective-permute-start.3 = (f32[4,4,16,128]{3,2,1,0:T(8,128)}, f32[4,4,16,128]{3,2,1,0:T(8,128)S(1)}, u32[]{:S(2)}, u32[]{:S(2)}) collective-permute-start(f32[4,4,16,128]{3,2,1,0:T(8,128)} %field.1), channel_id=1, source_target_pairs={{0,1},{1,0},{2,3},{3,2},{4,8},{5,9},{6,10},{7,11},{8,4},{9,5},{10,... | collective-permute-start | bytes 393224 | tf_op jit(solution)/shard_map/ppermute | solution.py:250
  8.5 4.7 %copy-start = (f32[4,9]{1,0:T(4,128)S(1)}, f32[4,9]{1,0:T(4,128)}, u32[]{:S(2)}) copy-start(f32[4,9]{1,0:T(4,128)} %rates.1) | copy-start | bytes 436
  8.5 3.1 %collective-permute-start.5 = (f32[4,2,2,128]{3,2,1,0:T(2,128)S(1)}, f32[4,2,2,128]{3,2,1,0:T(2,128)S(1)}, u32[]{:S(2)}, u32[]{:S(2)}) collective-permute-start(f32[4,2,2,128]{3,2,1,0:T(2,128)S(1)} %get-tuple-element.20), channel_id=1, source_target_pairs={{0,1},{1,0},{2,3},{3,2},{4,8},{5,9},{6,10},{7,11},{8,4},{9,5},{10,... | collective-permute-start | bytes 24584 | tf_op jit(solution)/shard_map/ppermute | solution.py:250
  8.6 4.7 %collective-permute-start.4 = (f32[4,2,2,128]{3,2,1,0:T(2,128)S(1)}, f32[4,2,2,128]{3,2,1,0:T(2,128)S(1)}, u32[]{:S(2)}, u32[]{:S(2)}) collective-permute-start(f32[4,2,2,128]{3,2,1,0:T(2,128)S(1)} %get-tuple-element.21), channel_id=1, source_target_pairs={{0,4},{1,5},{2,6},{3,7},{4,0},{5,1},{6,2},{7,3},{8,12},{9,13},{10,... | collective-permute-start | bytes 24584 | tf_op jit(solution)/shard_map/ppermute | solution.py:250

commit v6 on v5

--- a/solution.py
+++ b/solution.py
@@ -32,6 +32,41 @@
     return lax.broadcasted_iota(jnp.int32, (8, 128), 1) == first + row
 
 
+def lanes(depth):
+    lane = lax.broadcasted_iota(jnp.int32, (1, depth), 1)
+    amount_k = lane.astype(jnp.float32)
+    return amount_k, jnp.where(lane < depth - 1, amount_k + 1.0, 0.0), jnp.where(lane > 0, 1.0, 0.0)
+
+
+def apply(c, depth, i, make_u, make_v, lose_v, rest, centre, rows_by, left, right):
+    _, above_k, inner_k = lanes(depth)
+    value = make_u * rows_by(-1) + (c[1] * (i + 1.0)) * rows_by(1)
+    value = value + make_v * left
+    value = value + lose_v * right
+    pair = pltpu.roll(rows_by(2), 1, 1)
+    value = value + (inner_k * (0.5 * c[4] * (i + 2.0) * (i + 1.0))) * pair
+    split = c[5] * rows_by(-2) + c[6] * centre
+    value = value + above_k * pltpu.roll(split, depth - 1, 1)
+    out = rest + (c[1] * i + 0.5 * c[4] * i * (i - 1.0))
+    return value - out * centre
+
+
+def constants(rates, member, depth, amount_j):
+    c = [jnp.broadcast_to(rates[member : member + 1, r : r + 1], (1, depth)) for r in range(9)]
+    amount_k = lanes(depth)[0]
+    ratio_j, ratio_k = amount_j / c[7], amount_k / c[8]
+    make_u = c[0] / (1.0 + ratio_j * ratio_j)
+    make_v = c[2] / (1.0 + ratio_k * ratio_k)
+    lose_v = c[3] * (amount_j + 1.0)
+    rest = make_u + make_v + (c[3] * amount_j + (c[5] + c[6]) * amount_k)
+    return c, make_u, make_v, lose_v, rest
+
+
+def sides(even, odd, is_even, lower_inside, higher_inside):
+    lower, higher = jnp.where(is_even, odd, even), jnp.where(is_even, even, odd)
+    return jnp.where(lower_inside, lower, 0.0), jnp.where(higher_inside, higher, 0.0)
+
+
 def images_kernel(
     lattice,
     rates,
@@ -40,120 +75,146 @@
     odd_x,
     even_y,
     odd_y,
-    even_corners,
-    odd_corners,
     image_one,
     image_two,
-    message,
+    lines,
+    parts,
     wide,
     wide_image,
-    parts,
 ):
     members, rows, cols, depth = field.shape
     span = cols + 2 * GAP
+    tall = rows + 2 * HALF
     index_i, index_j = lax.axis_index("gx"), lax.axis_index("gy")
     first_i, first_j = index_i * rows, index_j * cols
     even_i, even_j = index_i % 2 == 0, index_j % 2 == 0
     count_i, count_j = lattice
 
-    ends_i, ends_j = first_i + rows < count_i, first_j + cols < count_j
-
-    def sides(even, odd, is_even, lower_inside, higher_inside):
-        lower, higher = jnp.where(is_even, odd, even), jnp.where(is_even, even, odd)
-        return jnp.where(lower_inside, lower, 0.0), jnp.where(higher_inside, higher, 0.0)
-
     def place(row, start, values):
         for at in range(values.shape[1]):
             first = (row + REACH + at) * span + GAP + start
             wide[:, first : first + values.shape[2]] = values[:, at]
 
-    def column(ref, member, row, at):
-        return ref[member, pl.ds(row * span + at, rows, stride=span), :]
-
     place(0, 0, field[...])
-    above, below = sides(even_x[...], odd_x[...], even_i, first_i > 0, ends_i)
+    above, below = sides(even_x[...], odd_x[...], even_i, first_i > 0, first_i + rows < count_i)
     place(-REACH, 0, above)
     place(rows, 0, below)
-    left, right = sides(even_y[...], odd_y[...], even_j, first_j > 0, ends_j)
+    left, right = sides(even_y[...], odd_y[...], even_j, first_j > 0, first_j + cols < count_j)
     place(0, -2, left)
     place(0, cols, right)
-    upper, lower = sides(even_corners[...], odd_corners[...], even_i, first_i > 0, ends_i)
-    for corners, row in ((upper, -HALF), (lower, rows)):
-        place(row, -1, jnp.where(first_j > 0, corners[:, :, :1], 0.0))
-        place(row, cols, jnp.where(ends_j, corners[:, :, 1:], 0.0))
-
-    lane = lax.broadcasted_iota(jnp.int32, (1, depth), 1)
-    amount_k = lane.astype(jnp.float32)
-    above_k = jnp.where(lane < depth - 1, amount_k + 1.0, 0.0)
-    inner_k = jnp.where(lane > 0, 1.0, 0.0)
+    corner = jnp.zeros((members, HALF, 1, depth), jnp.float32)
+    for row in (-HALF, rows):
+        place(row, -1, corner)
+        place(row, cols, corner)
+
     sublane = lax.broadcasted_iota(jnp.int32, (span, 1), 0)
     amount_j = (first_j - GAP + sublane).astype(jnp.float32)
+    place_j = lax.broadcasted_iota(jnp.int32, (cols, depth), 0)
+    inner_j = (place_j > 0) & (place_j < cols - 1)
 
     for member in range(members):
-        c = [jnp.broadcast_to(rates[member : member + 1, r : r + 1], (1, depth)) for r in range(9)]
-        ratio_j = amount_j / c[7]
-        ratio_k = amount_k / c[8]
-        make_u = c[0] / (1.0 + ratio_j * ratio_j)
-        make_v = c[2] / (1.0 + ratio_k * ratio_k)
-        lose_v = c[3] * (amount_j + 1.0)
-        rest = make_u + make_v + (c[3] * amount_j + (c[5] + c[6]) * amount_k)
-
-        def apply(read, row, start, size, i=None):
-            if i is None:
-                i = (first_i + row).astype(jnp.float32)
-            cut = slice(GAP + start, GAP + start + size)
-            centre = read(row, start, size)
-            value = make_u[cut] * read(row - 1, start, size)
-            value = value + (c[1] * (i + 1.0)) * read(row + 1, start, size)
-            value = value + make_v * read(row, start - 1, size)
-            value = value + lose_v[cut] * read(row, start + 1, size)
-            pair = pltpu.roll(read(row + 2, start, size), 1, 1)
-            value = value + (inner_k * (0.5 * c[4] * (i + 2.0) * (i + 1.0))) * pair
-            split = c[5] * read(row - 2, start, size) + c[6] * centre
-            value = value + above_k * pltpu.roll(split, depth - 1, 1)
-            out = rest[cut] + (c[1] * i + 0.5 * c[4] * i * (i - 1.0))
-            return value - out * centre
-
-        def read_field(row, start, size):
-            return wide[member, pl.ds((row + REACH) * span + GAP + start, size), :]
-
-        def read_image(row, start, size):
-            return wide_image[member, pl.ds((row + HALF) * span + GAP + start, size), :]
+        c, make_u, make_v, lose_v, rest = constants(rates, member, depth, amount_j)
+        make_u, lose_v, rest = [term[GAP : GAP + cols] for term in (make_u, lose_v, rest)]
+
+        def image(read, row):
+            i = (first_i + row).astype(jnp.float32)
+            rows_by = lambda by: read(row + by, 0)
+            return apply(c, depth, i, make_u, make_v, lose_v, rest, read(row, 0), rows_by, read(row, -1), read(row, 1))
+
+        def read_field(row, start):
+            return wide[member, pl.ds((row + REACH) * span + GAP + start, cols), :]
+
+        def read_image(row, start):
+            return wide_image[member, pl.ds((row + HALF) * span + GAP + start, cols), :]
 
         for row in range(-HALF, rows + HALF):
             inside = (first_i + row >= 0) & (first_i + row < count_i)
-            value = apply(read_field, row, 0, cols)
+            value = image(read_field, row)
             if row < 0 or row >= rows:
                 value = jnp.where(inside, value, 0.0)
             else:
                 image_one[member, row] = value
             wide_image[member, pl.ds((row + HALF) * span + GAP, cols), :] = value
 
-        def read_side(row, start, size):
-            return column(wide, member, row + REACH, GAP + start)
-
-        i = (first_i + lax.broadcasted_iota(jnp.int32, (rows, depth), 0)).astype(jnp.float32)
-        for start, inside in ((-1, first_j > 0), (cols, ends_j)):
-            value = jnp.where(inside, apply(read_side, 0, start, 1, i), 0.0)
-            wide_image[member, pl.ds(HALF * span + GAP + start, rows, stride=span), :] = value
-
         products = [jnp.zeros((cols, depth), jnp.float32) for _ in range(6)]
         for row in range(rows):
             zero = field[member, row]
             one = image_one[member, row]
-            two = apply(read_image, row, 0, cols)
+            two = jnp.where(inner_j, image(read_image, row), 0.0)
             image_two[member, row] = two
             terms = (zero * zero, zero * one, zero * two, one * one, one * two, two * two)
             products = [total + term for total, term in zip(products, terms)]
         for index, total in enumerate(products):
             parts[8 * index + member : 8 * index + member + 1, :] = jnp.sum(total, axis=0, keepdims=True)
 
+        for at, column in enumerate((0, cols - 1, 1, cols - 2)):
+            lines[member, at] = wide_image[member, pl.ds(GAP + column, tall, stride=span), :]
+        for at, column in enumerate((0, cols - 1, -1, cols, -2, cols + 1)):
+            lines[member, 4 + at] = wide[member, pl.ds(HALF * span + GAP + column, tall, stride=span), :]
+
     for index in range(6):
         parts[8 * index + members : 8 * index + 8, :] = jnp.zeros((8 - members, depth), jnp.float32)
+
+
+def corners_kernel(lattice, cols, rates, lines, odd_corners, even_corners, parts, columns_two, message, edge, total):
+    members, _, tall, depth = lines.shape
+    rows = tall - 2 * HALF
+    index_i, index_j = lax.axis_index("gx"), lax.axis_index("gy")
+    first_i, first_j = index_i * rows, index_j * cols
+    count_i, count_j = lattice
+    upper, lower = sides(
+        even_corners[...], odd_corners[...], index_i % 2 == 0, first_i > 0, first_i + rows < count_i
+    )
+    i = (first_i + lax.broadcasted_iota(jnp.int32, (rows, depth), 0)).astype(jnp.float32)
+    total[...] = parts[...]
+    for member in range(members):
+
+        def line(at):
+            return lines[member, at, pl.ds(HALF, rows), :]
+
+        sums = [jnp.zeros((rows, depth), jnp.float32) for _ in range(3)]
+        for side, column, beyond, inside in (
+            (0, 0, -1, first_j > 0),
+            (1, cols - 1, cols, first_j + cols < count_j),
+        ):
+
+            def at_column(column):
+                amount_j = jnp.broadcast_to((first_j + column).astype(jnp.float32), (1, depth))
+                return constants(rates, member, depth, amount_j)
+
+            outer, fixed = edge.at[member, side, 0], edge.at[member, side, 1]
+            outer[HALF : HALF + rows, :] = line(6 + side)
+            for row in range(HALF):
+                for first, corner in ((0, upper), (HALF + rows, lower)):
+                    value = corner[member, row, side : side + 1, :]
+                    outer[first + row : first + row + 1, :] = jnp.where(inside, value, 0.0)
+
+            c, make_u, make_v, lose_v, rest = at_column(beyond)
+            rows_by = lambda by: outer[pl.ds(HALF + by, rows), :]
+            beside = (line(8), line(4)) if side == 0 else (line(5), line(9))
+            value = apply(c, depth, i, make_u, make_v, lose_v, rest, rows_by(0), rows_by, *beside)
+            image_beyond = jnp.where(inside, value, 0.0)
+
+            c, make_u, make_v, lose_v, rest = at_column(column)
+            gain = make_v if side == 0 else lose_v
+            fixed[...] = lines[member, side]
+            for first in (0, HALF + rows):
+                fixed[first : first + HALF, :] = fixed[first : first + HALF, :] + gain * outer[first : first + HALF, :]
+
+            rows_by = lambda by: fixed[pl.ds(HALF + by, rows), :]
+            beside = (image_beyond, line(2)) if side == 0 else (line(3), image_beyond)
+            two = apply(c, depth, i, make_u, make_v, lose_v, rest, rows_by(0), rows_by, *beside)
+            columns_two[member, side] = two
+            terms = (line(4 + side) * two, line(side) * two, two * two)
+            sums = [value + term for value, term in zip(sums, terms)]
+        for index, value in zip((2, 4, 5), sums):
+            at = 8 * index + member
+            total[at : at + 1, :] = total[at : at + 1, :] + jnp.sum(value, axis=0, keepdims=True)
+
     row = jnp.zeros((8, depth), jnp.float32)
     for index in range(6):
-        total = jnp.sum(parts[8 * index : 8 * index + 8], axis=1, keepdims=True)
-        row = row + jnp.where(own_lane(8 * index), total, 0.0)
+        value = jnp.sum(total[8 * index : 8 * index + 8], axis=1, keepdims=True)
+        row = row + jnp.where(own_lane(8 * index), value, 0.0)
     message[...] = jnp.broadcast_to(jnp.sum(row, axis=0, keepdims=True), message.shape)
 
 
@@ -194,7 +255,7 @@
     return p00, p10, q0
 
 
-def combine_kernel(gathered, field, image_one, image_two, propagated, entries):
+def combine_kernel(gathered, field, image_one, image_two, columns_two, propagated, entries):
     members, rows, cols, depth = field.shape
     sums = jnp.broadcast_to(jnp.sum(gathered[...], axis=0, keepdims=True), (8, 128))
     g00, g01, g02, g11, g12, g22 = [
@@ -219,12 +280,13 @@
     for index, entry in enumerate((h00, h10, h01, h11)):
         table = jnp.where(lane == index, entry, table)
     entries[...] = (tau_step * table)[: entries.shape[0], : entries.shape[1]]
+    place_j = lax.broadcasted_iota(jnp.int32, (cols, depth), 0)
     for member in range(members):
         b0, b1, b2 = [jnp.broadcast_to(a[member : member + 1], (cols, depth)) for a in (a0, a1, a2)]
         for row in range(rows):
-            propagated[member, row] = (
-                b0 * field[member, row] + b1 * image_one[member, row] + b2 * image_two[member, row]
-            )
+            two = jnp.where(place_j == 0, columns_two[member, 0, row : row + 1], image_two[member, row])
+            two = jnp.where(place_j == cols - 1, columns_two[member, 1, row : row + 1], two)
+            propagated[member, row] = b0 * field[member, row] + b1 * image_one[member, row] + b2 * two
 
 
 def shards(density, rate_table):
@@ -289,30 +351,52 @@
 
     even_corners, odd_corners = swaps("gx", size_x, parity_x, corners(0), corners(rows - HALF))
 
-    image_one, image_two, message = pl.pallas_call(
-        functools.partial(images_kernel, (size_x * rows, size_y * cols)),
-        out_shape=[block, block, jax.ShapeDtypeStruct((devices, 128), jnp.float32)],
-        in_specs=[vmem] * 8,
-        out_specs=[vmem, vmem, vmem],
+    lattice = (size_x * rows, size_y * cols)
+    tall, span = rows + 2 * HALF, cols + 2 * GAP
+    image_one, image_two, lines, parts = pl.pallas_call(
+        functools.partial(images_kernel, lattice),
+        out_shape=[
+            block,
+            block,
+            jax.ShapeDtypeStruct((members, 10, tall, depth), jnp.float32),
+            jax.ShapeDtypeStruct((48, depth), jnp.float32),
+        ],
+        in_specs=[vmem] * 6,
+        out_specs=[vmem] * 4,
         scratch_shapes=[
-            pltpu.VMEM((members, (rows + 2 * REACH) * (cols + 2 * GAP), depth), jnp.float32),
-            pltpu.VMEM((members, (rows + 2 * HALF) * (cols + 2 * GAP), depth), jnp.float32),
-            pltpu.VMEM((48, depth), jnp.float32),
+            pltpu.VMEM((members, (rows + 2 * REACH) * span, depth), jnp.float32),
+            pltpu.VMEM((members, tall * span, depth), jnp.float32),
         ],
         compiler_params=pltpu.CompilerParams(vmem_limit_bytes=8 * 2**20),
         name="images",
-    )(rate_table, field, even_x, odd_x, even_y, odd_y, even_corners, odd_corners)
+    )(rate_table, field, even_x, odd_x, even_y, odd_y)
+
+    columns_two, message = pl.pallas_call(
+        functools.partial(corners_kernel, lattice, cols),
+        out_shape=[
+            jax.ShapeDtypeStruct((members, 2, rows, depth), jnp.float32),
+            jax.ShapeDtypeStruct((devices, 128), jnp.float32),
+        ],
+        in_specs=[vmem] * 5,
+        out_specs=[vmem, vmem],
+        scratch_shapes=[
+            pltpu.VMEM((members, 2, 2, tall, depth), jnp.float32),
+            pltpu.VMEM((48, depth), jnp.float32),
+        ],
+        compiler_params=pltpu.CompilerParams(vmem_limit_bytes=4 * 2**20),
+        name="corners",
+    )(rate_table, lines, odd_corners, even_corners, parts)
 
     gathered = lax.all_to_all(message, ("gx", "gy"), 0, 0, tiled=True)
 
     return pl.pallas_call(
         combine_kernel,
         out_shape=[block, jax.ShapeDtypeStruct((members, 5), jnp.float32)],
-        in_specs=[vmem] * 4,
+        in_specs=[vmem] * 5,
         out_specs=[vmem, vmem],
         compiler_params=pltpu.CompilerParams(vmem_limit_bytes=8 * 2**20),
         name="combine",
-    )(gathered, field, image_one, image_two)
+    )(gathered, field, image_one, image_two, columns_two)
 
 
 def solution(mesh):

time: 26.7 us -> 26.3 us (0.985)
  waiting for transfers between devices: 3.73 us -> 3.06 us
    ppermute x6, waiting for transfers between devices: 3.73 us -> 3.06 us  [swap(): return lax.ppermute(value, ('gx', 'gy'), pairs)]
    pallas_call x1 -> x2, Pallas kernels: 0.76 us -> 1.02 us  [the longest x1 0.65 us: shards(): pl.pallas_call(functools.partial(images_kernel, lattice), out_shape=[bloc...]
  transfers between devices with their start and end apart: 6 -> 6, of which waited for: 2 -> 2; matrix products, arithmetic and copies ran while one was open for 0% -> 0% of each run, Pallas kernels for 4% -> 6%
where the time goes in v6:
time: 26.3 us; the launch traced here: 26.2 us
  blocking collectives  11.7 us (44%)
  starting transfers between devices  7.8 us (30%)
  waiting for transfers between devices  3.06 us (12%)
  Pallas kernels  2.81 us (11%)
  between operations  0.71 us (3%)
    all_to_all x1, blocking collectives, shards(): gathered = lax.all_to_all(message, ('gx', 'gy'), 0, 0, tiled=True)  11.7 us
    ppermute x6, starting transfers between devices, swap(): return lax.ppermute(value, ('gx', 'gy'), pairs)  7.8 us
    ppermute x6, waiting for transfers between devices, swap(): return lax.ppermute(value, ('gx', 'gy'), pairs)  3.06 us
    pallas_call x1, Pallas kernels, shards(): pl.pallas_call(edges_kernel, out_shape=[edge, edge, block], in_specs=[pl....  0.96 us
    pallas_call x1, Pallas kernels, shards(): pl.pallas_call(combine_kernel, out_shape=[block, jax.ShapeDtypeStruct((me...  0.83 us
    pallas_call x1, Pallas kernels, shards(): pl.pallas_call(functools.partial(images_kernel, lattice), out_shape=[bloc...  0.65 us
  transfers between devices with their start and end apart: 6, of which 2 were waited for; matrix products, arithmetic and copies ran while one was open for 0% of the time, Pallas kernels for 6%

profile of v6, /device:TPU:0, one launch (start us, length us, event | category | flops | bytes accessed | tf_op | source)
XLA Modules:
  0.0 26.2 jit_solution(9096661015676286992)
XLA Ops:
  0.6 3.0 %collective-permute-start = (f32[4,4,16,128]{3,2,1,0:T(8,128)}, f32[4,4,16,128]{3,2,1,0:T(8,128)S(1)}, u32[]{:S(2)}, u32[]{:S(2)}) collective-permute-start(f32[4,4,16,128]{3,2,1,0:T(8,128)} %field.1), channel_id=1, source_target_pairs={{0,4},{1,5},{2,6},{3,7},{4,0},{5,1},{6,2},{7,3},{8,12},{9,13},{10,... | collective-permute-start | bytes 393224 | tf_op jit(solution)/shard_map/ppermute | solution.py:312
  3.6 1.0 %edges.1 = (f32[4,4,2,128]{3,2,1,0:T(2,128)S(1)}, f32[4,4,2,128]{3,2,1,0:T(2,128)S(1)}, f32[4,4,16,128]{3,2,1,0:T(8,128)S(1)}) custom-call(f32[4,4,16,128]{3,2,1,0:T(8,128)} %field.1), custom_call_target="tpu_custom_call" | custom-call | tf_op jit(solution)/shard_map/edges/pallas_call | solution.py:332
  4.6 0.1 collective-permute-start.1
  4.7 1.6 %collective-permute-start.2 = (f32[4,4,2,128]{3,2,1,0:T(2,128)S(1)}, f32[4,4,2,128]{3,2,1,0:T(2,128)S(1)}, u32[]{:S(2)}, u32[]{:S(2)}) collective-permute-start(f32[4,4,2,128]{3,2,1,0:T(2,128)S(1)} %get-tuple-element.16), channel_id=1, source_target_pairs={{0,1},{1,0},{2,3},{3,2},{4,5},{5,4},{6,7},{7,6},{8,9},{9,8},{10,11... | collective-permute-start | bytes 49160 | tf_op jit(solution)/shard_map/ppermute | solution.py:312
  6.3 0.0 collective-permute-start.3
  6.3 2.1 %collective-permute-done.1.odd_y = f32[4,4,2,128]{3,2,1,0:T(2,128)S(1)} collective-permute-done((f32[4,4,2,128]{3,2,1,0:T(2,128)S(1)}, f32[4,4,2,128]{3,2,1,0:T(2,128)S(1)}, u32[]{:S(2)}, u32[]{:S(2)}) %collective-permute-start.1) | collective-permute-done | bytes 16416 | tf_op jit(solution)/shard_map/ppermute | solution.py:312
  8.4 0.0 collective-permute-done.2.even_y
  8.4 0.0 collective-permute-done.even_x
  8.5 0.0 copy-start
  8.5 0.1 collective-permute-start.4
  8.6 3.0 %collective-permute-start.5 = (f32[4,2,2,128]{3,2,1,0:T(2,128)S(1)}, f32[4,2,2,128]{3,2,1,0:T(2,128)S(1)}, u32[]{:S(2)}, u32[]{:S(2)}) collective-permute-start(f32[4,2,2,128]{3,2,1,0:T(2,128)S(1)} %get-tuple-element.26), channel_id=1, source_target_pairs={{0,4},{1,5},{2,6},{3,7},{4,0},{5,1},{6,2},{7,3},{8,12},{9,13},{10,... | collective-permute-start | bytes 24584 | tf_op jit(solution)/shard_map/ppermute | solution.py:312
  11.6 0.0 collective-permute-done.3.odd_x
  11.6 0.0 copy-done
  11.6 0.7 %images.1 = (f32[4,4,16,128]{3,2,1,0:T(8,128)S(1)}, f32[4,4,16,128]{3,2,1,0:T(8,128)S(1)}, f32[4,10,8,128]{3,2,1,0:T(8,128)S(1)}, f32[48,128]{1,0:T(8,128)S(1)}) custom-call(f32[4,9]{1,0:T(4,128)S(1)} %copy-done, f32[4,4,16,128]{3,2,1,0:T(8,128)S(1)} %get-tuple-element.14.field, f32[4,4,16,128]{3,2,1,0:T(8,128)S(1)} %collective-permute-done.even_x, ...), custom_call_target="tpu_custom_call" | custom-call | tf_op jit(solution)/shard_map/images/pallas_call | solution.py:356
  12.3 0.0 collective-permute-done.4.odd_corners
  12.3 1.0 %collective-permute-done.5.even_corners = f32[4,2,2,128]{3,2,1,0:T(2,128)S(1)} collective-permute-done((f32[4,2,2,128]{3,2,1,0:T(2,128)S(1)}, f32[4,2,2,128]{3,2,1,0:T(2,128)S(1)}, u32[]{:S(2)}, u32[]{:S(2)}) %collective-permute-start.5) | collective-permute-done | bytes 8224 | tf_op jit(solution)/shard_map/ppermute | solution.py:312
  13.2 0.4 %corners.1 = (f32[4,2,4,128]{3,2,1,0:T(4,128)S(1)}, f32[32,128]{1,0:T(8,128)S(1)}) custom-call(f32[4,9]{1,0:T(4,128)S(1)} %copy-done, f32[4,10,8,128]{3,2,1,0:T(8,128)S(1)} %get-tuple-element.20.lines, f32[4,2,2,128]{3,2,1,0:T(2,128)S(1)} %collective-permute-done.4.odd_corners, f32[4,2,2,128]{3,2,1,0:T(2,128)S(1)} %collective-permute-done.5.even_corners, ...), custom_call_target="tpu_custom_call" | custom-call | tf_op jit(solution)/shard_map/corners/pallas_call | solution.py:374
  13.6 11.7 %all_to_all.11 = f32[32,1,128]{2,1,0:T(1,128)S(1)} all-to-all(f32[32,1,128]{2,1,0:T(1,128)S(1)} %bitcast.5), channel_id=1, replica_groups=mesh['gx'=8,'gy'=4] {'gx','gy'}, dimensions={0} | all-to-all | bytes 32768 | tf_op jit(solution)/shard_map/all_to_all | solution.py:390
  25.4 0.8 %combine.1 = (f32[4,4,16,128]{3,2,1,0:T(8,128)}, f32[4,5]{1,0:T(4,128)}) custom-call(f32[32,128]{1,0:T(8,128)S(1)} %bitcast.4, f32[4,4,16,128]{3,2,1,0:T(8,128)S(1)} %get-tuple-element.14.field, f32[4,4,16,128]{3,2,1,0:T(8,128)S(1)} %get-tuple-element.23.image_one, f32[4,4,16,128]{3,2,1,0:T(8,128)S(1)} %get-tuple-element.24.image_two, ...), custom_call_target="tpu_custom_call" | custom-call | tf_op jit(solution)/shard_map/combine/pallas_call | solution.py:392
  (4 shorter events, 0.1 us)
Async XLA Ops:
  0.6 7.8 %collective-permute-start = (f32[4,4,16,128]{3,2,1,0:T(8,128)}, f32[4,4,16,128]{3,2,1,0:T(8,128)S(1)}, u32[]{:S(2)}, u32[]{:S(2)}) collective-permute-start(f32[4,4,16,128]{3,2,1,0:T(8,128)} %field.1), channel_id=1, source_target_pairs={{0,4},{1,5},{2,6},{3,7},{4,0},{5,1},{6,2},{7,3},{8,12},{9,13},{10,... | collective-permute-start | bytes 393224 | tf_op jit(solution)/shard_map/ppermute | solution.py:312
  4.6 3.8 %collective-permute-start.1 = (f32[4,4,2,128]{3,2,1,0:T(2,128)S(1)}, f32[4,4,2,128]{3,2,1,0:T(2,128)S(1)}, u32[]{:S(2)}, u32[]{:S(2)}) collective-permute-start(f32[4,4,2,128]{3,2,1,0:T(2,128)S(1)} %get-tuple-element.15), channel_id=1, source_target_pairs={{0,4},{1,2},{2,1},{3,7},{4,0},{5,6},{6,5},{7,3},{8,12},{9,10},{10,... | collective-permute-start | bytes 49160 | tf_op jit(solution)/shard_map/ppermute | solution.py:312
  4.7 3.7 %collective-permute-start.2 = (f32[4,4,2,128]{3,2,1,0:T(2,128)S(1)}, f32[4,4,2,128]{3,2,1,0:T(2,128)S(1)}, u32[]{:S(2)}, u32[]{:S(2)}) collective-permute-start(f32[4,4,2,128]{3,2,1,0:T(2,128)S(1)} %get-tuple-element.16), channel_id=1, source_target_pairs={{0,1},{1,0},{2,3},{3,2},{4,5},{5,4},{6,7},{7,6},{8,9},{9,8},{10,11... | collective-permute-start | bytes 49160 | tf_op jit(solution)/shard_map/ppermute | solution.py:312
  6.3 5.3 %collective-permute-start.3 = (f32[4,4,16,128]{3,2,1,0:T(8,128)}, f32[4,4,16,128]{3,2,1,0:T(8,128)S(1)}, u32[]{:S(2)}, u32[]{:S(2)}) collective-permute-start(f32[4,4,16,128]{3,2,1,0:T(8,128)} %field.1), channel_id=1, source_target_pairs={{0,1},{1,0},{2,3},{3,2},{4,8},{5,9},{6,10},{7,11},{8,4},{9,5},{10,... | collective-permute-start | bytes 393224 | tf_op jit(solution)/shard_map/ppermute | solution.py:312
  8.5 3.1 %copy-start = (f32[4,9]{1,0:T(4,128)S(1)}, f32[4,9]{1,0:T(4,128)}, u32[]{:S(2)}) copy-start(f32[4,9]{1,0:T(4,128)} %rates.3) | copy-start | bytes 436
  8.5 3.8 %collective-permute-start.4 = (f32[4,2,2,128]{3,2,1,0:T(2,128)S(1)}, f32[4,2,2,128]{3,2,1,0:T(2,128)S(1)}, u32[]{:S(2)}, u32[]{:S(2)}) collective-permute-start(f32[4,2,2,128]{3,2,1,0:T(2,128)S(1)} %get-tuple-element.27), channel_id=1, source_target_pairs={{0,1},{1,0},{2,3},{3,2},{4,8},{5,9},{6,10},{7,11},{8,4},{9,5},{10,... | collective-permute-start | bytes 24584 | tf_op jit(solution)/shard_map/ppermute | solution.py:312
  8.6 4.7 %collective-permute-start.5 = (f32[4,2,2,128]{3,2,1,0:T(2,128)S(1)}, f32[4,2,2,128]{3,2,1,0:T(2,128)S(1)}, u32[]{:S(2)}, u32[]{:S(2)}) collective-permute-start(f32[4,2,2,128]{3,2,1,0:T(2,128)S(1)} %get-tuple-element.26), channel_id=1, source_target_pairs={{0,4},{1,5},{2,6},{3,7},{4,0},{5,1},{6,2},{7,3},{8,12},{9,13},{10,... | collective-permute-start | bytes 24584 | tf_op jit(solution)/shard_map/ppermute | solution.py:312

commit v7 on v6

--- a/solution.py
+++ b/solution.py
@@ -52,7 +52,8 @@
 
 
 def constants(rates, member, depth, amount_j):
-    c = [jnp.broadcast_to(rates[member : member + 1, r : r + 1], (1, depth)) for r in range(9)]
+    row = rates[pl.ds(member, 1), :]
+    c = [jnp.broadcast_to(row[:, r : r + 1], (1, depth)) for r in range(9)]
     amount_k = lanes(depth)[0]
     ratio_j, ratio_k = amount_j / c[7], amount_k / c[8]
     make_u = c[0] / (1.0 + ratio_j * ratio_j)
@@ -112,7 +113,8 @@
     place_j = lax.broadcasted_iota(jnp.int32, (cols, depth), 0)
     inner_j = (place_j > 0) & (place_j < cols - 1)
 
-    for member in range(members):
+    @pl.loop(0, members)
+    def _(member):
         c, make_u, make_v, lose_v, rest = constants(rates, member, depth, amount_j)
         make_u, lose_v, rest = [term[GAP : GAP + cols] for term in (make_u, lose_v, rest)]
 
@@ -145,7 +147,7 @@
             terms = (zero * zero, zero * one, zero * two, one * one, one * two, two * two)
             products = [total + term for total, term in zip(products, terms)]
         for index, total in enumerate(products):
-            parts[8 * index + member : 8 * index + member + 1, :] = jnp.sum(total, axis=0, keepdims=True)
+            parts[pl.ds(8 * index + member, 1), :] = jnp.sum(total, axis=0, keepdims=True)
 
         for at, column in enumerate((0, cols - 1, 1, cols - 2)):
             lines[member, at] = wide_image[member, pl.ds(GAP + column, tall, stride=span), :]

time: 26.3 us -> 26.5 us (level)
  Pallas kernels: 2.81 us -> 3.4 us
  waiting for transfers between devices: 3.06 us -> 2.47 us
    ppermute x6, waiting for transfers between devices: 3.06 us -> 2.47 us  [swap(): return lax.ppermute(value, ('gx', 'gy'), pairs)]
    pallas_call x1, Pallas kernels: 0.65 us -> 1.24 us  [shards(): pl.pallas_call(functools.partial(images_kernel, lattice), out_shape=[bloc...]
  transfers between devices with their start and end apart: 6 -> 6, of which waited for: 2 -> 2; matrix products, arithmetic and copies ran while one was open for 0% -> 0% of each run, Pallas kernels for 6% -> 8%
where the time goes in v7:
time: 26.5 us; the launch traced here: 26.4 us
  blocking collectives  11.9 us (45%)
  starting transfers between devices  7.8 us (29%)
  Pallas kernels  3.4 us (13%)
  waiting for transfers between devices  2.47 us (9%)
  between operations  0.71 us (3%)
    all_to_all x1, blocking collectives, shards(): gathered = lax.all_to_all(message, ('gx', 'gy'), 0, 0, tiled=True)  11.9 us
    ppermute x6, starting transfers between devices, swap(): return lax.ppermute(value, ('gx', 'gy'), pairs)  7.8 us
    ppermute x6, waiting for transfers between devices, swap(): return lax.ppermute(value, ('gx', 'gy'), pairs)  2.47 us
    pallas_call x1, Pallas kernels, shards(): pl.pallas_call(functools.partial(images_kernel, lattice), out_shape=[bloc...  1.24 us
    pallas_call x1, Pallas kernels, shards(): pl.pallas_call(edges_kernel, out_shape=[edge, edge, block], in_specs=[pl....  0.96 us
    pallas_call x1, Pallas kernels, shards(): pl.pallas_call(combine_kernel, out_shape=[block, jax.ShapeDtypeStruct((me...  0.83 us
  transfers between devices with their start and end apart: 6, of which 2 were waited for; matrix products, arithmetic and copies ran while one was open for 0% of the time, Pallas kernels for 8%

profile of v7, /device:TPU:0, one launch (start us, length us, event | category | flops | bytes accessed | tf_op | source)
XLA Modules:
  0.0 26.4 jit_solution(10951474939619407167)
XLA Ops:
  0.6 3.0 %collective-permute-start = (f32[4,4,16,128]{3,2,1,0:T(8,128)}, f32[4,4,16,128]{3,2,1,0:T(8,128)S(1)}, u32[]{:S(2)}, u32[]{:S(2)}) collective-permute-start(f32[4,4,16,128]{3,2,1,0:T(8,128)} %field.1), channel_id=1, source_target_pairs={{0,4},{1,5},{2,6},{3,7},{4,0},{5,1},{6,2},{7,3},{8,12},{9,13},{10,... | collective-permute-start | bytes 393224 | tf_op jit(solution)/shard_map/ppermute | solution.py:314
  3.6 1.0 %edges.1 = (f32[4,4,2,128]{3,2,1,0:T(2,128)S(1)}, f32[4,4,2,128]{3,2,1,0:T(2,128)S(1)}, f32[4,4,16,128]{3,2,1,0:T(8,128)S(1)}) custom-call(f32[4,4,16,128]{3,2,1,0:T(8,128)} %field.1), custom_call_target="tpu_custom_call" | custom-call | tf_op jit(solution)/shard_map/edges/pallas_call | solution.py:334
  4.6 0.1 collective-permute-start.1
  4.7 1.6 %collective-permute-start.2 = (f32[4,4,2,128]{3,2,1,0:T(2,128)S(1)}, f32[4,4,2,128]{3,2,1,0:T(2,128)S(1)}, u32[]{:S(2)}, u32[]{:S(2)}) collective-permute-start(f32[4,4,2,128]{3,2,1,0:T(2,128)S(1)} %get-tuple-element.16), channel_id=1, source_target_pairs={{0,1},{1,0},{2,3},{3,2},{4,5},{5,4},{6,7},{7,6},{8,9},{9,8},{10,11... | collective-permute-start | bytes 49160 | tf_op jit(solution)/shard_map/ppermute | solution.py:314
  6.3 0.0 collective-permute-start.3
  6.3 2.1 %collective-permute-done.1.odd_y = f32[4,4,2,128]{3,2,1,0:T(2,128)S(1)} collective-permute-done((f32[4,4,2,128]{3,2,1,0:T(2,128)S(1)}, f32[4,4,2,128]{3,2,1,0:T(2,128)S(1)}, u32[]{:S(2)}, u32[]{:S(2)}) %collective-permute-start.1) | collective-permute-done | bytes 16416 | tf_op jit(solution)/shard_map/ppermute | solution.py:314
  8.4 0.0 collective-permute-done.2.even_y
  8.4 0.0 collective-permute-done.even_x
  8.5 0.0 copy-start
  8.5 0.1 collective-permute-start.4
  8.6 3.0 %collective-permute-start.5 = (f32[4,2,2,128]{3,2,1,0:T(2,128)S(1)}, f32[4,2,2,128]{3,2,1,0:T(2,128)S(1)}, u32[]{:S(2)}, u32[]{:S(2)}) collective-permute-start(f32[4,2,2,128]{3,2,1,0:T(2,128)S(1)} %get-tuple-element.26), channel_id=1, source_target_pairs={{0,4},{1,5},{2,6},{3,7},{4,0},{5,1},{6,2},{7,3},{8,12},{9,13},{10,... | collective-permute-start | bytes 24584 | tf_op jit(solution)/shard_map/ppermute | solution.py:314
  11.6 0.0 collective-permute-done.3.odd_x
  11.6 0.0 copy-done
  11.6 1.2 %images.1 = (f32[4,4,16,128]{3,2,1,0:T(8,128)S(1)}, f32[4,4,16,128]{3,2,1,0:T(8,128)S(1)}, f32[4,10,8,128]{3,2,1,0:T(8,128)S(1)}, f32[48,128]{1,0:T(8,128)S(1)}) custom-call(f32[4,9]{1,0:T(4,128)S(1)} %copy-done, f32[4,4,16,128]{3,2,1,0:T(8,128)S(1)} %get-tuple-element.14.field, f32[4,4,16,128]{3,2,1,0:T(8,128)S(1)} %collective-permute-done.even_x, ...), custom_call_target="tpu_custom_call" | custom-call | tf_op jit(solution)/shard_map/images/pallas_call | solution.py:358
  12.9 0.0 collective-permute-done.4.odd_corners
  12.9 0.4 %collective-permute-done.5.even_corners = f32[4,2,2,128]{3,2,1,0:T(2,128)S(1)} collective-permute-done((f32[4,2,2,128]{3,2,1,0:T(2,128)S(1)}, f32[4,2,2,128]{3,2,1,0:T(2,128)S(1)}, u32[]{:S(2)}, u32[]{:S(2)}) %collective-permute-start.5) | collective-permute-done | bytes 8224 | tf_op jit(solution)/shard_map/ppermute | solution.py:314
  13.2 0.4 %corners.1 = (f32[4,2,4,128]{3,2,1,0:T(4,128)S(1)}, f32[32,128]{1,0:T(8,128)S(1)}) custom-call(f32[4,9]{1,0:T(4,128)S(1)} %copy-done, f32[4,10,8,128]{3,2,1,0:T(8,128)S(1)} %get-tuple-element.20.lines, f32[4,2,2,128]{3,2,1,0:T(2,128)S(1)} %collective-permute-done.4.odd_corners, f32[4,2,2,128]{3,2,1,0:T(2,128)S(1)} %collective-permute-done.5.even_corners, ...), custom_call_target="tpu_custom_call" | custom-call | tf_op jit(solution)/shard_map/corners/pallas_call | solution.py:376
  13.6 11.9 %all_to_all.11 = f32[32,1,128]{2,1,0:T(1,128)S(1)} all-to-all(f32[32,1,128]{2,1,0:T(1,128)S(1)} %bitcast.5), channel_id=1, replica_groups=mesh['gx'=8,'gy'=4] {'gx','gy'}, dimensions={0} | all-to-all | bytes 32768 | tf_op jit(solution)/shard_map/all_to_all | solution.py:392
  25.6 0.8 %combine.1 = (f32[4,4,16,128]{3,2,1,0:T(8,128)}, f32[4,5]{1,0:T(4,128)}) custom-call(f32[32,128]{1,0:T(8,128)S(1)} %bitcast.4, f32[4,4,16,128]{3,2,1,0:T(8,128)S(1)} %get-tuple-element.14.field, f32[4,4,16,128]{3,2,1,0:T(8,128)S(1)} %get-tuple-element.23.image_one, f32[4,4,16,128]{3,2,1,0:T(8,128)S(1)} %get-tuple-element.24.image_two, ...), custom_call_target="tpu_custom_call" | custom-call | tf_op jit(solution)/shard_map/combine/pallas_call | solution.py:394
  (4 shorter events, 0.1 us)
Async XLA Ops:
  0.6 7.8 %collective-permute-start = (f32[4,4,16,128]{3,2,1,0:T(8,128)}, f32[4,4,16,128]{3,2,1,0:T(8,128)S(1)}, u32[]{:S(2)}, u32[]{:S(2)}) collective-permute-start(f32[4,4,16,128]{3,2,1,0:T(8,128)} %field.1), channel_id=1, source_target_pairs={{0,4},{1,5},{2,6},{3,7},{4,0},{5,1},{6,2},{7,3},{8,12},{9,13},{10,... | collective-permute-start | bytes 393224 | tf_op jit(solution)/shard_map/ppermute | solution.py:314
  4.6 3.8 %collective-permute-start.1 = (f32[4,4,2,128]{3,2,1,0:T(2,128)S(1)}, f32[4,4,2,128]{3,2,1,0:T(2,128)S(1)}, u32[]{:S(2)}, u32[]{:S(2)}) collective-permute-start(f32[4,4,2,128]{3,2,1,0:T(2,128)S(1)} %get-tuple-element.15), channel_id=1, source_target_pairs={{0,4},{1,2},{2,1},{3,7},{4,0},{5,6},{6,5},{7,3},{8,12},{9,10},{10,... | collective-permute-start | bytes 49160 | tf_op jit(solution)/shard_map/ppermute | solution.py:314
  4.7 3.7 %collective-permute-start.2 = (f32[4,4,2,128]{3,2,1,0:T(2,128)S(1)}, f32[4,4,2,128]{3,2,1,0:T(2,128)S(1)}, u32[]{:S(2)}, u32[]{:S(2)}) collective-permute-start(f32[4,4,2,128]{3,2,1,0:T(2,128)S(1)} %get-tuple-element.16), channel_id=1, source_target_pairs={{0,1},{1,0},{2,3},{3,2},{4,5},{5,4},{6,7},{7,6},{8,9},{9,8},{10,11... | collective-permute-start | bytes 49160 | tf_op jit(solution)/shard_map/ppermute | solution.py:314
  6.3 5.3 %collective-permute-start.3 = (f32[4,4,16,128]{3,2,1,0:T(8,128)}, f32[4,4,16,128]{3,2,1,0:T(8,128)S(1)}, u32[]{:S(2)}, u32[]{:S(2)}) collective-permute-start(f32[4,4,16,128]{3,2,1,0:T(8,128)} %field.1), channel_id=1, source_target_pairs={{0,1},{1,0},{2,3},{3,2},{4,8},{5,9},{6,10},{7,11},{8,4},{9,5},{10,... | collective-permute-start | bytes 393224 | tf_op jit(solution)/shard_map/ppermute | solution.py:314
  8.5 3.1 %copy-start = (f32[4,9]{1,0:T(4,128)S(1)}, f32[4,9]{1,0:T(4,128)}, u32[]{:S(2)}) copy-start(f32[4,9]{1,0:T(4,128)} %rates.3) | copy-start | bytes 436
  8.5 4.4 %collective-permute-start.4 = (f32[4,2,2,128]{3,2,1,0:T(2,128)S(1)}, f32[4,2,2,128]{3,2,1,0:T(2,128)S(1)}, u32[]{:S(2)}, u32[]{:S(2)}) collective-permute-start(f32[4,2,2,128]{3,2,1,0:T(2,128)S(1)} %get-tuple-element.27), channel_id=1, source_target_pairs={{0,1},{1,0},{2,3},{3,2},{4,8},{5,9},{6,10},{7,11},{8,4},{9,5},{10,... | collective-permute-start | bytes 24584 | tf_op jit(solution)/shard_map/ppermute | solution.py:314
  8.6 4.7 %collective-permute-start.5 = (f32[4,2,2,128]{3,2,1,0:T(2,128)S(1)}, f32[4,2,2,128]{3,2,1,0:T(2,128)S(1)}, u32[]{:S(2)}, u32[]{:S(2)}) collective-permute-start(f32[4,2,2,128]{3,2,1,0:T(2,128)S(1)} %get-tuple-element.26), channel_id=1, source_target_pairs={{0,4},{1,5},{2,6},{3,7},{4,0},{5,1},{6,2},{7,3},{8,12},{9,13},{10,... | collective-permute-start | bytes 24584 | tf_op jit(solution)/shard_map/ppermute | solution.py:314

commit v8 on v6

--- a/solution.py
+++ b/solution.py
@@ -387,7 +387,7 @@
         name="corners",
     )(rate_table, lines, odd_corners, even_corners, parts)
 
-    gathered = lax.all_to_all(message, ("gx", "gy"), 0, 0, tiled=True)
+    gathered = lax.all_to_all(message, ("gy", "gx"), 0, 0, tiled=True)
 
     return pl.pallas_call(
         combine_kernel,

time: 26.3 us -> 26.3 us (level)
  no operation moved by 1% of the time
where the time goes in v8:
time: 26.3 us; the launch traced here: 26.2 us
  blocking collectives  11.7 us (44%)
  starting transfers between devices  7.8 us (30%)
  waiting for transfers between devices  3.06 us (12%)
  Pallas kernels  2.81 us (11%)
  between operations  0.71 us (3%)
    all_to_all x1, blocking collectives, shards(): gathered = lax.all_to_all(message, ('gy', 'gx'), 0, 0, tiled=True)  11.7 us
    ppermute x6, starting transfers between devices, swap(): return lax.ppermute(value, ('gx', 'gy'), pairs)  7.8 us
    ppermute x6, waiting for transfers between devices, swap(): return lax.ppermute(value, ('gx', 'gy'), pairs)  3.06 us
    pallas_call x1, Pallas kernels, shards(): pl.pallas_call(edges_kernel, out_shape=[edge, edge, block], in_specs=[pl....  0.96 us
    pallas_call x1, Pallas kernels, shards(): pl.pallas_call(combine_kernel, out_shape=[block, jax.ShapeDtypeStruct((me...  0.83 us
    pallas_call x1, Pallas kernels, shards(): pl.pallas_call(functools.partial(images_kernel, lattice), out_shape=[bloc...  0.65 us
  transfers between devices with their start and end apart: 6, of which 2 were waited for; matrix products, arithmetic and copies ran while one was open for 0% of the time, Pallas kernels for 6%

profile of v8, /device:TPU:0, one launch (start us, length us, event | category | flops | bytes accessed | tf_op | source)
XLA Modules:
  0.0 26.2 jit_solution(2502449394231920909)
XLA Ops:
  0.6 3.0 %collective-permute-start = (f32[4,4,16,128]{3,2,1,0:T(8,128)}, f32[4,4,16,128]{3,2,1,0:T(8,128)S(1)}, u32[]{:S(2)}, u32[]{:S(2)}) collective-permute-start(f32[4,4,16,128]{3,2,1,0:T(8,128)} %field.1), channel_id=1, source_target_pairs={{0,4},{1,5},{2,6},{3,7},{4,0},{5,1},{6,2},{7,3},{8,12},{9,13},{10,... | collective-permute-start | bytes 393224 | tf_op jit(solution)/shard_map/ppermute | solution.py:312
  3.6 1.0 %edges.1 = (f32[4,4,2,128]{3,2,1,0:T(2,128)S(1)}, f32[4,4,2,128]{3,2,1,0:T(2,128)S(1)}, f32[4,4,16,128]{3,2,1,0:T(8,128)S(1)}) custom-call(f32[4,4,16,128]{3,2,1,0:T(8,128)} %field.1), custom_call_target="tpu_custom_call" | custom-call | tf_op jit(solution)/shard_map/edges/pallas_call | solution.py:332
  4.6 0.1 collective-permute-start.1
  4.7 1.6 %collective-permute-start.2 = (f32[4,4,2,128]{3,2,1,0:T(2,128)S(1)}, f32[4,4,2,128]{3,2,1,0:T(2,128)S(1)}, u32[]{:S(2)}, u32[]{:S(2)}) collective-permute-start(f32[4,4,2,128]{3,2,1,0:T(2,128)S(1)} %get-tuple-element.16), channel_id=1, source_target_pairs={{0,1},{1,0},{2,3},{3,2},{4,5},{5,4},{6,7},{7,6},{8,9},{9,8},{10,11... | collective-permute-start | bytes 49160 | tf_op jit(solution)/shard_map/ppermute | solution.py:312
  6.3 0.0 collective-permute-start.3
  6.3 2.1 %collective-permute-done.1.odd_y = f32[4,4,2,128]{3,2,1,0:T(2,128)S(1)} collective-permute-done((f32[4,4,2,128]{3,2,1,0:T(2,128)S(1)}, f32[4,4,2,128]{3,2,1,0:T(2,128)S(1)}, u32[]{:S(2)}, u32[]{:S(2)}) %collective-permute-start.1) | collective-permute-done | bytes 16416 | tf_op jit(solution)/shard_map/ppermute | solution.py:312
  8.4 0.0 collective-permute-done.2.even_y
  8.4 0.0 collective-permute-done.even_x
  8.5 0.0 copy-start
  8.5 0.1 collective-permute-start.4
  8.6 3.0 %collective-permute-start.5 = (f32[4,2,2,128]{3,2,1,0:T(2,128)S(1)}, f32[4,2,2,128]{3,2,1,0:T(2,128)S(1)}, u32[]{:S(2)}, u32[]{:S(2)}) collective-permute-start(f32[4,2,2,128]{3,2,1,0:T(2,128)S(1)} %get-tuple-element.26), channel_id=1, source_target_pairs={{0,4},{1,5},{2,6},{3,7},{4,0},{5,1},{6,2},{7,3},{8,12},{9,13},{10,... | collective-permute-start | bytes 24584 | tf_op jit(solution)/shard_map/ppermute | solution.py:312
  11.6 0.0 collective-permute-done.3.odd_x
  11.6 0.0 copy-done
  11.6 0.7 %images.1 = (f32[4,4,16,128]{3,2,1,0:T(8,128)S(1)}, f32[4,4,16,128]{3,2,1,0:T(8,128)S(1)}, f32[4,10,8,128]{3,2,1,0:T(8,128)S(1)}, f32[48,128]{1,0:T(8,128)S(1)}) custom-call(f32[4,9]{1,0:T(4,128)S(1)} %copy-done, f32[4,4,16,128]{3,2,1,0:T(8,128)S(1)} %get-tuple-element.14.field, f32[4,4,16,128]{3,2,1,0:T(8,128)S(1)} %collective-permute-done.even_x, ...), custom_call_target="tpu_custom_call" | custom-call | tf_op jit(solution)/shard_map/images/pallas_call | solution.py:356
  12.3 0.0 collective-permute-done.4.odd_corners
  12.3 1.0 %collective-permute-done.5.even_corners = f32[4,2,2,128]{3,2,1,0:T(2,128)S(1)} collective-permute-done((f32[4,2,2,128]{3,2,1,0:T(2,128)S(1)}, f32[4,2,2,128]{3,2,1,0:T(2,128)S(1)}, u32[]{:S(2)}, u32[]{:S(2)}) %collective-permute-start.5) | collective-permute-done | bytes 8224 | tf_op jit(solution)/shard_map/ppermute | solution.py:312
  13.2 0.4 %corners.1 = (f32[4,2,4,128]{3,2,1,0:T(4,128)S(1)}, f32[32,128]{1,0:T(8,128)S(1)}) custom-call(f32[4,9]{1,0:T(4,128)S(1)} %copy-done, f32[4,10,8,128]{3,2,1,0:T(8,128)S(1)} %get-tuple-element.20.lines, f32[4,2,2,128]{3,2,1,0:T(2,128)S(1)} %collective-permute-done.4.odd_corners, f32[4,2,2,128]{3,2,1,0:T(2,128)S(1)} %collective-permute-done.5.even_corners, ...), custom_call_target="tpu_custom_call" | custom-call | tf_op jit(solution)/shard_map/corners/pallas_call | solution.py:374
  13.6 11.7 %all_to_all.11 = f32[32,1,128]{2,1,0:T(1,128)S(1)} all-to-all(f32[32,1,128]{2,1,0:T(1,128)S(1)} %bitcast.5), channel_id=1, replica_groups=mesh['gx'=8,'gy'=4] {'gy','gx'}, dimensions={0} | all-to-all | bytes 32768 | tf_op jit(solution)/shard_map/all_to_all | solution.py:390
  25.3 0.8 %combine.1 = (f32[4,4,16,128]{3,2,1,0:T(8,128)}, f32[4,5]{1,0:T(4,128)}) custom-call(f32[32,128]{1,0:T(8,128)S(1)} %bitcast.4, f32[4,4,16,128]{3,2,1,0:T(8,128)S(1)} %get-tuple-element.14.field, f32[4,4,16,128]{3,2,1,0:T(8,128)S(1)} %get-tuple-element.23.image_one, f32[4,4,16,128]{3,2,1,0:T(8,128)S(1)} %get-tuple-element.24.image_two, ...), custom_call_target="tpu_custom_call" | custom-call | tf_op jit(solution)/shard_map/combine/pallas_call | solution.py:392
  (4 shorter events, 0.1 us)
Async XLA Ops:
  0.6 7.8 %collective-permute-start = (f32[4,4,16,128]{3,2,1,0:T(8,128)}, f32[4,4,16,128]{3,2,1,0:T(8,128)S(1)}, u32[]{:S(2)}, u32[]{:S(2)}) collective-permute-start(f32[4,4,16,128]{3,2,1,0:T(8,128)} %field.1), channel_id=1, source_target_pairs={{0,4},{1,5},{2,6},{3,7},{4,0},{5,1},{6,2},{7,3},{8,12},{9,13},{10,... | collective-permute-start | bytes 393224 | tf_op jit(solution)/shard_map/ppermute | solution.py:312
  4.6 3.8 %collective-permute-start.1 = (f32[4,4,2,128]{3,2,1,0:T(2,128)S(1)}, f32[4,4,2,128]{3,2,1,0:T(2,128)S(1)}, u32[]{:S(2)}, u32[]{:S(2)}) collective-permute-start(f32[4,4,2,128]{3,2,1,0:T(2,128)S(1)} %get-tuple-element.15), channel_id=1, source_target_pairs={{0,4},{1,2},{2,1},{3,7},{4,0},{5,6},{6,5},{7,3},{8,12},{9,10},{10,... | collective-permute-start | bytes 49160 | tf_op jit(solution)/shard_map/ppermute | solution.py:312
  4.7 3.7 %collective-permute-start.2 = (f32[4,4,2,128]{3,2,1,0:T(2,128)S(1)}, f32[4,4,2,128]{3,2,1,0:T(2,128)S(1)}, u32[]{:S(2)}, u32[]{:S(2)}) collective-permute-start(f32[4,4,2,128]{3,2,1,0:T(2,128)S(1)} %get-tuple-element.16), channel_id=1, source_target_pairs={{0,1},{1,0},{2,3},{3,2},{4,5},{5,4},{6,7},{7,6},{8,9},{9,8},{10,11... | collective-permute-start | bytes 49160 | tf_op jit(solution)/shard_map/ppermute | solution.py:312
  6.3 5.3 %collective-permute-start.3 = (f32[4,4,16,128]{3,2,1,0:T(8,128)}, f32[4,4,16,128]{3,2,1,0:T(8,128)S(1)}, u32[]{:S(2)}, u32[]{:S(2)}) collective-permute-start(f32[4,4,16,128]{3,2,1,0:T(8,128)} %field.1), channel_id=1, source_target_pairs={{0,1},{1,0},{2,3},{3,2},{4,8},{5,9},{6,10},{7,11},{8,4},{9,5},{10,... | collective-permute-start | bytes 393224 | tf_op jit(solution)/shard_map/ppermute | solution.py:312
  8.5 3.1 %copy-start = (f32[4,9]{1,0:T(4,128)S(1)}, f32[4,9]{1,0:T(4,128)}, u32[]{:S(2)}) copy-start(f32[4,9]{1,0:T(4,128)} %rates.3) | copy-start | bytes 436
  8.5 3.8 %collective-permute-start.4 = (f32[4,2,2,128]{3,2,1,0:T(2,128)S(1)}, f32[4,2,2,128]{3,2,1,0:T(2,128)S(1)}, u32[]{:S(2)}, u32[]{:S(2)}) collective-permute-start(f32[4,2,2,128]{3,2,1,0:T(2,128)S(1)} %get-tuple-element.27), channel_id=1, source_target_pairs={{0,1},{1,0},{2,3},{3,2},{4,8},{5,9},{6,10},{7,11},{8,4},{9,5},{10,... | collective-permute-start | bytes 24584 | tf_op jit(solution)/shard_map/ppermute | solution.py:312
  8.6 4.7 %collective-permute-start.5 = (f32[4,2,2,128]{3,2,1,0:T(2,128)S(1)}, f32[4,2,2,128]{3,2,1,0:T(2,128)S(1)}, u32[]{:S(2)}, u32[]{:S(2)}) collective-permute-start(f32[4,2,2,128]{3,2,1,0:T(2,128)S(1)} %get-tuple-element.26), channel_id=1, source_target_pairs={{0,4},{1,5},{2,6},{3,7},{4,0},{5,1},{6,2},{7,3},{8,12},{9,13},{10,... | collective-permute-start | bytes 24584 | tf_op jit(solution)/shard_map/ppermute | solution.py:312

commit v9 on v8

--- a/solution.py
+++ b/solution.py
@@ -301,7 +301,7 @@
             at = x if axis == "gx" else y
             other = at + 1 if (at - first) % 2 == 0 else at - 1
             if not 0 <= other < size:
-                return (x, y ^ 1) if axis == "gx" else (x ^ 1, y)
+                return (x, y ^ 1) if axis == "gx" else (x, other % size)
             return (other, y) if axis == "gx" else (x, other)
 
         pairs = [
@@ -341,7 +341,7 @@
     odd_y = swap("gy", size_y, 1, for_odd)
     even_y = swap("gy", size_y, 0, for_even)
 
-    even_x, odd_y, even_y = lax.optimization_barrier((even_x, odd_y, even_y))
+    even_x, even_y, odd_y = lax.optimization_barrier((even_x, even_y, odd_y))
 
     def corners(first):
         even, odd = even_y[:, first : first + HALF], odd_y[:, first : first + HALF]

time: 26.3 us -> 26.4 us (level)
  blocking collectives: 11.7 us -> 12.3 us
  waiting for transfers between devices: 3.06 us -> 2.49 us
    all_to_all x1, blocking collectives: 11.7 us -> 12.3 us  [shards(): gathered = lax.all_to_all(message, ('gy', 'gx'), 0, 0, tiled=True)]
    ppermute x6, waiting for transfers between devices: 3.06 us -> 2.49 us  [swap(): return lax.ppermute(value, ('gx', 'gy'), pairs)]
where the time goes in v9:
time: 26.4 us; the launch traced here: 26.2 us
  blocking collectives  12.3 us (47%)
  starting transfers between devices  7.88 us (30%)
  Pallas kernels  2.81 us (11%)
  waiting for transfers between devices  2.49 us (9%)
  between operations  0.7 us (3%)
    all_to_all x1, blocking collectives, shards(): gathered = lax.all_to_all(message, ('gy', 'gx'), 0, 0, tiled=True)  12.3 us
    ppermute x6, starting transfers between devices, swap(): return lax.ppermute(value, ('gx', 'gy'), pairs)  7.88 us
    ppermute x6, waiting for transfers between devices, swap(): return lax.ppermute(value, ('gx', 'gy'), pairs)  2.49 us
    pallas_call x1, Pallas kernels, shards(): pl.pallas_call(edges_kernel, out_shape=[edge, edge, block], in_specs=[pl....  0.96 us
    pallas_call x1, Pallas kernels, shards(): pl.pallas_call(combine_kernel, out_shape=[block, jax.ShapeDtypeStruct((me...  0.83 us
    pallas_call x1, Pallas kernels, shards(): pl.pallas_call(functools.partial(images_kernel, lattice), out_shape=[bloc...  0.65 us
  transfers between devices with their start and end apart: 6, of which 2 were waited for; matrix products, arithmetic and copies ran while one was open for 0% of the time, Pallas kernels for 6%

profile of v9, /device:TPU:0, one launch (start us, length us, event | category | flops | bytes accessed | tf_op | source)
XLA Modules:
  0.0 26.2 jit_solution(5758320198339077415)
XLA Ops:
  0.6 3.0 %collective-permute-start = (f32[4,4,16,128]{3,2,1,0:T(8,128)}, f32[4,4,16,128]{3,2,1,0:T(8,128)S(1)}, u32[]{:S(2)}, u32[]{:S(2)}) collective-permute-start(f32[4,4,16,128]{3,2,1,0:T(8,128)} %field.1), channel_id=1, source_target_pairs={{0,4},{1,5},{2,6},{3,7},{4,0},{5,1},{6,2},{7,3},{8,12},{9,13},{10,... | collective-permute-start | bytes 393224 | tf_op jit(solution)/shard_map/ppermute | solution.py:312
  3.6 1.0 %edges.1 = (f32[4,4,2,128]{3,2,1,0:T(2,128)S(1)}, f32[4,4,2,128]{3,2,1,0:T(2,128)S(1)}, f32[4,4,16,128]{3,2,1,0:T(8,128)S(1)}) custom-call(f32[4,4,16,128]{3,2,1,0:T(8,128)} %field.1), custom_call_target="tpu_custom_call" | custom-call | tf_op jit(solution)/shard_map/edges/pallas_call | solution.py:332
  4.6 0.1 collective-permute-start.1
  4.7 1.6 %collective-permute-start.2 = (f32[4,4,2,128]{3,2,1,0:T(2,128)S(1)}, f32[4,4,2,128]{3,2,1,0:T(2,128)S(1)}, u32[]{:S(2)}, u32[]{:S(2)}) collective-permute-start(f32[4,4,2,128]{3,2,1,0:T(2,128)S(1)} %get-tuple-element.16), channel_id=1, source_target_pairs={{0,3},{1,2},{2,1},{3,0},{4,7},{5,6},{6,5},{7,4},{8,11},{9,10},{10,... | collective-permute-start | bytes 49160 | tf_op jit(solution)/shard_map/ppermute | solution.py:312
  6.3 0.1 collective-permute-start.3
  6.4 0.0 collective-permute-done.1.even_y
  6.4 1.5 %collective-permute-done.2.odd_y = f32[4,4,2,128]{3,2,1,0:T(2,128)S(1)} collective-permute-done((f32[4,4,2,128]{3,2,1,0:T(2,128)S(1)}, f32[4,4,2,128]{3,2,1,0:T(2,128)S(1)}, u32[]{:S(2)}, u32[]{:S(2)}) %collective-permute-start.2) | collective-permute-done | bytes 16416 | tf_op jit(solution)/shard_map/ppermute | solution.py:312
  7.9 0.0 collective-permute-done.even_x
  8.0 0.0 copy-start
  8.0 0.5 %collective-permute-start.4 = (f32[4,2,2,128]{3,2,1,0:T(2,128)S(1)}, f32[4,2,2,128]{3,2,1,0:T(2,128)S(1)}, u32[]{:S(2)}, u32[]{:S(2)}) collective-permute-start(f32[4,2,2,128]{3,2,1,0:T(2,128)S(1)} %get-tuple-element.27), channel_id=1, source_target_pairs={{0,1},{1,0},{2,3},{3,2},{4,8},{5,9},{6,10},{7,11},{8,4},{9,5},{10,... | collective-permute-start | bytes 24584 | tf_op jit(solution)/shard_map/ppermute | solution.py:312
  8.5 2.6 %collective-permute-start.5 = (f32[4,2,2,128]{3,2,1,0:T(2,128)S(1)}, f32[4,2,2,128]{3,2,1,0:T(2,128)S(1)}, u32[]{:S(2)}, u32[]{:S(2)}) collective-permute-start(f32[4,2,2,128]{3,2,1,0:T(2,128)S(1)} %get-tuple-element.26), channel_id=1, source_target_pairs={{0,4},{1,5},{2,6},{3,7},{4,0},{5,1},{6,2},{7,3},{8,12},{9,13},{10,... | collective-permute-start | bytes 24584 | tf_op jit(solution)/shard_map/ppermute | solution.py:312
  11.1 0.0 collective-permute-done.3.odd_x
  11.1 0.0 copy-done
  11.1 0.7 %images.1 = (f32[4,4,16,128]{3,2,1,0:T(8,128)S(1)}, f32[4,4,16,128]{3,2,1,0:T(8,128)S(1)}, f32[4,10,8,128]{3,2,1,0:T(8,128)S(1)}, f32[48,128]{1,0:T(8,128)S(1)}) custom-call(f32[4,9]{1,0:T(4,128)S(1)} %copy-done, f32[4,4,16,128]{3,2,1,0:T(8,128)S(1)} %get-tuple-element.14.field, f32[4,4,16,128]{3,2,1,0:T(8,128)S(1)} %collective-permute-done.even_x, ...), custom_call_target="tpu_custom_call" | custom-call | tf_op jit(solution)/shard_map/images/pallas_call | solution.py:356
  11.8 0.0 collective-permute-done.4.odd_corners
  11.8 1.0 %collective-permute-done.5.even_corners = f32[4,2,2,128]{3,2,1,0:T(2,128)S(1)} collective-permute-done((f32[4,2,2,128]{3,2,1,0:T(2,128)S(1)}, f32[4,2,2,128]{3,2,1,0:T(2,128)S(1)}, u32[]{:S(2)}, u32[]{:S(2)}) %collective-permute-start.5) | collective-permute-done | bytes 8224 | tf_op jit(solution)/shard_map/ppermute | solution.py:312
  12.7 0.4 %corners.1 = (f32[4,2,4,128]{3,2,1,0:T(4,128)S(1)}, f32[32,128]{1,0:T(8,128)S(1)}) custom-call(f32[4,9]{1,0:T(4,128)S(1)} %copy-done, f32[4,10,8,128]{3,2,1,0:T(8,128)S(1)} %get-tuple-element.20.lines, f32[4,2,2,128]{3,2,1,0:T(2,128)S(1)} %collective-permute-done.4.odd_corners, f32[4,2,2,128]{3,2,1,0:T(2,128)S(1)} %collective-permute-done.5.even_corners, ...), custom_call_target="tpu_custom_call" | custom-call | tf_op jit(solution)/shard_map/corners/pallas_call | solution.py:374
  13.1 12.3 %all_to_all.11 = f32[32,1,128]{2,1,0:T(1,128)S(1)} all-to-all(f32[32,1,128]{2,1,0:T(1,128)S(1)} %bitcast.5), channel_id=1, replica_groups=mesh['gx'=8,'gy'=4] {'gy','gx'}, dimensions={0} | all-to-all | bytes 32768 | tf_op jit(solution)/shard_map/all_to_all | solution.py:390
  25.4 0.8 %combine.1 = (f32[4,4,16,128]{3,2,1,0:T(8,128)}, f32[4,5]{1,0:T(4,128)}) custom-call(f32[32,128]{1,0:T(8,128)S(1)} %bitcast.4, f32[4,4,16,128]{3,2,1,0:T(8,128)S(1)} %get-tuple-element.14.field, f32[4,4,16,128]{3,2,1,0:T(8,128)S(1)} %get-tuple-element.23.image_one, f32[4,4,16,128]{3,2,1,0:T(8,128)S(1)} %get-tuple-element.24.image_two, ...), custom_call_target="tpu_custom_call" | custom-call | tf_op jit(solution)/shard_map/combine/pallas_call | solution.py:392
  (4 shorter events, 0.1 us)
Async XLA Ops:
  0.6 7.3 %collective-permute-start = (f32[4,4,16,128]{3,2,1,0:T(8,128)}, f32[4,4,16,128]{3,2,1,0:T(8,128)S(1)}, u32[]{:S(2)}, u32[]{:S(2)}) collective-permute-start(f32[4,4,16,128]{3,2,1,0:T(8,128)} %field.1), channel_id=1, source_target_pairs={{0,4},{1,5},{2,6},{3,7},{4,0},{5,1},{6,2},{7,3},{8,12},{9,13},{10,... | collective-permute-start | bytes 393224 | tf_op jit(solution)/shard_map/ppermute | solution.py:312
  4.6 1.8 %collective-permute-start.1 = (f32[4,4,2,128]{3,2,1,0:T(2,128)S(1)}, f32[4,4,2,128]{3,2,1,0:T(2,128)S(1)}, u32[]{:S(2)}, u32[]{:S(2)}) collective-permute-start(f32[4,4,2,128]{3,2,1,0:T(2,128)S(1)} %get-tuple-element.15), channel_id=1, source_target_pairs={{0,1},{1,0},{2,3},{3,2},{4,5},{5,4},{6,7},{7,6},{8,9},{9,8},{10,11... | collective-permute-start | bytes 49160 | tf_op jit(solution)/shard_map/ppermute | solution.py:312
  4.7 3.2 %collective-permute-start.2 = (f32[4,4,2,128]{3,2,1,0:T(2,128)S(1)}, f32[4,4,2,128]{3,2,1,0:T(2,128)S(1)}, u32[]{:S(2)}, u32[]{:S(2)}) collective-permute-start(f32[4,4,2,128]{3,2,1,0:T(2,128)S(1)} %get-tuple-element.16), channel_id=1, source_target_pairs={{0,3},{1,2},{2,1},{3,0},{4,7},{5,6},{6,5},{7,4},{8,11},{9,10},{10,... | collective-permute-start | bytes 49160 | tf_op jit(solution)/shard_map/ppermute | solution.py:312
  6.3 4.8 %collective-permute-start.3 = (f32[4,4,16,128]{3,2,1,0:T(8,128)}, f32[4,4,16,128]{3,2,1,0:T(8,128)S(1)}, u32[]{:S(2)}, u32[]{:S(2)}) collective-permute-start(f32[4,4,16,128]{3,2,1,0:T(8,128)} %field.1), channel_id=1, source_target_pairs={{0,1},{1,0},{2,3},{3,2},{4,8},{5,9},{6,10},{7,11},{8,4},{9,5},{10,... | collective-permute-start | bytes 393224 | tf_op jit(solution)/shard_map/ppermute | solution.py:312
  8.0 3.1 %copy-start = (f32[4,9]{1,0:T(4,128)S(1)}, f32[4,9]{1,0:T(4,128)}, u32[]{:S(2)}) copy-start(f32[4,9]{1,0:T(4,128)} %rates.3) | copy-start | bytes 436
  8.0 3.8 %collective-permute-start.4 = (f32[4,2,2,128]{3,2,1,0:T(2,128)S(1)}, f32[4,2,2,128]{3,2,1,0:T(2,128)S(1)}, u32[]{:S(2)}, u32[]{:S(2)}) collective-permute-start(f32[4,2,2,128]{3,2,1,0:T(2,128)S(1)} %get-tuple-element.27), channel_id=1, source_target_pairs={{0,1},{1,0},{2,3},{3,2},{4,8},{5,9},{6,10},{7,11},{8,4},{9,5},{10,... | collective-permute-start | bytes 24584 | tf_op jit(solution)/shard_map/ppermute | solution.py:312
  8.5 4.2 %collective-permute-start.5 = (f32[4,2,2,128]{3,2,1,0:T(2,128)S(1)}, f32[4,2,2,128]{3,2,1,0:T(2,128)S(1)}, u32[]{:S(2)}, u32[]{:S(2)}) collective-permute-start(f32[4,2,2,128]{3,2,1,0:T(2,128)S(1)} %get-tuple-element.26), channel_id=1, source_target_pairs={{0,4},{1,5},{2,6},{3,7},{4,0},{5,1},{6,2},{7,3},{8,12},{9,13},{10,... | collective-permute-start | bytes 24584 | tf_op jit(solution)/shard_map/ppermute | solution.py:312

commit v10 on v8

--- a/solution.py
+++ b/solution.py
@@ -16,13 +16,14 @@
 GAP = 8
 
 
-def edges_kernel(field, for_odd, for_even, block, arrived):
-    copy = pltpu.make_async_copy(field, block, arrived)
-    copy.start()
-    is_even = lax.axis_index("gy") % 2 == 0
-    cols = block.shape[2]
-    copy.wait()
-    low, high = block[:, :, :2], block[:, :, cols - 2 :]
+def parity_kernel(parity):
+    parity[...] = jnp.full(parity.shape, lax.axis_index("gy") % 2, jnp.int32)
+
+
+def edges_kernel(parity, field, for_odd, for_even):
+    is_even = jnp.broadcast_to(parity[:1], for_odd.shape[1:3] + parity.shape[1:])[None] == 0
+    cols = field.shape[2]
+    low, high = field[:, :, :2], field[:, :, cols - 2 :]
     for_even[...] = jnp.where(is_even, high, low)
     for_odd[...] = jnp.where(is_even, low, high)
 
@@ -329,15 +330,22 @@
 
     edge = jax.ShapeDtypeStruct((members, rows, 2, depth), jnp.float32)
     block = jax.ShapeDtypeStruct(density.shape, jnp.float32)
-    for_odd, for_even, field = pl.pallas_call(
+    parity = pl.pallas_call(
+        parity_kernel,
+        out_shape=jax.ShapeDtypeStruct((8, depth), jnp.int32),
+        out_specs=vmem,
+        compiler_params=pltpu.CompilerParams(vmem_limit_bytes=2**20),
+        cost_estimate=pl.CostEstimate(flops=10**8, bytes_accessed=0, transcendentals=0),
+        name="parity",
+    )()
+    for_odd, for_even = pl.pallas_call(
         edges_kernel,
-        out_shape=[edge, edge, block],
-        in_specs=[pl.BlockSpec(memory_space=pl.ANY)],
-        out_specs=[vmem] * 3,
-        scratch_shapes=[pltpu.SemaphoreType.DMA],
-        compiler_params=pltpu.CompilerParams(vmem_limit_bytes=4 * 2**20),
+        out_shape=[edge, edge],
+        in_specs=[vmem, vmem],
+        out_specs=[vmem] * 2,
+        compiler_params=pltpu.CompilerParams(vmem_limit_bytes=2 * 2**20),
         name="edges",
-    )(density)
+    )(parity, density)
     odd_y = swap("gy", size_y, 1, for_odd)
     even_y = swap("gy", size_y, 0, for_even)
 
@@ -369,7 +377,7 @@
         ],
         compiler_params=pltpu.CompilerParams(vmem_limit_bytes=8 * 2**20),
         name="images",
-    )(rate_table, field, even_x, odd_x, even_y, odd_y)
+    )(rate_table, density, even_x, odd_x, even_y, odd_y)
 
     columns_two, message = pl.pallas_call(
         functools.partial(corners_kernel, lattice, cols),
@@ -396,7 +404,7 @@
         out_specs=[vmem, vmem],
         compiler_params=pltpu.CompilerParams(vmem_limit_bytes=8 * 2**20),
         name="combine",
-    )(gathered, field, image_one, image_two, columns_two)
+    )(gathered, density, image_one, image_two, columns_two)
 
 
 def solution(mesh):

time: 26.3 us -> 29 us (1.10)
  blocking collectives: 11.7 us -> 15 us
  Pallas kernels: 2.81 us -> 1.87 us
    all_to_all x1, blocking collectives: 11.7 us -> 15 us  [shards(): gathered = lax.all_to_all(message, ('gy', 'gx'), 0, 0, tiled=True)]
    pallas_call x1 -> x2, Pallas kernels: 0.96 us -> 0.02 us  [the longest x1 0.01 us: shards(): pl.pallas_call(edges_kernel, out_shape=[edge, edge], in_specs=[vmem, vmem...]
  transfers between devices with their start and end apart: 6 -> 6, of which waited for: 2 -> 2; matrix products, arithmetic and copies ran while one was open for 0% -> 0% of each run, Pallas kernels for 6% -> 2%
where the time goes in v10:
time: 29 us; the launch traced here: 28.8 us
  blocking collectives  15 us (52%)
  starting transfers between devices  8.05 us (28%)
  waiting for transfers between devices  3.12 us (11%)
  Pallas kernels  1.87 us (6%)
  between operations  0.71 us (2%)
    all_to_all x1, blocking collectives, shards(): gathered = lax.all_to_all(message, ('gy', 'gx'), 0, 0, tiled=True)  15 us
    ppermute x6, starting transfers between devices, swap(): return lax.ppermute(value, ('gx', 'gy'), pairs)  8.05 us
    ppermute x6, waiting for transfers between devices, swap(): return lax.ppermute(value, ('gx', 'gy'), pairs)  3.12 us
    pallas_call x1, Pallas kernels, shards(): pl.pallas_call(combine_kernel, out_shape=[block, jax.ShapeDtypeStruct((me...  0.83 us
    pallas_call x1, Pallas kernels, shards(): pl.pallas_call(functools.partial(images_kernel, lattice), out_shape=[bloc...  0.65 us
  transfers between devices with their start and end apart: 6, of which 2 were waited for; matrix products, arithmetic and copies ran while one was open for 0% of the time, Pallas kernels for 2%

profile of v10, /device:TPU:0, one launch (start us, length us, event | category | flops | bytes accessed | tf_op | source)
XLA Modules:
  0.0 28.8 jit_solution(13330175347991999383)
XLA Ops:
  0.6 0.0 copy-start
  0.6 3.0 %collective-permute-start = (f32[4,4,16,128]{3,2,1,0:T(8,128)}, f32[4,4,16,128]{3,2,1,0:T(8,128)S(1)}, u32[]{:S(2)}, u32[]{:S(2)}) collective-permute-start(f32[4,4,16,128]{3,2,1,0:T(8,128)} %field.5), channel_id=1, source_target_pairs={{0,4},{1,5},{2,6},{3,7},{4,0},{5,1},{6,2},{7,3},{8,12},{9,13},{10,... | collective-permute-start | bytes 393224 | tf_op jit(solution)/shard_map/ppermute | solution.py:313
  3.6 0.0 copy-done
  3.7 0.9 %collective-permute-start.1 = (f32[4,4,2,128]{3,2,1,0:T(2,128)S(1)}, f32[4,4,2,128]{3,2,1,0:T(2,128)S(1)}, u32[]{:S(2)}, u32[]{:S(2)}) collective-permute-start(f32[4,4,2,128]{3,2,1,0:T(2,128)S(1)} %get-tuple-element.13), channel_id=1, source_target_pairs={{0,4},{1,2},{2,1},{3,7},{4,0},{5,6},{6,5},{7,3},{8,12},{9,10},{10,... | collective-permute-start | bytes 49160 | tf_op jit(solution)/shard_map/ppermute | solution.py:313
  4.6 0.8 %collective-permute-start.2 = (f32[4,4,2,128]{3,2,1,0:T(2,128)S(1)}, f32[4,4,2,128]{3,2,1,0:T(2,128)S(1)}, u32[]{:S(2)}, u32[]{:S(2)}) collective-permute-start(f32[4,4,2,128]{3,2,1,0:T(2,128)S(1)} %get-tuple-element.14), channel_id=1, source_target_pairs={{0,1},{1,0},{2,3},{3,2},{4,5},{5,4},{6,7},{7,6},{8,9},{9,8},{10,11... | collective-permute-start | bytes 49160 | tf_op jit(solution)/shard_map/ppermute | solution.py:313
  5.4 0.0 collective-permute-start.3
  5.4 2.2 %collective-permute-done.1.odd_y = f32[4,4,2,128]{3,2,1,0:T(2,128)S(1)} collective-permute-done((f32[4,4,2,128]{3,2,1,0:T(2,128)S(1)}, f32[4,4,2,128]{3,2,1,0:T(2,128)S(1)}, u32[]{:S(2)}, u32[]{:S(2)}) %collective-permute-start.1) | collective-permute-done | bytes 16416 | tf_op jit(solution)/shard_map/ppermute | solution.py:313
  7.5 0.0 collective-permute-done.2.even_y
  7.5 0.0 collective-permute-done.even_x
  7.6 0.0 copy-start.1
  7.6 0.1 collective-permute-start.4
  7.7 3.3 %collective-permute-start.5 = (f32[4,2,2,128]{3,2,1,0:T(2,128)S(1)}, f32[4,2,2,128]{3,2,1,0:T(2,128)S(1)}, u32[]{:S(2)}, u32[]{:S(2)}) collective-permute-start(f32[4,2,2,128]{3,2,1,0:T(2,128)S(1)} %get-tuple-element.24), channel_id=1, source_target_pairs={{0,4},{1,5},{2,6},{3,7},{4,0},{5,1},{6,2},{7,3},{8,12},{9,13},{10,... | collective-permute-start | bytes 24584 | tf_op jit(solution)/shard_map/ppermute | solution.py:313
  11.0 0.0 collective-permute-done.3.odd_x
  11.0 0.0 copy-done.1
  11.0 0.7 %images.1 = (f32[4,4,16,128]{3,2,1,0:T(8,128)S(1)}, f32[4,4,16,128]{3,2,1,0:T(8,128)S(1)}, f32[4,10,8,128]{3,2,1,0:T(8,128)S(1)}, f32[48,128]{1,0:T(8,128)S(1)}) custom-call(f32[4,9]{1,0:T(4,128)S(1)} %copy-done.1, f32[4,4,16,128]{3,2,1,0:T(8,128)S(1)} %copy-done, f32[4,4,16,128]{3,2,1,0:T(8,128)S(1)} %collective-permute-done.even_x, ...), custom_call_target="tpu_custom_call" | custom-call | tf_op jit(solution)/shard_map/images/pallas_call | solution.py:364
  11.6 0.0 collective-permute-done.4.odd_corners
  11.7 1.0 %collective-permute-done.5.even_corners = f32[4,2,2,128]{3,2,1,0:T(2,128)S(1)} collective-permute-done((f32[4,2,2,128]{3,2,1,0:T(2,128)S(1)}, f32[4,2,2,128]{3,2,1,0:T(2,128)S(1)}, u32[]{:S(2)}, u32[]{:S(2)}) %collective-permute-start.5) | collective-permute-done | bytes 8224 | tf_op jit(solution)/shard_map/ppermute | solution.py:313
  12.6 0.4 %corners.1 = (f32[4,2,4,128]{3,2,1,0:T(4,128)S(1)}, f32[32,128]{1,0:T(8,128)S(1)}) custom-call(f32[4,9]{1,0:T(4,128)S(1)} %copy-done.1, f32[4,10,8,128]{3,2,1,0:T(8,128)S(1)} %get-tuple-element.18.lines, f32[4,2,2,128]{3,2,1,0:T(2,128)S(1)} %collective-permute-done.4.odd_corners, f32[4,2,2,128]{3,2,1,0:T(2,128)S(1)} %collective-permute-done.5.even_corners, ...), custom_call_target="tpu_custom_call" | custom-call | tf_op jit(solution)/shard_map/corners/pallas_call | solution.py:382
  13.0 15.0 %all_to_all.11 = f32[32,1,128]{2,1,0:T(1,128)S(1)} all-to-all(f32[32,1,128]{2,1,0:T(1,128)S(1)} %bitcast.5), channel_id=1, replica_groups=mesh['gx'=8,'gy'=4] {'gy','gx'}, dimensions={0} | all-to-all | bytes 32768 | tf_op jit(solution)/shard_map/all_to_all | solution.py:398
  28.0 0.8 %combine.1 = (f32[4,4,16,128]{3,2,1,0:T(8,128)}, f32[4,5]{1,0:T(4,128)}) custom-call(f32[32,128]{1,0:T(8,128)S(1)} %bitcast.4, f32[4,4,16,128]{3,2,1,0:T(8,128)S(1)} %copy-done, f32[4,4,16,128]{3,2,1,0:T(8,128)S(1)} %get-tuple-element.21.image_one, f32[4,4,16,128]{3,2,1,0:T(8,128)S(1)} %get-tuple-element.22.image_two, ...), custom_call_target="tpu_custom_call" | custom-call | tf_op jit(solution)/shard_map/combine/pallas_call | solution.py:400
  (6 shorter events, 0.1 us)
Async XLA Ops:
  0.6 3.0 %copy-start = (f32[4,4,16,128]{3,2,1,0:T(8,128)S(1)}, f32[4,4,16,128]{3,2,1,0:T(8,128)}, u32[]{:S(2)}) copy-start(f32[4,4,16,128]{3,2,1,0:T(8,128)} %field.5) | copy-start | bytes 393220
  0.6 6.9 %collective-permute-start = (f32[4,4,16,128]{3,2,1,0:T(8,128)}, f32[4,4,16,128]{3,2,1,0:T(8,128)S(1)}, u32[]{:S(2)}, u32[]{:S(2)}) collective-permute-start(f32[4,4,16,128]{3,2,1,0:T(8,128)} %field.5), channel_id=1, source_target_pairs={{0,4},{1,5},{2,6},{3,7},{4,0},{5,1},{6,2},{7,3},{8,12},{9,13},{10,... | collective-permute-start | bytes 393224 | tf_op jit(solution)/shard_map/ppermute | solution.py:313
  3.7 3.9 %collective-permute-start.1 = (f32[4,4,2,128]{3,2,1,0:T(2,128)S(1)}, f32[4,4,2,128]{3,2,1,0:T(2,128)S(1)}, u32[]{:S(2)}, u32[]{:S(2)}) collective-permute-start(f32[4,4,2,128]{3,2,1,0:T(2,128)S(1)} %get-tuple-element.13), channel_id=1, source_target_pairs={{0,4},{1,2},{2,1},{3,7},{4,0},{5,6},{6,5},{7,3},{8,12},{9,10},{10,... | collective-permute-start | bytes 49160 | tf_op jit(solution)/shard_map/ppermute | solution.py:313
  4.6 3.0 %collective-permute-start.2 = (f32[4,4,2,128]{3,2,1,0:T(2,128)S(1)}, f32[4,4,2,128]{3,2,1,0:T(2,128)S(1)}, u32[]{:S(2)}, u32[]{:S(2)}) collective-permute-start(f32[4,4,2,128]{3,2,1,0:T(2,128)S(1)} %get-tuple-element.14), channel_id=1, source_target_pairs={{0,1},{1,0},{2,3},{3,2},{4,5},{5,4},{6,7},{7,6},{8,9},{9,8},{10,11... | collective-permute-start | bytes 49160 | tf_op jit(solution)/shard_map/ppermute | solution.py:313
  5.4 5.6 %collective-permute-start.3 = (f32[4,4,16,128]{3,2,1,0:T(8,128)S(1)}, f32[4,4,16,128]{3,2,1,0:T(8,128)S(1)}, u32[]{:S(2)}, u32[]{:S(2)}) collective-permute-start(f32[4,4,16,128]{3,2,1,0:T(8,128)S(1)} %copy-done), channel_id=1, source_target_pairs={{0,1},{1,0},{2,3},{3,2},{4,8},{5,9},{6,10},{7,11},{8,4},{9,5},{10,... | collective-permute-start | bytes 393224 | tf_op jit(solution)/shard_map/ppermute | solution.py:313
  7.6 3.4 %copy-start.1 = (f32[4,9]{1,0:T(4,128)S(1)}, f32[4,9]{1,0:T(4,128)}, u32[]{:S(2)}) copy-start(f32[4,9]{1,0:T(4,128)} %rates.3) | copy-start | bytes 436
  7.6 4.0 %collective-permute-start.4 = (f32[4,2,2,128]{3,2,1,0:T(2,128)S(1)}, f32[4,2,2,128]{3,2,1,0:T(2,128)S(1)}, u32[]{:S(2)}, u32[]{:S(2)}) collective-permute-start(f32[4,2,2,128]{3,2,1,0:T(2,128)S(1)} %get-tuple-element.25), channel_id=1, source_target_pairs={{0,1},{1,0},{2,3},{3,2},{4,8},{5,9},{6,10},{7,11},{8,4},{9,5},{10,... | collective-permute-start | bytes 24584 | tf_op jit(solution)/shard_map/ppermute | solution.py:313
  7.7 4.9 %collective-permute-start.5 = (f32[4,2,2,128]{3,2,1,0:T(2,128)S(1)}, f32[4,2,2,128]{3,2,1,0:T(2,128)S(1)}, u32[]{:S(2)}, u32[]{:S(2)}) collective-permute-start(f32[4,2,2,128]{3,2,1,0:T(2,128)S(1)} %get-tuple-element.24), channel_id=1, source_target_pairs={{0,4},{1,5},{2,6},{3,7},{4,0},{5,1},{6,2},{7,3},{8,12},{9,13},{10,... | collective-permute-start | bytes 24584 | tf_op jit(solution)/shard_map/ppermute | solution.py:313

commit v11 on v10

--- a/solution.py
+++ b/solution.py
@@ -323,10 +323,9 @@
             swap(axis, size, 1, jnp.where(is_even, initial, last)),
         )
 
-    if rows == REACH:
-        even_x, odd_x = swaps("gx", size_x, parity_x, density, density)
-    else:
-        even_x, odd_x = swaps("gx", size_x, parity_x, density[:, :REACH], density[:, rows - REACH :])
+    initial, last = (density, density) if rows == REACH else (density[:, :REACH], density[:, rows - REACH :])
+    is_even = parity_x == 0
+    even_x = swap("gx", size_x, 0, initial if rows == REACH else jnp.where(is_even, last, initial))
 
     edge = jax.ShapeDtypeStruct((members, rows, 2, depth), jnp.float32)
     block = jax.ShapeDtypeStruct(density.shape, jnp.float32)
@@ -349,6 +348,8 @@
     odd_y = swap("gy", size_y, 1, for_odd)
     even_y = swap("gy", size_y, 0, for_even)
 
+    even_y, for_odd_x = lax.optimization_barrier((even_y, initial if rows == REACH else jnp.where(is_even, initial, last)))
+    odd_x = swap("gx", size_x, 1, for_odd_x)
     even_x, odd_y, even_y = lax.optimization_barrier((even_x, odd_y, even_y))
 
     def corners(first):

time: 29 us -> 26.2 us (0.903)
  blocking collectives: 15 us -> 12.3 us
    all_to_all x1, blocking collectives: 15 us -> 12.3 us  [shards(): gathered = lax.all_to_all(message, ('gy', 'gx'), 0, 0, tiled=True)]
  transfers between devices with their start and end apart: 6 -> 6, of which waited for: 2 -> 3; matrix products, arithmetic and copies ran while one was open for 0% -> 0% of each run, Pallas kernels for 2% -> 3%
where the time goes in v11:
time: 26.2 us; the launch traced here: 26.1 us
  blocking collectives  12.3 us (47%)
  starting transfers between devices  7.83 us (30%)
  waiting for transfers between devices  3.34 us (13%)
  Pallas kernels  1.88 us (7%)
  between operations  0.71 us (3%)
    all_to_all x1, blocking collectives, shards(): gathered = lax.all_to_all(message, ('gy', 'gx'), 0, 0, tiled=True)  12.3 us
    ppermute x6, starting transfers between devices, swap(): return lax.ppermute(value, ('gx', 'gy'), pairs)  7.83 us
    ppermute x6, waiting for transfers between devices, swap(): return lax.ppermute(value, ('gx', 'gy'), pairs)  3.34 us
    pallas_call x1, Pallas kernels, shards(): pl.pallas_call(combine_kernel, out_shape=[block, jax.ShapeDtypeStruct((me...  0.83 us
    pallas_call x1, Pallas kernels, shards(): pl.pallas_call(functools.partial(images_kernel, lattice), out_shape=[bloc...  0.65 us
  transfers between devices with their start and end apart: 6, of which 3 were waited for; matrix products, arithmetic and copies ran while one was open for 0% of the time, Pallas kernels for 3%

profile of v11, /device:TPU:0, one launch (start us, length us, event | category | flops | bytes accessed | tf_op | source)
XLA Modules:
  0.0 26.1 jit_solution(12220030960334339410)
XLA Ops:
  0.6 0.0 copy-start
  0.6 3.0 %collective-permute-start = (f32[4,4,16,128]{3,2,1,0:T(8,128)}, f32[4,4,16,128]{3,2,1,0:T(8,128)S(1)}, u32[]{:S(2)}, u32[]{:S(2)}) collective-permute-start(f32[4,4,16,128]{3,2,1,0:T(8,128)} %field.5), channel_id=1, source_target_pairs={{0,4},{1,5},{2,6},{3,7},{4,0},{5,1},{6,2},{7,3},{8,12},{9,13},{10,... | collective-permute-start | bytes 393224 | tf_op jit(solution)/shard_map/ppermute | solution.py:313
  3.6 0.0 copy-done
  3.7 0.1 collective-permute-start.2
  3.7 0.9 %collective-permute-start.1 = (f32[4,4,2,128]{3,2,1,0:T(2,128)S(1)}, f32[4,4,2,128]{3,2,1,0:T(2,128)S(1)}, u32[]{:S(2)}, u32[]{:S(2)}) collective-permute-start(f32[4,4,2,128]{3,2,1,0:T(2,128)S(1)} %get-tuple-element.15), channel_id=1, source_target_pairs={{0,4},{1,2},{2,1},{3,7},{4,0},{5,6},{6,5},{7,3},{8,12},{9,10},{10,... | collective-permute-start | bytes 49160 | tf_op jit(solution)/shard_map/ppermute | solution.py:313
  4.6 0.3 %collective-permute-done.2.even_y = f32[4,4,2,128]{3,2,1,0:T(2,128)S(1)} collective-permute-done((f32[4,4,2,128]{3,2,1,0:T(2,128)S(1)}, f32[4,4,2,128]{3,2,1,0:T(2,128)S(1)}, u32[]{:S(2)}, u32[]{:S(2)}) %collective-permute-start.2) | collective-permute-done | bytes 16416 | tf_op jit(solution)/shard_map/ppermute | solution.py:313
  4.9 0.5 %collective-permute-start.3 = (f32[4,4,16,128]{3,2,1,0:T(8,128)S(1)}, f32[4,4,16,128]{3,2,1,0:T(8,128)S(1)}, u32[]{:S(2)}, u32[]{:S(2)}) collective-permute-start(f32[4,4,16,128]{3,2,1,0:T(8,128)S(1)} %copy-done), channel_id=1, source_target_pairs={{0,1},{1,0},{2,3},{3,2},{4,8},{5,9},{6,10},{7,11},{8,4},{9,5},{10,... | collective-permute-start | bytes 393224 | tf_op jit(solution)/shard_map/ppermute | solution.py:313
  5.4 2.1 %collective-permute-done.1.odd_y = f32[4,4,2,128]{3,2,1,0:T(2,128)S(1)} collective-permute-done((f32[4,4,2,128]{3,2,1,0:T(2,128)S(1)}, f32[4,4,2,128]{3,2,1,0:T(2,128)S(1)}, u32[]{:S(2)}, u32[]{:S(2)}) %collective-permute-start.1) | collective-permute-done | bytes 16416 | tf_op jit(solution)/shard_map/ppermute | solution.py:313
  7.5 0.0 collective-permute-done.even_x
  7.6 0.0 copy-start.1
  7.6 0.2 collective-permute-start.4
  7.8 3.2 %collective-permute-start.5 = (f32[4,2,2,128]{3,2,1,0:T(2,128)S(1)}, f32[4,2,2,128]{3,2,1,0:T(2,128)S(1)}, u32[]{:S(2)}, u32[]{:S(2)}) collective-permute-start(f32[4,2,2,128]{3,2,1,0:T(2,128)S(1)} %get-tuple-element.28), channel_id=1, source_target_pairs={{0,4},{1,5},{2,6},{3,7},{4,0},{5,1},{6,2},{7,3},{8,12},{9,13},{10,... | collective-permute-start | bytes 24584 | tf_op jit(solution)/shard_map/ppermute | solution.py:313
  11.0 0.0 collective-permute-done.3.odd_x
  11.0 0.0 copy-done.1
  11.0 0.7 %images.1 = (f32[4,4,16,128]{3,2,1,0:T(8,128)S(1)}, f32[4,4,16,128]{3,2,1,0:T(8,128)S(1)}, f32[4,10,8,128]{3,2,1,0:T(8,128)S(1)}, f32[48,128]{1,0:T(8,128)S(1)}) custom-call(f32[4,9]{1,0:T(4,128)S(1)} %copy-done.1, f32[4,4,16,128]{3,2,1,0:T(8,128)S(1)} %copy-done, f32[4,4,16,128]{3,2,1,0:T(8,128)S(1)} %collective-permute-done.even_x, ...), custom_call_target="tpu_custom_call" | custom-call | tf_op jit(solution)/shard_map/images/pallas_call | solution.py:365
  11.6 0.0 collective-permute-done.4.odd_corners
  11.7 0.9 %collective-permute-done.5.even_corners = f32[4,2,2,128]{3,2,1,0:T(2,128)S(1)} collective-permute-done((f32[4,2,2,128]{3,2,1,0:T(2,128)S(1)}, f32[4,2,2,128]{3,2,1,0:T(2,128)S(1)}, u32[]{:S(2)}, u32[]{:S(2)}) %collective-permute-start.5) | collective-permute-done | bytes 8224 | tf_op jit(solution)/shard_map/ppermute | solution.py:313
  12.6 0.4 %corners.1 = (f32[4,2,4,128]{3,2,1,0:T(4,128)S(1)}, f32[32,128]{1,0:T(8,128)S(1)}) custom-call(f32[4,9]{1,0:T(4,128)S(1)} %copy-done.1, f32[4,10,8,128]{3,2,1,0:T(8,128)S(1)} %get-tuple-element.22.lines, f32[4,2,2,128]{3,2,1,0:T(2,128)S(1)} %collective-permute-done.4.odd_corners, f32[4,2,2,128]{3,2,1,0:T(2,128)S(1)} %collective-permute-done.5.even_corners, ...), custom_call_target="tpu_custom_call" | custom-call | tf_op jit(solution)/shard_map/corners/pallas_call | solution.py:383
  13.0 12.3 %all_to_all.11 = f32[32,1,128]{2,1,0:T(1,128)S(1)} all-to-all(f32[32,1,128]{2,1,0:T(1,128)S(1)} %bitcast.5), channel_id=1, replica_groups=mesh['gx'=8,'gy'=4] {'gy','gx'}, dimensions={0} | all-to-all | bytes 32768 | tf_op jit(solution)/shard_map/all_to_all | solution.py:399
  25.3 0.8 %combine.1 = (f32[4,4,16,128]{3,2,1,0:T(8,128)}, f32[4,5]{1,0:T(4,128)}) custom-call(f32[32,128]{1,0:T(8,128)S(1)} %bitcast.4, f32[4,4,16,128]{3,2,1,0:T(8,128)S(1)} %copy-done, f32[4,4,16,128]{3,2,1,0:T(8,128)S(1)} %get-tuple-element.25.image_one, f32[4,4,16,128]{3,2,1,0:T(8,128)S(1)} %get-tuple-element.26.image_two, ...), custom_call_target="tpu_custom_call" | custom-call | tf_op jit(solution)/shard_map/combine/pallas_call | solution.py:401
  (6 shorter events, 0.1 us)
Async XLA Ops:
  0.6 3.0 %copy-start = (f32[4,4,16,128]{3,2,1,0:T(8,128)S(1)}, f32[4,4,16,128]{3,2,1,0:T(8,128)}, u32[]{:S(2)}) copy-start(f32[4,4,16,128]{3,2,1,0:T(8,128)} %field.5) | copy-start | bytes 393220
  0.6 6.9 %collective-permute-start = (f32[4,4,16,128]{3,2,1,0:T(8,128)}, f32[4,4,16,128]{3,2,1,0:T(8,128)S(1)}, u32[]{:S(2)}, u32[]{:S(2)}) collective-permute-start(f32[4,4,16,128]{3,2,1,0:T(8,128)} %field.5), channel_id=1, source_target_pairs={{0,4},{1,5},{2,6},{3,7},{4,0},{5,1},{6,2},{7,3},{8,12},{9,13},{10,... | collective-permute-start | bytes 393224 | tf_op jit(solution)/shard_map/ppermute | solution.py:313
  3.7 1.2 %collective-permute-start.2 = (f32[4,4,2,128]{3,2,1,0:T(2,128)S(1)}, f32[4,4,2,128]{3,2,1,0:T(2,128)S(1)}, u32[]{:S(2)}, u32[]{:S(2)}) collective-permute-start(f32[4,4,2,128]{3,2,1,0:T(2,128)S(1)} %get-tuple-element.16), channel_id=1, source_target_pairs={{0,1},{1,0},{2,3},{3,2},{4,5},{5,4},{6,7},{7,6},{8,9},{9,8},{10,11... | collective-permute-start | bytes 49160 | tf_op jit(solution)/shard_map/ppermute | solution.py:313
  3.7 3.8 %collective-permute-start.1 = (f32[4,4,2,128]{3,2,1,0:T(2,128)S(1)}, f32[4,4,2,128]{3,2,1,0:T(2,128)S(1)}, u32[]{:S(2)}, u32[]{:S(2)}) collective-permute-start(f32[4,4,2,128]{3,2,1,0:T(2,128)S(1)} %get-tuple-element.15), channel_id=1, source_target_pairs={{0,4},{1,2},{2,1},{3,7},{4,0},{5,6},{6,5},{7,3},{8,12},{9,10},{10,... | collective-permute-start | bytes 49160 | tf_op jit(solution)/shard_map/ppermute | solution.py:313
  4.9 6.1 %collective-permute-start.3 = (f32[4,4,16,128]{3,2,1,0:T(8,128)S(1)}, f32[4,4,16,128]{3,2,1,0:T(8,128)S(1)}, u32[]{:S(2)}, u32[]{:S(2)}) collective-permute-start(f32[4,4,16,128]{3,2,1,0:T(8,128)S(1)} %copy-done), channel_id=1, source_target_pairs={{0,1},{1,0},{2,3},{3,2},{4,8},{5,9},{6,10},{7,11},{8,4},{9,5},{10,... | collective-permute-start | bytes 393224 | tf_op jit(solution)/shard_map/ppermute | solution.py:313
  7.6 3.4 %copy-start.1 = (f32[4,9]{1,0:T(4,128)S(1)}, f32[4,9]{1,0:T(4,128)}, u32[]{:S(2)}) copy-start(f32[4,9]{1,0:T(4,128)} %rates.3) | copy-start | bytes 436
  7.6 4.0 %collective-permute-start.4 = (f32[4,2,2,128]{3,2,1,0:T(2,128)S(1)}, f32[4,2,2,128]{3,2,1,0:T(2,128)S(1)}, u32[]{:S(2)}, u32[]{:S(2)}) collective-permute-start(f32[4,2,2,128]{3,2,1,0:T(2,128)S(1)} %get-tuple-element.29), channel_id=1, source_target_pairs={{0,1},{1,0},{2,3},{3,2},{4,8},{5,9},{6,10},{7,11},{8,4},{9,5},{10,... | collective-permute-start | bytes 24584 | tf_op jit(solution)/shard_map/ppermute | solution.py:313
  7.8 4.8 %collective-permute-start.5 = (f32[4,2,2,128]{3,2,1,0:T(2,128)S(1)}, f32[4,2,2,128]{3,2,1,0:T(2,128)S(1)}, u32[]{:S(2)}, u32[]{:S(2)}) collective-permute-start(f32[4,2,2,128]{3,2,1,0:T(2,128)S(1)} %get-tuple-element.28), channel_id=1, source_target_pairs={{0,4},{1,5},{2,6},{3,7},{4,0},{5,1},{6,2},{7,3},{8,12},{9,13},{10,... | collective-permute-start | bytes 24584 | tf_op jit(solution)/shard_map/ppermute | solution.py:313

commit v12 on v11

--- a/solution.py
+++ b/solution.py
@@ -396,7 +396,8 @@
         name="corners",
     )(rate_table, lines, odd_corners, even_corners, parts)
 
-    gathered = lax.all_to_all(message, ("gy", "gx"), 0, 0, tiled=True)
+    order = [0] + [i for i in range(devices - 1, 0, -1)]
+    gathered = lax.all_to_all(message, ("gx", "gy"), 0, 0, axis_index_groups=[order], tiled=True)
 
     return pl.pallas_call(
         combine_kernel,

time: 26.2 us -> 26.2 us (level)
  no operation moved by 1% of the time
where the time goes in v12:
time: 26.2 us; the launch traced here: 26.1 us
  blocking collectives  12.3 us (47%)
  starting transfers between devices  7.83 us (30%)
  waiting for transfers between devices  3.34 us (13%)
  Pallas kernels  1.88 us (7%)
  between operations  0.71 us (3%)
    all_to_all x1, blocking collectives, shards(): lax.all_to_all(message, ('gx', 'gy'), 0, 0, axis_index_groups=[order], ti...  12.3 us
    ppermute x6, starting transfers between devices, swap(): return lax.ppermute(value, ('gx', 'gy'), pairs)  7.83 us
    ppermute x6, waiting for transfers between devices, swap(): return lax.ppermute(value, ('gx', 'gy'), pairs)  3.34 us
    pallas_call x1, Pallas kernels, shards(): pl.pallas_call(combine_kernel, out_shape=[block, jax.ShapeDtypeStruct((me...  0.83 us
    pallas_call x1, Pallas kernels, shards(): pl.pallas_call(functools.partial(images_kernel, lattice), out_shape=[bloc...  0.65 us
  transfers between devices with their start and end apart: 6, of which 3 were waited for; matrix products, arithmetic and copies ran while one was open for 0% of the time, Pallas kernels for 3%

profile of v12, /device:TPU:0, one launch (start us, length us, event | category | flops | bytes accessed | tf_op | source)
XLA Modules:
  0.0 26.1 jit_solution(7268820473846387493)
XLA Ops:
  0.6 0.0 copy-start
  0.6 3.0 %collective-permute-start = (f32[4,4,16,128]{3,2,1,0:T(8,128)}, f32[4,4,16,128]{3,2,1,0:T(8,128)S(1)}, u32[]{:S(2)}, u32[]{:S(2)}) collective-permute-start(f32[4,4,16,128]{3,2,1,0:T(8,128)} %field.5), channel_id=1, source_target_pairs={{0,4},{1,5},{2,6},{3,7},{4,0},{5,1},{6,2},{7,3},{8,12},{9,13},{10,... | collective-permute-start | bytes 393224 | tf_op jit(solution)/shard_map/ppermute | solution.py:313
  3.6 0.0 copy-done
  3.7 0.1 collective-permute-start.2
  3.7 0.9 %collective-permute-start.1 = (f32[4,4,2,128]{3,2,1,0:T(2,128)S(1)}, f32[4,4,2,128]{3,2,1,0:T(2,128)S(1)}, u32[]{:S(2)}, u32[]{:S(2)}) collective-permute-start(f32[4,4,2,128]{3,2,1,0:T(2,128)S(1)} %get-tuple-element.15), channel_id=1, source_target_pairs={{0,4},{1,2},{2,1},{3,7},{4,0},{5,6},{6,5},{7,3},{8,12},{9,10},{10,... | collective-permute-start | bytes 49160 | tf_op jit(solution)/shard_map/ppermute | solution.py:313
  4.6 0.3 %collective-permute-done.2.even_y = f32[4,4,2,128]{3,2,1,0:T(2,128)S(1)} collective-permute-done((f32[4,4,2,128]{3,2,1,0:T(2,128)S(1)}, f32[4,4,2,128]{3,2,1,0:T(2,128)S(1)}, u32[]{:S(2)}, u32[]{:S(2)}) %collective-permute-start.2) | collective-permute-done | bytes 16416 | tf_op jit(solution)/shard_map/ppermute | solution.py:313
  4.9 0.5 %collective-permute-start.3 = (f32[4,4,16,128]{3,2,1,0:T(8,128)S(1)}, f32[4,4,16,128]{3,2,1,0:T(8,128)S(1)}, u32[]{:S(2)}, u32[]{:S(2)}) collective-permute-start(f32[4,4,16,128]{3,2,1,0:T(8,128)S(1)} %copy-done), channel_id=1, source_target_pairs={{0,1},{1,0},{2,3},{3,2},{4,8},{5,9},{6,10},{7,11},{8,4},{9,5},{10,... | collective-permute-start | bytes 393224 | tf_op jit(solution)/shard_map/ppermute | solution.py:313
  5.4 2.1 %collective-permute-done.1.odd_y = f32[4,4,2,128]{3,2,1,0:T(2,128)S(1)} collective-permute-done((f32[4,4,2,128]{3,2,1,0:T(2,128)S(1)}, f32[4,4,2,128]{3,2,1,0:T(2,128)S(1)}, u32[]{:S(2)}, u32[]{:S(2)}) %collective-permute-start.1) | collective-permute-done | bytes 16416 | tf_op jit(solution)/shard_map/ppermute | solution.py:313
  7.5 0.0 collective-permute-done.even_x
  7.6 0.0 copy-start.1
  7.6 0.2 collective-permute-start.4
  7.8 3.2 %collective-permute-start.5 = (f32[4,2,2,128]{3,2,1,0:T(2,128)S(1)}, f32[4,2,2,128]{3,2,1,0:T(2,128)S(1)}, u32[]{:S(2)}, u32[]{:S(2)}) collective-permute-start(f32[4,2,2,128]{3,2,1,0:T(2,128)S(1)} %get-tuple-element.28), channel_id=1, source_target_pairs={{0,4},{1,5},{2,6},{3,7},{4,0},{5,1},{6,2},{7,3},{8,12},{9,13},{10,... | collective-permute-start | bytes 24584 | tf_op jit(solution)/shard_map/ppermute | solution.py:313
  11.0 0.0 collective-permute-done.3.odd_x
  11.0 0.0 copy-done.1
  11.0 0.7 %images.1 = (f32[4,4,16,128]{3,2,1,0:T(8,128)S(1)}, f32[4,4,16,128]{3,2,1,0:T(8,128)S(1)}, f32[4,10,8,128]{3,2,1,0:T(8,128)S(1)}, f32[48,128]{1,0:T(8,128)S(1)}) custom-call(f32[4,9]{1,0:T(4,128)S(1)} %copy-done.1, f32[4,4,16,128]{3,2,1,0:T(8,128)S(1)} %copy-done, f32[4,4,16,128]{3,2,1,0:T(8,128)S(1)} %collective-permute-done.even_x, ...), custom_call_target="tpu_custom_call" | custom-call | tf_op jit(solution)/shard_map/images/pallas_call | solution.py:365
  11.6 0.0 collective-permute-done.4.odd_corners
  11.7 0.9 %collective-permute-done.5.even_corners = f32[4,2,2,128]{3,2,1,0:T(2,128)S(1)} collective-permute-done((f32[4,2,2,128]{3,2,1,0:T(2,128)S(1)}, f32[4,2,2,128]{3,2,1,0:T(2,128)S(1)}, u32[]{:S(2)}, u32[]{:S(2)}) %collective-permute-start.5) | collective-permute-done | bytes 8224 | tf_op jit(solution)/shard_map/ppermute | solution.py:313
  12.6 0.4 %corners.1 = (f32[4,2,4,128]{3,2,1,0:T(4,128)S(1)}, f32[32,128]{1,0:T(8,128)S(1)}) custom-call(f32[4,9]{1,0:T(4,128)S(1)} %copy-done.1, f32[4,10,8,128]{3,2,1,0:T(8,128)S(1)} %get-tuple-element.22.lines, f32[4,2,2,128]{3,2,1,0:T(2,128)S(1)} %collective-permute-done.4.odd_corners, f32[4,2,2,128]{3,2,1,0:T(2,128)S(1)} %collective-permute-done.5.even_corners, ...), custom_call_target="tpu_custom_call" | custom-call | tf_op jit(solution)/shard_map/corners/pallas_call | solution.py:383
  13.0 12.3 %all_to_all.11 = f32[32,1,128]{2,1,0:T(1,128)S(1)} all-to-all(f32[32,1,128]{2,1,0:T(1,128)S(1)} %bitcast.5), channel_id=1, replica_groups={{0,31,30,29,28,27,26,25,24,23,22,21,20,19,18,17,16,15,14,13,12,11,10,9,..., dimensions={0} | all-to-all | bytes 32768 | tf_op jit(solution)/shard_map/all_to_all | solution.py:400
  25.3 0.8 %combine.1 = (f32[4,4,16,128]{3,2,1,0:T(8,128)}, f32[4,5]{1,0:T(4,128)}) custom-call(f32[32,128]{1,0:T(8,128)S(1)} %bitcast.4, f32[4,4,16,128]{3,2,1,0:T(8,128)S(1)} %copy-done, f32[4,4,16,128]{3,2,1,0:T(8,128)S(1)} %get-tuple-element.25.image_one, f32[4,4,16,128]{3,2,1,0:T(8,128)S(1)} %get-tuple-element.26.image_two, ...), custom_call_target="tpu_custom_call" | custom-call | tf_op jit(solution)/shard_map/combine/pallas_call | solution.py:402
  (6 shorter events, 0.1 us)
Async XLA Ops:
  0.6 3.0 %copy-start = (f32[4,4,16,128]{3,2,1,0:T(8,128)S(1)}, f32[4,4,16,128]{3,2,1,0:T(8,128)}, u32[]{:S(2)}) copy-start(f32[4,4,16,128]{3,2,1,0:T(8,128)} %field.5) | copy-start | bytes 393220
  0.6 6.9 %collective-permute-start = (f32[4,4,16,128]{3,2,1,0:T(8,128)}, f32[4,4,16,128]{3,2,1,0:T(8,128)S(1)}, u32[]{:S(2)}, u32[]{:S(2)}) collective-permute-start(f32[4,4,16,128]{3,2,1,0:T(8,128)} %field.5), channel_id=1, source_target_pairs={{0,4},{1,5},{2,6},{3,7},{4,0},{5,1},{6,2},{7,3},{8,12},{9,13},{10,... | collective-permute-start | bytes 393224 | tf_op jit(solution)/shard_map/ppermute | solution.py:313
  3.7 1.2 %collective-permute-start.2 = (f32[4,4,2,128]{3,2,1,0:T(2,128)S(1)}, f32[4,4,2,128]{3,2,1,0:T(2,128)S(1)}, u32[]{:S(2)}, u32[]{:S(2)}) collective-permute-start(f32[4,4,2,128]{3,2,1,0:T(2,128)S(1)} %get-tuple-element.16), channel_id=1, source_target_pairs={{0,1},{1,0},{2,3},{3,2},{4,5},{5,4},{6,7},{7,6},{8,9},{9,8},{10,11... | collective-permute-start | bytes 49160 | tf_op jit(solution)/shard_map/ppermute | solution.py:313
  3.7 3.8 %collective-permute-start.1 = (f32[4,4,2,128]{3,2,1,0:T(2,128)S(1)}, f32[4,4,2,128]{3,2,1,0:T(2,128)S(1)}, u32[]{:S(2)}, u32[]{:S(2)}) collective-permute-start(f32[4,4,2,128]{3,2,1,0:T(2,128)S(1)} %get-tuple-element.15), channel_id=1, source_target_pairs={{0,4},{1,2},{2,1},{3,7},{4,0},{5,6},{6,5},{7,3},{8,12},{9,10},{10,... | collective-permute-start | bytes 49160 | tf_op jit(solution)/shard_map/ppermute | solution.py:313
  4.9 6.1 %collective-permute-start.3 = (f32[4,4,16,128]{3,2,1,0:T(8,128)S(1)}, f32[4,4,16,128]{3,2,1,0:T(8,128)S(1)}, u32[]{:S(2)}, u32[]{:S(2)}) collective-permute-start(f32[4,4,16,128]{3,2,1,0:T(8,128)S(1)} %copy-done), channel_id=1, source_target_pairs={{0,1},{1,0},{2,3},{3,2},{4,8},{5,9},{6,10},{7,11},{8,4},{9,5},{10,... | collective-permute-start | bytes 393224 | tf_op jit(solution)/shard_map/ppermute | solution.py:313
  7.6 3.4 %copy-start.1 = (f32[4,9]{1,0:T(4,128)S(1)}, f32[4,9]{1,0:T(4,128)}, u32[]{:S(2)}) copy-start(f32[4,9]{1,0:T(4,128)} %rates.3) | copy-start | bytes 436
  7.6 4.0 %collective-permute-start.4 = (f32[4,2,2,128]{3,2,1,0:T(2,128)S(1)}, f32[4,2,2,128]{3,2,1,0:T(2,128)S(1)}, u32[]{:S(2)}, u32[]{:S(2)}) collective-permute-start(f32[4,2,2,128]{3,2,1,0:T(2,128)S(1)} %get-tuple-element.29), channel_id=1, source_target_pairs={{0,1},{1,0},{2,3},{3,2},{4,8},{5,9},{6,10},{7,11},{8,4},{9,5},{10,... | collective-permute-start | bytes 24584 | tf_op jit(solution)/shard_map/ppermute | solution.py:313
  7.8 4.8 %collective-permute-start.5 = (f32[4,2,2,128]{3,2,1,0:T(2,128)S(1)}, f32[4,2,2,128]{3,2,1,0:T(2,128)S(1)}, u32[]{:S(2)}, u32[]{:S(2)}) collective-permute-start(f32[4,2,2,128]{3,2,1,0:T(2,128)S(1)} %get-tuple-element.28), channel_id=1, source_target_pairs={{0,4},{1,5},{2,6},{3,7},{4,0},{5,1},{6,2},{7,3},{8,12},{9,13},{10,... | collective-permute-start | bytes 24584 | tf_op jit(solution)/shard_map/ppermute | solution.py:313

commit v13 on v12

--- a/solution.py
+++ b/solution.py
@@ -396,7 +396,7 @@
         name="corners",
     )(rate_table, lines, odd_corners, even_corners, parts)
 
-    order = [0] + [i for i in range(devices - 1, 0, -1)]
+    order = list(range(devices - 1, -1, -1))
     gathered = lax.all_to_all(message, ("gx", "gy"), 0, 0, axis_index_groups=[order], tiled=True)
 
     return pl.pallas_call(

time: 26.2 us -> 26.2 us (level)
  no operation moved by 1% of the time
where the time goes in v13:
time: 26.2 us; the launch traced here: 26.1 us
  blocking collectives  12.3 us (47%)
  starting transfers between devices  7.83 us (30%)
  waiting for transfers between devices  3.34 us (13%)
  Pallas kernels  1.88 us (7%)
  between operations  0.71 us (3%)
    all_to_all x1, blocking collectives, shards(): lax.all_to_all(message, ('gx', 'gy'), 0, 0, axis_index_groups=[order], ti...  12.3 us
    ppermute x6, starting transfers between devices, swap(): return lax.ppermute(value, ('gx', 'gy'), pairs)  7.83 us
    ppermute x6, waiting for transfers between devices, swap(): return lax.ppermute(value, ('gx', 'gy'), pairs)  3.34 us
    pallas_call x1, Pallas kernels, shards(): pl.pallas_call(combine_kernel, out_shape=[block, jax.ShapeDtypeStruct((me...  0.83 us
    pallas_call x1, Pallas kernels, shards(): pl.pallas_call(functools.partial(images_kernel, lattice), out_shape=[bloc...  0.65 us
  transfers between devices with their start and end apart: 6, of which 3 were waited for; matrix products, arithmetic and copies ran while one was open for 0% of the time, Pallas kernels for 3%

profile of v13, /device:TPU:0, one launch (start us, length us, event | category | flops | bytes accessed | tf_op | source)
XLA Modules:
  0.0 26.1 jit_solution(956031888590698999)
XLA Ops:
  0.6 0.0 copy-start
  0.6 3.0 %collective-permute-start = (f32[4,4,16,128]{3,2,1,0:T(8,128)}, f32[4,4,16,128]{3,2,1,0:T(8,128)S(1)}, u32[]{:S(2)}, u32[]{:S(2)}) collective-permute-start(f32[4,4,16,128]{3,2,1,0:T(8,128)} %field.5), channel_id=1, source_target_pairs={{0,4},{1,5},{2,6},{3,7},{4,0},{5,1},{6,2},{7,3},{8,12},{9,13},{10,... | collective-permute-start | bytes 393224 | tf_op jit(solution)/shard_map/ppermute | solution.py:313
  3.6 0.0 copy-done
  3.7 0.1 collective-permute-start.2
  3.7 0.9 %collective-permute-start.1 = (f32[4,4,2,128]{3,2,1,0:T(2,128)S(1)}, f32[4,4,2,128]{3,2,1,0:T(2,128)S(1)}, u32[]{:S(2)}, u32[]{:S(2)}) collective-permute-start(f32[4,4,2,128]{3,2,1,0:T(2,128)S(1)} %get-tuple-element.15), channel_id=1, source_target_pairs={{0,4},{1,2},{2,1},{3,7},{4,0},{5,6},{6,5},{7,3},{8,12},{9,10},{10,... | collective-permute-start | bytes 49160 | tf_op jit(solution)/shard_map/ppermute | solution.py:313
  4.6 0.3 %collective-permute-done.2.even_y = f32[4,4,2,128]{3,2,1,0:T(2,128)S(1)} collective-permute-done((f32[4,4,2,128]{3,2,1,0:T(2,128)S(1)}, f32[4,4,2,128]{3,2,1,0:T(2,128)S(1)}, u32[]{:S(2)}, u32[]{:S(2)}) %collective-permute-start.2) | collective-permute-done | bytes 16416 | tf_op jit(solution)/shard_map/ppermute | solution.py:313
  4.9 0.5 %collective-permute-start.3 = (f32[4,4,16,128]{3,2,1,0:T(8,128)S(1)}, f32[4,4,16,128]{3,2,1,0:T(8,128)S(1)}, u32[]{:S(2)}, u32[]{:S(2)}) collective-permute-start(f32[4,4,16,128]{3,2,1,0:T(8,128)S(1)} %copy-done), channel_id=1, source_target_pairs={{0,1},{1,0},{2,3},{3,2},{4,8},{5,9},{6,10},{7,11},{8,4},{9,5},{10,... | collective-permute-start | bytes 393224 | tf_op jit(solution)/shard_map/ppermute | solution.py:313
  5.4 2.1 %collective-permute-done.1.odd_y = f32[4,4,2,128]{3,2,1,0:T(2,128)S(1)} collective-permute-done((f32[4,4,2,128]{3,2,1,0:T(2,128)S(1)}, f32[4,4,2,128]{3,2,1,0:T(2,128)S(1)}, u32[]{:S(2)}, u32[]{:S(2)}) %collective-permute-start.1) | collective-permute-done | bytes 16416 | tf_op jit(solution)/shard_map/ppermute | solution.py:313
  7.5 0.0 collective-permute-done.even_x
  7.6 0.0 copy-start.1
  7.6 0.2 collective-permute-start.4
  7.8 3.2 %collective-permute-start.5 = (f32[4,2,2,128]{3,2,1,0:T(2,128)S(1)}, f32[4,2,2,128]{3,2,1,0:T(2,128)S(1)}, u32[]{:S(2)}, u32[]{:S(2)}) collective-permute-start(f32[4,2,2,128]{3,2,1,0:T(2,128)S(1)} %get-tuple-element.28), channel_id=1, source_target_pairs={{0,4},{1,5},{2,6},{3,7},{4,0},{5,1},{6,2},{7,3},{8,12},{9,13},{10,... | collective-permute-start | bytes 24584 | tf_op jit(solution)/shard_map/ppermute | solution.py:313
  11.0 0.0 collective-permute-done.3.odd_x
  11.0 0.0 copy-done.1
  11.0 0.7 %images.1 = (f32[4,4,16,128]{3,2,1,0:T(8,128)S(1)}, f32[4,4,16,128]{3,2,1,0:T(8,128)S(1)}, f32[4,10,8,128]{3,2,1,0:T(8,128)S(1)}, f32[48,128]{1,0:T(8,128)S(1)}) custom-call(f32[4,9]{1,0:T(4,128)S(1)} %copy-done.1, f32[4,4,16,128]{3,2,1,0:T(8,128)S(1)} %copy-done, f32[4,4,16,128]{3,2,1,0:T(8,128)S(1)} %collective-permute-done.even_x, ...), custom_call_target="tpu_custom_call" | custom-call | tf_op jit(solution)/shard_map/images/pallas_call | solution.py:365
  11.6 0.0 collective-permute-done.4.odd_corners
  11.7 0.9 %collective-permute-done.5.even_corners = f32[4,2,2,128]{3,2,1,0:T(2,128)S(1)} collective-permute-done((f32[4,2,2,128]{3,2,1,0:T(2,128)S(1)}, f32[4,2,2,128]{3,2,1,0:T(2,128)S(1)}, u32[]{:S(2)}, u32[]{:S(2)}) %collective-permute-start.5) | collective-permute-done | bytes 8224 | tf_op jit(solution)/shard_map/ppermute | solution.py:313
  12.6 0.4 %corners.1 = (f32[4,2,4,128]{3,2,1,0:T(4,128)S(1)}, f32[32,128]{1,0:T(8,128)S(1)}) custom-call(f32[4,9]{1,0:T(4,128)S(1)} %copy-done.1, f32[4,10,8,128]{3,2,1,0:T(8,128)S(1)} %get-tuple-element.22.lines, f32[4,2,2,128]{3,2,1,0:T(2,128)S(1)} %collective-permute-done.4.odd_corners, f32[4,2,2,128]{3,2,1,0:T(2,128)S(1)} %collective-permute-done.5.even_corners, ...), custom_call_target="tpu_custom_call" | custom-call | tf_op jit(solution)/shard_map/corners/pallas_call | solution.py:383
  13.0 12.3 %all_to_all.11 = f32[32,1,128]{2,1,0:T(1,128)S(1)} all-to-all(f32[32,1,128]{2,1,0:T(1,128)S(1)} %bitcast.5), channel_id=1, replica_groups={{31,30,29,28,27,26,25,24,23,22,21,20,19,18,17,16,15,14,13,12,11,10,9,8,..., dimensions={0} | all-to-all | bytes 32768 | tf_op jit(solution)/shard_map/all_to_all | solution.py:400
  25.3 0.8 %combine.1 = (f32[4,4,16,128]{3,2,1,0:T(8,128)}, f32[4,5]{1,0:T(4,128)}) custom-call(f32[32,128]{1,0:T(8,128)S(1)} %bitcast.4, f32[4,4,16,128]{3,2,1,0:T(8,128)S(1)} %copy-done, f32[4,4,16,128]{3,2,1,0:T(8,128)S(1)} %get-tuple-element.25.image_one, f32[4,4,16,128]{3,2,1,0:T(8,128)S(1)} %get-tuple-element.26.image_two, ...), custom_call_target="tpu_custom_call" | custom-call | tf_op jit(solution)/shard_map/combine/pallas_call | solution.py:402
  (6 shorter events, 0.1 us)
Async XLA Ops:
  0.6 3.0 %copy-start = (f32[4,4,16,128]{3,2,1,0:T(8,128)S(1)}, f32[4,4,16,128]{3,2,1,0:T(8,128)}, u32[]{:S(2)}) copy-start(f32[4,4,16,128]{3,2,1,0:T(8,128)} %field.5) | copy-start | bytes 393220
  0.6 6.9 %collective-permute-start = (f32[4,4,16,128]{3,2,1,0:T(8,128)}, f32[4,4,16,128]{3,2,1,0:T(8,128)S(1)}, u32[]{:S(2)}, u32[]{:S(2)}) collective-permute-start(f32[4,4,16,128]{3,2,1,0:T(8,128)} %field.5), channel_id=1, source_target_pairs={{0,4},{1,5},{2,6},{3,7},{4,0},{5,1},{6,2},{7,3},{8,12},{9,13},{10,... | collective-permute-start | bytes 393224 | tf_op jit(solution)/shard_map/ppermute | solution.py:313
  3.7 1.2 %collective-permute-start.2 = (f32[4,4,2,128]{3,2,1,0:T(2,128)S(1)}, f32[4,4,2,128]{3,2,1,0:T(2,128)S(1)}, u32[]{:S(2)}, u32[]{:S(2)}) collective-permute-start(f32[4,4,2,128]{3,2,1,0:T(2,128)S(1)} %get-tuple-element.16), channel_id=1, source_target_pairs={{0,1},{1,0},{2,3},{3,2},{4,5},{5,4},{6,7},{7,6},{8,9},{9,8},{10,11... | collective-permute-start | bytes 49160 | tf_op jit(solution)/shard_map/ppermute | solution.py:313
  3.7 3.8 %collective-permute-start.1 = (f32[4,4,2,128]{3,2,1,0:T(2,128)S(1)}, f32[4,4,2,128]{3,2,1,0:T(2,128)S(1)}, u32[]{:S(2)}, u32[]{:S(2)}) collective-permute-start(f32[4,4,2,128]{3,2,1,0:T(2,128)S(1)} %get-tuple-element.15), channel_id=1, source_target_pairs={{0,4},{1,2},{2,1},{3,7},{4,0},{5,6},{6,5},{7,3},{8,12},{9,10},{10,... | collective-permute-start | bytes 49160 | tf_op jit(solution)/shard_map/ppermute | solution.py:313
  4.9 6.1 %collective-permute-start.3 = (f32[4,4,16,128]{3,2,1,0:T(8,128)S(1)}, f32[4,4,16,128]{3,2,1,0:T(8,128)S(1)}, u32[]{:S(2)}, u32[]{:S(2)}) collective-permute-start(f32[4,4,16,128]{3,2,1,0:T(8,128)S(1)} %copy-done), channel_id=1, source_target_pairs={{0,1},{1,0},{2,3},{3,2},{4,8},{5,9},{6,10},{7,11},{8,4},{9,5},{10,... | collective-permute-start | bytes 393224 | tf_op jit(solution)/shard_map/ppermute | solution.py:313
  7.6 3.4 %copy-start.1 = (f32[4,9]{1,0:T(4,128)S(1)}, f32[4,9]{1,0:T(4,128)}, u32[]{:S(2)}) copy-start(f32[4,9]{1,0:T(4,128)} %rates.3) | copy-start | bytes 436
  7.6 4.0 %collective-permute-start.4 = (f32[4,2,2,128]{3,2,1,0:T(2,128)S(1)}, f32[4,2,2,128]{3,2,1,0:T(2,128)S(1)}, u32[]{:S(2)}, u32[]{:S(2)}) collective-permute-start(f32[4,2,2,128]{3,2,1,0:T(2,128)S(1)} %get-tuple-element.29), channel_id=1, source_target_pairs={{0,1},{1,0},{2,3},{3,2},{4,8},{5,9},{6,10},{7,11},{8,4},{9,5},{10,... | collective-permute-start | bytes 24584 | tf_op jit(solution)/shard_map/ppermute | solution.py:313
  7.8 4.8 %collective-permute-start.5 = (f32[4,2,2,128]{3,2,1,0:T(2,128)S(1)}, f32[4,2,2,128]{3,2,1,0:T(2,128)S(1)}, u32[]{:S(2)}, u32[]{:S(2)}) collective-permute-start(f32[4,2,2,128]{3,2,1,0:T(2,128)S(1)} %get-tuple-element.28), channel_id=1, source_target_pairs={{0,4},{1,5},{2,6},{3,7},{4,0},{5,1},{6,2},{7,3},{8,12},{9,13},{10,... | collective-permute-start | bytes 24584 | tf_op jit(solution)/shard_map/ppermute | solution.py:313

commit v14 on v11

--- a/solution.py
+++ b/solution.py
@@ -198,7 +198,7 @@
 
             c, make_u, make_v, lose_v, rest = at_column(column)
             gain = make_v if side == 0 else lose_v
-            fixed[...] = lines[member, side]
+            fixed[:tall, :] = lines[member, side]
             for first in (0, HALF + rows):
                 fixed[first : first + HALF, :] = fixed[first : first + HALF, :] + gain * outer[first : first + HALF, :]
 
@@ -374,7 +374,7 @@
         out_specs=[vmem] * 4,
         scratch_shapes=[
             pltpu.VMEM((members, (rows + 2 * REACH) * span, depth), jnp.float32),
-            pltpu.VMEM((members, tall * span, depth), jnp.float32),
+            pltpu.VMEM((members, (tall + 1) * span, depth), jnp.float32),
         ],
         compiler_params=pltpu.CompilerParams(vmem_limit_bytes=8 * 2**20),
         name="images",
@@ -389,7 +389,7 @@
         in_specs=[vmem] * 5,
         out_specs=[vmem, vmem],
         scratch_shapes=[
-            pltpu.VMEM((members, 2, 2, tall, depth), jnp.float32),
+            pltpu.VMEM((members, 2, 2, 2 * tall, depth), jnp.float32),
             pltpu.VMEM((48, depth), jnp.float32),
         ],
         compiler_params=pltpu.CompilerParams(vmem_limit_bytes=4 * 2**20),

time: 26.2 us -> 26.2 us (level)
  no operation moved by 1% of the time
where the time goes in v14:
time: 26.2 us; the launch traced here: 26.1 us
  blocking collectives  12.3 us (47%)
  starting transfers between devices  7.83 us (30%)
  waiting for transfers between devices  3.34 us (13%)
  Pallas kernels  1.88 us (7%)
  between operations  0.7 us (3%)
    all_to_all x1, blocking collectives, shards(): gathered = lax.all_to_all(message, ('gy', 'gx'), 0, 0, tiled=True)  12.3 us
    ppermute x6, starting transfers between devices, swap(): return lax.ppermute(value, ('gx', 'gy'), pairs)  7.83 us
    ppermute x6, waiting for transfers between devices, swap(): return lax.ppermute(value, ('gx', 'gy'), pairs)  3.34 us
    pallas_call x1, Pallas kernels, shards(): pl.pallas_call(combine_kernel, out_shape=[block, jax.ShapeDtypeStruct((me...  0.83 us
    pallas_call x1, Pallas kernels, shards(): pl.pallas_call(functools.partial(images_kernel, lattice), out_shape=[bloc...  0.65 us
  transfers between devices with their start and end apart: 6, of which 3 were waited for; matrix products, arithmetic and copies ran while one was open for 0% of the time, Pallas kernels for 3%

profile of v14, /device:TPU:0, one launch (start us, length us, event | category | flops | bytes accessed | tf_op | source)
XLA Modules:
  0.0 26.1 jit_solution(17807563052619784145)
XLA Ops:
  0.6 0.0 copy-start
  0.6 3.0 %collective-permute-start = (f32[4,4,16,128]{3,2,1,0:T(8,128)}, f32[4,4,16,128]{3,2,1,0:T(8,128)S(1)}, u32[]{:S(2)}, u32[]{:S(2)}) collective-permute-start(f32[4,4,16,128]{3,2,1,0:T(8,128)} %field.5), channel_id=1, source_target_pairs={{0,4},{1,5},{2,6},{3,7},{4,0},{5,1},{6,2},{7,3},{8,12},{9,13},{10,... | collective-permute-start | bytes 393224 | tf_op jit(solution)/shard_map/ppermute | solution.py:313
  3.6 0.0 copy-done
  3.7 0.1 collective-permute-start.2
  3.7 0.9 %collective-permute-start.1 = (f32[4,4,2,128]{3,2,1,0:T(2,128)S(1)}, f32[4,4,2,128]{3,2,1,0:T(2,128)S(1)}, u32[]{:S(2)}, u32[]{:S(2)}) collective-permute-start(f32[4,4,2,128]{3,2,1,0:T(2,128)S(1)} %get-tuple-element.15), channel_id=1, source_target_pairs={{0,4},{1,2},{2,1},{3,7},{4,0},{5,6},{6,5},{7,3},{8,12},{9,10},{10,... | collective-permute-start | bytes 49160 | tf_op jit(solution)/shard_map/ppermute | solution.py:313
  4.6 0.3 %collective-permute-done.2.even_y = f32[4,4,2,128]{3,2,1,0:T(2,128)S(1)} collective-permute-done((f32[4,4,2,128]{3,2,1,0:T(2,128)S(1)}, f32[4,4,2,128]{3,2,1,0:T(2,128)S(1)}, u32[]{:S(2)}, u32[]{:S(2)}) %collective-permute-start.2) | collective-permute-done | bytes 16416 | tf_op jit(solution)/shard_map/ppermute | solution.py:313
  4.9 0.5 %collective-permute-start.3 = (f32[4,4,16,128]{3,2,1,0:T(8,128)S(1)}, f32[4,4,16,128]{3,2,1,0:T(8,128)S(1)}, u32[]{:S(2)}, u32[]{:S(2)}) collective-permute-start(f32[4,4,16,128]{3,2,1,0:T(8,128)S(1)} %copy-done), channel_id=1, source_target_pairs={{0,1},{1,0},{2,3},{3,2},{4,8},{5,9},{6,10},{7,11},{8,4},{9,5},{10,... | collective-permute-start | bytes 393224 | tf_op jit(solution)/shard_map/ppermute | solution.py:313
  5.4 2.1 %collective-permute-done.1.odd_y = f32[4,4,2,128]{3,2,1,0:T(2,128)S(1)} collective-permute-done((f32[4,4,2,128]{3,2,1,0:T(2,128)S(1)}, f32[4,4,2,128]{3,2,1,0:T(2,128)S(1)}, u32[]{:S(2)}, u32[]{:S(2)}) %collective-permute-start.1) | collective-permute-done | bytes 16416 | tf_op jit(solution)/shard_map/ppermute | solution.py:313
  7.5 0.0 collective-permute-done.even_x
  7.6 0.0 copy-start.1
  7.6 0.2 collective-permute-start.4
  7.8 3.2 %collective-permute-start.5 = (f32[4,2,2,128]{3,2,1,0:T(2,128)S(1)}, f32[4,2,2,128]{3,2,1,0:T(2,128)S(1)}, u32[]{:S(2)}, u32[]{:S(2)}) collective-permute-start(f32[4,2,2,128]{3,2,1,0:T(2,128)S(1)} %get-tuple-element.28), channel_id=1, source_target_pairs={{0,4},{1,5},{2,6},{3,7},{4,0},{5,1},{6,2},{7,3},{8,12},{9,13},{10,... | collective-permute-start | bytes 24584 | tf_op jit(solution)/shard_map/ppermute | solution.py:313
  11.0 0.0 collective-permute-done.3.odd_x
  11.0 0.0 copy-done.1
  11.0 0.7 %images.1 = (f32[4,4,16,128]{3,2,1,0:T(8,128)S(1)}, f32[4,4,16,128]{3,2,1,0:T(8,128)S(1)}, f32[4,10,8,128]{3,2,1,0:T(8,128)S(1)}, f32[48,128]{1,0:T(8,128)S(1)}) custom-call(f32[4,9]{1,0:T(4,128)S(1)} %copy-done.1, f32[4,4,16,128]{3,2,1,0:T(8,128)S(1)} %copy-done, f32[4,4,16,128]{3,2,1,0:T(8,128)S(1)} %collective-permute-done.even_x, ...), custom_call_target="tpu_custom_call" | custom-call | tf_op jit(solution)/shard_map/images/pallas_call | solution.py:365
  11.6 0.0 collective-permute-done.4.odd_corners
  11.7 0.9 %collective-permute-done.5.even_corners = f32[4,2,2,128]{3,2,1,0:T(2,128)S(1)} collective-permute-done((f32[4,2,2,128]{3,2,1,0:T(2,128)S(1)}, f32[4,2,2,128]{3,2,1,0:T(2,128)S(1)}, u32[]{:S(2)}, u32[]{:S(2)}) %collective-permute-start.5) | collective-permute-done | bytes 8224 | tf_op jit(solution)/shard_map/ppermute | solution.py:313
  12.6 0.4 %corners.1 = (f32[4,2,4,128]{3,2,1,0:T(4,128)S(1)}, f32[32,128]{1,0:T(8,128)S(1)}) custom-call(f32[4,9]{1,0:T(4,128)S(1)} %copy-done.1, f32[4,10,8,128]{3,2,1,0:T(8,128)S(1)} %get-tuple-element.22.lines, f32[4,2,2,128]{3,2,1,0:T(2,128)S(1)} %collective-permute-done.4.odd_corners, f32[4,2,2,128]{3,2,1,0:T(2,128)S(1)} %collective-permute-done.5.even_corners, ...), custom_call_target="tpu_custom_call" | custom-call | tf_op jit(solution)/shard_map/corners/pallas_call | solution.py:383
  13.0 12.3 %all_to_all.11 = f32[32,1,128]{2,1,0:T(1,128)S(1)} all-to-all(f32[32,1,128]{2,1,0:T(1,128)S(1)} %bitcast.5), channel_id=1, replica_groups=mesh['gx'=8,'gy'=4] {'gy','gx'}, dimensions={0} | all-to-all | bytes 32768 | tf_op jit(solution)/shard_map/all_to_all | solution.py:399
  25.3 0.8 %combine.1 = (f32[4,4,16,128]{3,2,1,0:T(8,128)}, f32[4,5]{1,0:T(4,128)}) custom-call(f32[32,128]{1,0:T(8,128)S(1)} %bitcast.4, f32[4,4,16,128]{3,2,1,0:T(8,128)S(1)} %copy-done, f32[4,4,16,128]{3,2,1,0:T(8,128)S(1)} %get-tuple-element.25.image_one, f32[4,4,16,128]{3,2,1,0:T(8,128)S(1)} %get-tuple-element.26.image_two, ...), custom_call_target="tpu_custom_call" | custom-call | tf_op jit(solution)/shard_map/combine/pallas_call | solution.py:401
  (6 shorter events, 0.1 us)
Async XLA Ops:
  0.6 3.0 %copy-start = (f32[4,4,16,128]{3,2,1,0:T(8,128)S(1)}, f32[4,4,16,128]{3,2,1,0:T(8,128)}, u32[]{:S(2)}) copy-start(f32[4,4,16,128]{3,2,1,0:T(8,128)} %field.5) | copy-start | bytes 393220
  0.6 6.9 %collective-permute-start = (f32[4,4,16,128]{3,2,1,0:T(8,128)}, f32[4,4,16,128]{3,2,1,0:T(8,128)S(1)}, u32[]{:S(2)}, u32[]{:S(2)}) collective-permute-start(f32[4,4,16,128]{3,2,1,0:T(8,128)} %field.5), channel_id=1, source_target_pairs={{0,4},{1,5},{2,6},{3,7},{4,0},{5,1},{6,2},{7,3},{8,12},{9,13},{10,... | collective-permute-start | bytes 393224 | tf_op jit(solution)/shard_map/ppermute | solution.py:313
  3.7 1.2 %collective-permute-start.2 = (f32[4,4,2,128]{3,2,1,0:T(2,128)S(1)}, f32[4,4,2,128]{3,2,1,0:T(2,128)S(1)}, u32[]{:S(2)}, u32[]{:S(2)}) collective-permute-start(f32[4,4,2,128]{3,2,1,0:T(2,128)S(1)} %get-tuple-element.16), channel_id=1, source_target_pairs={{0,1},{1,0},{2,3},{3,2},{4,5},{5,4},{6,7},{7,6},{8,9},{9,8},{10,11... | collective-permute-start | bytes 49160 | tf_op jit(solution)/shard_map/ppermute | solution.py:313
  3.7 3.8 %collective-permute-start.1 = (f32[4,4,2,128]{3,2,1,0:T(2,128)S(1)}, f32[4,4,2,128]{3,2,1,0:T(2,128)S(1)}, u32[]{:S(2)}, u32[]{:S(2)}) collective-permute-start(f32[4,4,2,128]{3,2,1,0:T(2,128)S(1)} %get-tuple-element.15), channel_id=1, source_target_pairs={{0,4},{1,2},{2,1},{3,7},{4,0},{5,6},{6,5},{7,3},{8,12},{9,10},{10,... | collective-permute-start | bytes 49160 | tf_op jit(solution)/shard_map/ppermute | solution.py:313
  4.9 6.1 %collective-permute-start.3 = (f32[4,4,16,128]{3,2,1,0:T(8,128)S(1)}, f32[4,4,16,128]{3,2,1,0:T(8,128)S(1)}, u32[]{:S(2)}, u32[]{:S(2)}) collective-permute-start(f32[4,4,16,128]{3,2,1,0:T(8,128)S(1)} %copy-done), channel_id=1, source_target_pairs={{0,1},{1,0},{2,3},{3,2},{4,8},{5,9},{6,10},{7,11},{8,4},{9,5},{10,... | collective-permute-start | bytes 393224 | tf_op jit(solution)/shard_map/ppermute | solution.py:313
  7.6 3.4 %copy-start.1 = (f32[4,9]{1,0:T(4,128)S(1)}, f32[4,9]{1,0:T(4,128)}, u32[]{:S(2)}) copy-start(f32[4,9]{1,0:T(4,128)} %rates.3) | copy-start | bytes 436
  7.6 4.0 %collective-permute-start.4 = (f32[4,2,2,128]{3,2,1,0:T(2,128)S(1)}, f32[4,2,2,128]{3,2,1,0:T(2,128)S(1)}, u32[]{:S(2)}, u32[]{:S(2)}) collective-permute-start(f32[4,2,2,128]{3,2,1,0:T(2,128)S(1)} %get-tuple-element.29), channel_id=1, source_target_pairs={{0,1},{1,0},{2,3},{3,2},{4,8},{5,9},{6,10},{7,11},{8,4},{9,5},{10,... | collective-permute-start | bytes 24584 | tf_op jit(solution)/shard_map/ppermute | solution.py:313
  7.8 4.8 %collective-permute-start.5 = (f32[4,2,2,128]{3,2,1,0:T(2,128)S(1)}, f32[4,2,2,128]{3,2,1,0:T(2,128)S(1)}, u32[]{:S(2)}, u32[]{:S(2)}) collective-permute-start(f32[4,2,2,128]{3,2,1,0:T(2,128)S(1)} %get-tuple-element.28), channel_id=1, source_target_pairs={{0,4},{1,5},{2,6},{3,7},{4,0},{5,1},{6,2},{7,3},{8,12},{9,13},{10,... | collective-permute-start | bytes 24584 | tf_op jit(solution)/shard_map/ppermute | solution.py:313

commit v15 on v14

--- a/solution.py
+++ b/solution.py
@@ -350,7 +350,6 @@
 
     even_y, for_odd_x = lax.optimization_barrier((even_y, initial if rows == REACH else jnp.where(is_even, initial, last)))
     odd_x = swap("gx", size_x, 1, for_odd_x)
-    even_x, odd_y, even_y = lax.optimization_barrier((even_x, odd_y, even_y))
 
     def corners(first):
         even, odd = even_y[:, first : first + HALF], odd_y[:, first : first + HALF]

time: 26.2 us -> 29.5 us (1.13)
  waiting for transfers between devices: 3.34 us -> 5.78 us
  local copies, waits for them, and re-layouts: 0.02 us -> 0.89 us
    ppermute x6, waiting for transfers between devices: 3.34 us -> 5.78 us  [swap(): return lax.ppermute(value, ('gx', 'gy'), pairs)]
    unnamed x4, local copies, waits for them, and re-layouts: 0.01 us -> 0.88 us
  transfers between devices with their start and end apart: 6 -> 6, of which waited for: 3 -> 2; matrix products, arithmetic and copies ran while one was open for 0% -> 0% of each run, Pallas kernels for 3% -> 2%
where the time goes in v15:
time: 29.5 us; the launch traced here: 29.3 us
  blocking collectives  12.2 us (41%)
  starting transfers between devices  7.81 us (26%)
  waiting for transfers between devices  5.78 us (20%)
  Pallas kernels  1.89 us (6%)
  local copies, waits for them, and re-layouts  0.89 us (3%)
  between operations  0.7 us (2%)
    all_to_all x1, blocking collectives, shards(): gathered = lax.all_to_all(message, ('gy', 'gx'), 0, 0, tiled=True)  12.2 us
    ppermute x6, starting transfers between devices, swap(): return lax.ppermute(value, ('gx', 'gy'), pairs)  7.81 us
    ppermute x6, waiting for transfers between devices, swap(): return lax.ppermute(value, ('gx', 'gy'), pairs)  5.78 us
    unnamed x4, local copies, waits for them, and re-layouts  0.88 us
    pallas_call x1, Pallas kernels, shards(): pl.pallas_call(combine_kernel, out_shape=[block, jax.ShapeDtypeStruct((me...  0.83 us
    pallas_call x1, Pallas kernels, shards(): pl.pallas_call(functools.partial(images_kernel, lattice), out_shape=[bloc...  0.66 us
  transfers between devices with their start and end apart: 6, of which 2 were waited for; matrix products, arithmetic and copies ran while one was open for 0% of the time, Pallas kernels for 2%

profile of v15, /device:TPU:0, one launch (start us, length us, event | category | flops | bytes accessed | tf_op | source)
XLA Modules:
  0.0 29.3 jit_solution(13185739583715033394)
XLA Ops:
  0.6 0.0 copy-start
  0.7 0.9 %copy-done = f32[4,4,16,128]{3,2,1,0:T(8,128)S(1)} copy-done((f32[4,4,16,128]{3,2,1,0:T(8,128)S(1)}, f32[4,4,16,128]{3,2,1,0:T(8,128)}, u32[]{:S(2)}) %copy-start) | copy-done | bytes 131096
  1.6 0.5 %collective-permute-start.1 = (f32[4,4,2,128]{3,2,1,0:T(2,128)S(1)}, f32[4,4,2,128]{3,2,1,0:T(2,128)S(1)}, u32[]{:S(2)}, u32[]{:S(2)}) collective-permute-start(f32[4,4,2,128]{3,2,1,0:T(2,128)S(1)} %get-tuple-element.12), channel_id=1, source_target_pairs={{0,1},{1,0},{2,3},{3,2},{4,5},{5,4},{6,7},{7,6},{8,9},{9,8},{10,11... | collective-permute-start | bytes 49160 | tf_op jit(solution)/shard_map/ppermute | solution.py:313
  2.1 2.6 %collective-permute-start = (f32[4,4,16,128]{3,2,1,0:T(8,128)S(1)}, f32[4,4,16,128]{3,2,1,0:T(8,128)S(1)}, u32[]{:S(2)}, u32[]{:S(2)}) collective-permute-start(f32[4,4,16,128]{3,2,1,0:T(8,128)S(1)} %copy-done), channel_id=1, source_target_pairs={{0,4},{1,5},{2,6},{3,7},{4,0},{5,1},{6,2},{7,3},{8,12},{9,13},{10,... | collective-permute-start | bytes 393224 | tf_op jit(solution)/shard_map/ppermute | solution.py:313
  4.6 0.1 collective-permute-start.3
  4.7 0.0 collective-permute-done.1.even_y
  4.7 1.6 %collective-permute-start.2 = (f32[4,4,16,128]{3,2,1,0:T(8,128)S(1)}, f32[4,4,16,128]{3,2,1,0:T(8,128)S(1)}, u32[]{:S(2)}, u32[]{:S(2)}) collective-permute-start(f32[4,4,16,128]{3,2,1,0:T(8,128)S(1)} %copy-done), channel_id=1, source_target_pairs={{0,1},{1,0},{2,3},{3,2},{4,8},{5,9},{6,10},{7,11},{8,4},{9,5},{10,... | collective-permute-start | bytes 393224 | tf_op jit(solution)/shard_map/ppermute | solution.py:313
  6.3 4.8 %collective-permute-done.3.odd_y = f32[4,4,2,128]{3,2,1,0:T(2,128)S(1)} collective-permute-done((f32[4,4,2,128]{3,2,1,0:T(2,128)S(1)}, f32[4,4,2,128]{3,2,1,0:T(2,128)S(1)}, u32[]{:S(2)}, u32[]{:S(2)}) %collective-permute-start.3) | collective-permute-done | bytes 16416 | tf_op jit(solution)/shard_map/ppermute | solution.py:313
  11.2 0.0 copy-start.1
  11.2 0.1 collective-permute-start.4
  11.3 3.0 %collective-permute-start.5 = (f32[4,2,2,128]{3,2,1,0:T(2,128)S(1)}, f32[4,2,2,128]{3,2,1,0:T(2,128)S(1)}, u32[]{:S(2)}, u32[]{:S(2)}) collective-permute-start(f32[4,2,2,128]{3,2,1,0:T(2,128)S(1)} %get-tuple-element.22), channel_id=1, source_target_pairs={{0,4},{1,5},{2,6},{3,7},{4,0},{5,1},{6,2},{7,3},{8,12},{9,13},{10,... | collective-permute-start | bytes 24584 | tf_op jit(solution)/shard_map/ppermute | solution.py:313
  14.3 0.0 collective-permute-done.even_x
  14.3 0.0 collective-permute-done.2.odd_x
  14.3 0.0 copy-done.1
  14.3 0.7 %images.1 = (f32[4,4,16,128]{3,2,1,0:T(8,128)S(1)}, f32[4,4,16,128]{3,2,1,0:T(8,128)S(1)}, f32[4,10,8,128]{3,2,1,0:T(8,128)S(1)}, f32[48,128]{1,0:T(8,128)S(1)}) custom-call(f32[4,9]{1,0:T(4,128)S(1)} %copy-done.1, f32[4,4,16,128]{3,2,1,0:T(8,128)S(1)} %copy-done, f32[4,4,16,128]{3,2,1,0:T(8,128)S(1)} %collective-permute-done.even_x, ...), custom_call_target="tpu_custom_call" | custom-call | tf_op jit(solution)/shard_map/images/pallas_call | solution.py:364
  15.0 0.0 collective-permute-done.4.odd_corners
  15.0 0.9 %collective-permute-done.5.even_corners = f32[4,2,2,128]{3,2,1,0:T(2,128)S(1)} collective-permute-done((f32[4,2,2,128]{3,2,1,0:T(2,128)S(1)}, f32[4,2,2,128]{3,2,1,0:T(2,128)S(1)}, u32[]{:S(2)}, u32[]{:S(2)}) %collective-permute-start.5) | collective-permute-done | bytes 8224 | tf_op jit(solution)/shard_map/ppermute | solution.py:313
  15.9 0.4 %corners.1 = (f32[4,2,4,128]{3,2,1,0:T(4,128)S(1)}, f32[32,128]{1,0:T(8,128)S(1)}) custom-call(f32[4,9]{1,0:T(4,128)S(1)} %copy-done.1, f32[4,10,8,128]{3,2,1,0:T(8,128)S(1)} %get-tuple-element.16.lines, f32[4,2,2,128]{3,2,1,0:T(2,128)S(1)} %collective-permute-done.4.odd_corners, f32[4,2,2,128]{3,2,1,0:T(2,128)S(1)} %collective-permute-done.5.even_corners, ...), custom_call_target="tpu_custom_call" | custom-call | tf_op jit(solution)/shard_map/corners/pallas_call | solution.py:382
  16.3 12.2 %all_to_all.11 = f32[32,1,128]{2,1,0:T(1,128)S(1)} all-to-all(f32[32,1,128]{2,1,0:T(1,128)S(1)} %bitcast.5), channel_id=1, replica_groups=mesh['gx'=8,'gy'=4] {'gy','gx'}, dimensions={0} | all-to-all | bytes 32768 | tf_op jit(solution)/shard_map/all_to_all | solution.py:398
  28.5 0.8 %combine.1 = (f32[4,4,16,128]{3,2,1,0:T(8,128)}, f32[4,5]{1,0:T(4,128)}) custom-call(f32[32,128]{1,0:T(8,128)S(1)} %bitcast.4, f32[4,4,16,128]{3,2,1,0:T(8,128)S(1)} %copy-done, f32[4,4,16,128]{3,2,1,0:T(8,128)S(1)} %get-tuple-element.19.image_one, f32[4,4,16,128]{3,2,1,0:T(8,128)S(1)} %get-tuple-element.20.image_two, ...), custom_call_target="tpu_custom_call" | custom-call | tf_op jit(solution)/shard_map/combine/pallas_call | solution.py:400
  (6 shorter events, 0.1 us)
Async XLA Ops:
  0.6 0.9 %copy-start = (f32[4,4,16,128]{3,2,1,0:T(8,128)S(1)}, f32[4,4,16,128]{3,2,1,0:T(8,128)}, u32[]{:S(2)}) copy-start(f32[4,4,16,128]{3,2,1,0:T(8,128)} %field.5) | copy-start | bytes 393220
  1.6 3.2 %collective-permute-start.1 = (f32[4,4,2,128]{3,2,1,0:T(2,128)S(1)}, f32[4,4,2,128]{3,2,1,0:T(2,128)S(1)}, u32[]{:S(2)}, u32[]{:S(2)}) collective-permute-start(f32[4,4,2,128]{3,2,1,0:T(2,128)S(1)} %get-tuple-element.12), channel_id=1, source_target_pairs={{0,1},{1,0},{2,3},{3,2},{4,5},{5,4},{6,7},{7,6},{8,9},{9,8},{10,11... | collective-permute-start | bytes 49160 | tf_op jit(solution)/shard_map/ppermute | solution.py:313
  2.1 12.2 %collective-permute-start = (f32[4,4,16,128]{3,2,1,0:T(8,128)S(1)}, f32[4,4,16,128]{3,2,1,0:T(8,128)S(1)}, u32[]{:S(2)}, u32[]{:S(2)}) collective-permute-start(f32[4,4,16,128]{3,2,1,0:T(8,128)S(1)} %copy-done), channel_id=1, source_target_pairs={{0,4},{1,5},{2,6},{3,7},{4,0},{5,1},{6,2},{7,3},{8,12},{9,13},{10,... | collective-permute-start | bytes 393224 | tf_op jit(solution)/shard_map/ppermute | solution.py:313
  4.6 6.5 %collective-permute-start.3 = (f32[4,4,2,128]{3,2,1,0:T(2,128)S(1)}, f32[4,4,2,128]{3,2,1,0:T(2,128)S(1)}, u32[]{:S(2)}, u32[]{:S(2)}) collective-permute-start(f32[4,4,2,128]{3,2,1,0:T(2,128)S(1)} %get-tuple-element.15), channel_id=1, source_target_pairs={{0,4},{1,2},{2,1},{3,7},{4,0},{5,6},{6,5},{7,3},{8,12},{9,10},{10,... | collective-permute-start | bytes 49160 | tf_op jit(solution)/shard_map/ppermute | solution.py:313
  4.7 9.6 %collective-permute-start.2 = (f32[4,4,16,128]{3,2,1,0:T(8,128)S(1)}, f32[4,4,16,128]{3,2,1,0:T(8,128)S(1)}, u32[]{:S(2)}, u32[]{:S(2)}) collective-permute-start(f32[4,4,16,128]{3,2,1,0:T(8,128)S(1)} %copy-done), channel_id=1, source_target_pairs={{0,1},{1,0},{2,3},{3,2},{4,8},{5,9},{6,10},{7,11},{8,4},{9,5},{10,... | collective-permute-start | bytes 393224 | tf_op jit(solution)/shard_map/ppermute | solution.py:313
  11.2 3.1 %copy-start.1 = (f32[4,9]{1,0:T(4,128)S(1)}, f32[4,9]{1,0:T(4,128)}, u32[]{:S(2)}) copy-start(f32[4,9]{1,0:T(4,128)} %rates.3) | copy-start | bytes 436
  11.2 3.8 %collective-permute-start.4 = (f32[4,2,2,128]{3,2,1,0:T(2,128)S(1)}, f32[4,2,2,128]{3,2,1,0:T(2,128)S(1)}, u32[]{:S(2)}, u32[]{:S(2)}) collective-permute-start(f32[4,2,2,128]{3,2,1,0:T(2,128)S(1)} %get-tuple-element.23), channel_id=1, source_target_pairs={{0,1},{1,0},{2,3},{3,2},{4,8},{5,9},{6,10},{7,11},{8,4},{9,5},{10,... | collective-permute-start | bytes 24584 | tf_op jit(solution)/shard_map/ppermute | solution.py:313
  11.3 4.7 %collective-permute-start.5 = (f32[4,2,2,128]{3,2,1,0:T(2,128)S(1)}, f32[4,2,2,128]{3,2,1,0:T(2,128)S(1)}, u32[]{:S(2)}, u32[]{:S(2)}) collective-permute-start(f32[4,2,2,128]{3,2,1,0:T(2,128)S(1)} %get-tuple-element.22), channel_id=1, source_target_pairs={{0,4},{1,5},{2,6},{3,7},{4,0},{5,1},{6,2},{7,3},{8,12},{9,13},{10,... | collective-permute-start | bytes 24584 | tf_op jit(solution)/shard_map/ppermute | solution.py:313

commit v16 on v15

--- a/solution.py
+++ b/solution.py
@@ -302,7 +302,7 @@
             at = x if axis == "gx" else y
             other = at + 1 if (at - first) % 2 == 0 else at - 1
             if not 0 <= other < size:
-                return (x, y ^ 1) if axis == "gx" else (x ^ 1, y)
+                return (x, y ^ 1) if axis == "gx" else (x, other % size)
             return (other, y) if axis == "gx" else (x, other)
 
         pairs = [

time: 29.5 us -> 26.2 us (0.89)
  waiting for transfers between devices: 5.78 us -> 2.47 us
    ppermute x6, waiting for transfers between devices: 5.78 us -> 2.47 us  [swap(): return lax.ppermute(value, ('gx', 'gy'), pairs)]
  transfers between devices with their start and end apart: 6 -> 6, of which waited for: 2 -> 2; matrix products, arithmetic and copies ran while one was open for 0% -> 0% of each run, Pallas kernels for 2% -> 3%
where the time goes in v16:
time: 26.2 us; the launch traced here: 26.1 us
  blocking collectives  12.3 us (47%)
  starting transfers between devices  7.82 us (30%)
  waiting for transfers between devices  2.47 us (9%)
  Pallas kernels  1.89 us (7%)
  local copies, waits for them, and re-layouts  0.89 us (3%)
  between operations  0.69 us (3%)
    all_to_all x1, blocking collectives, shards(): gathered = lax.all_to_all(message, ('gy', 'gx'), 0, 0, tiled=True)  12.3 us
    ppermute x6, starting transfers between devices, swap(): return lax.ppermute(value, ('gx', 'gy'), pairs)  7.82 us
    ppermute x6, waiting for transfers between devices, swap(): return lax.ppermute(value, ('gx', 'gy'), pairs)  2.47 us
    unnamed x4, local copies, waits for them, and re-layouts  0.88 us
    pallas_call x1, Pallas kernels, shards(): pl.pallas_call(combine_kernel, out_shape=[block, jax.ShapeDtypeStruct((me...  0.83 us
    pallas_call x1, Pallas kernels, shards(): pl.pallas_call(functools.partial(images_kernel, lattice), out_shape=[bloc...  0.66 us
  transfers between devices with their start and end apart: 6, of which 2 were waited for; matrix products, arithmetic and copies ran while one was open for 0% of the time, Pallas kernels for 3%

profile of v16, /device:TPU:0, one launch (start us, length us, event | category | flops | bytes accessed | tf_op | source)
XLA Modules:
  0.0 26.1 jit_solution(16047094577087884152)
XLA Ops:
  0.6 0.0 copy-start
  0.7 0.9 %copy-done = f32[4,4,16,128]{3,2,1,0:T(8,128)S(1)} copy-done((f32[4,4,16,128]{3,2,1,0:T(8,128)S(1)}, f32[4,4,16,128]{3,2,1,0:T(8,128)}, u32[]{:S(2)}) %copy-start) | copy-done | bytes 131096
  1.6 0.5 %collective-permute-start.1 = (f32[4,4,2,128]{3,2,1,0:T(2,128)S(1)}, f32[4,4,2,128]{3,2,1,0:T(2,128)S(1)}, u32[]{:S(2)}, u32[]{:S(2)}) collective-permute-start(f32[4,4,2,128]{3,2,1,0:T(2,128)S(1)} %get-tuple-element.12), channel_id=1, source_target_pairs={{0,1},{1,0},{2,3},{3,2},{4,5},{5,4},{6,7},{7,6},{8,9},{9,8},{10,11... | collective-permute-start | bytes 49160 | tf_op jit(solution)/shard_map/ppermute | solution.py:313
  2.1 2.6 %collective-permute-start = (f32[4,4,16,128]{3,2,1,0:T(8,128)S(1)}, f32[4,4,16,128]{3,2,1,0:T(8,128)S(1)}, u32[]{:S(2)}, u32[]{:S(2)}) collective-permute-start(f32[4,4,16,128]{3,2,1,0:T(8,128)S(1)} %copy-done), channel_id=1, source_target_pairs={{0,4},{1,5},{2,6},{3,7},{4,0},{5,1},{6,2},{7,3},{8,12},{9,13},{10,... | collective-permute-start | bytes 393224 | tf_op jit(solution)/shard_map/ppermute | solution.py:313
  4.6 1.3 %collective-permute-start.3 = (f32[4,4,2,128]{3,2,1,0:T(2,128)S(1)}, f32[4,4,2,128]{3,2,1,0:T(2,128)S(1)}, u32[]{:S(2)}, u32[]{:S(2)}) collective-permute-start(f32[4,4,2,128]{3,2,1,0:T(2,128)S(1)} %get-tuple-element.15), channel_id=1, source_target_pairs={{0,3},{1,2},{2,1},{3,0},{4,7},{5,6},{6,5},{7,4},{8,11},{9,10},{10,... | collective-permute-start | bytes 49160 | tf_op jit(solution)/shard_map/ppermute | solution.py:313
  5.9 0.0 collective-permute-done.1.even_y
  5.9 0.3 %collective-permute-start.2 = (f32[4,4,16,128]{3,2,1,0:T(8,128)S(1)}, f32[4,4,16,128]{3,2,1,0:T(8,128)S(1)}, u32[]{:S(2)}, u32[]{:S(2)}) collective-permute-start(f32[4,4,16,128]{3,2,1,0:T(8,128)S(1)} %copy-done), channel_id=1, source_target_pairs={{0,1},{1,0},{2,3},{3,2},{4,8},{5,9},{6,10},{7,11},{8,4},{9,5},{10,... | collective-permute-start | bytes 393224 | tf_op jit(solution)/shard_map/ppermute | solution.py:313
  6.3 1.5 %collective-permute-done.3.odd_y = f32[4,4,2,128]{3,2,1,0:T(2,128)S(1)} collective-permute-done((f32[4,4,2,128]{3,2,1,0:T(2,128)S(1)}, f32[4,4,2,128]{3,2,1,0:T(2,128)S(1)}, u32[]{:S(2)}, u32[]{:S(2)}) %collective-permute-start.3) | collective-permute-done | bytes 16416 | tf_op jit(solution)/shard_map/ppermute | solution.py:313
  7.9 0.0 copy-start.1
  7.9 0.5 %collective-permute-start.4 = (f32[4,2,2,128]{3,2,1,0:T(2,128)S(1)}, f32[4,2,2,128]{3,2,1,0:T(2,128)S(1)}, u32[]{:S(2)}, u32[]{:S(2)}) collective-permute-start(f32[4,2,2,128]{3,2,1,0:T(2,128)S(1)} %get-tuple-element.23), channel_id=1, source_target_pairs={{0,1},{1,0},{2,3},{3,2},{4,8},{5,9},{6,10},{7,11},{8,4},{9,5},{10,... | collective-permute-start | bytes 24584 | tf_op jit(solution)/shard_map/ppermute | solution.py:313
  8.4 2.6 %collective-permute-start.5 = (f32[4,2,2,128]{3,2,1,0:T(2,128)S(1)}, f32[4,2,2,128]{3,2,1,0:T(2,128)S(1)}, u32[]{:S(2)}, u32[]{:S(2)}) collective-permute-start(f32[4,2,2,128]{3,2,1,0:T(2,128)S(1)} %get-tuple-element.22), channel_id=1, source_target_pairs={{0,4},{1,5},{2,6},{3,7},{4,0},{5,1},{6,2},{7,3},{8,12},{9,13},{10,... | collective-permute-start | bytes 24584 | tf_op jit(solution)/shard_map/ppermute | solution.py:313
  11.0 0.0 collective-permute-done.even_x
  11.0 0.0 collective-permute-done.2.odd_x
  11.0 0.0 copy-done.1
  11.0 0.7 %images.1 = (f32[4,4,16,128]{3,2,1,0:T(8,128)S(1)}, f32[4,4,16,128]{3,2,1,0:T(8,128)S(1)}, f32[4,10,8,128]{3,2,1,0:T(8,128)S(1)}, f32[48,128]{1,0:T(8,128)S(1)}) custom-call(f32[4,9]{1,0:T(4,128)S(1)} %copy-done.1, f32[4,4,16,128]{3,2,1,0:T(8,128)S(1)} %copy-done, f32[4,4,16,128]{3,2,1,0:T(8,128)S(1)} %collective-permute-done.even_x, ...), custom_call_target="tpu_custom_call" | custom-call | tf_op jit(solution)/shard_map/images/pallas_call | solution.py:364
  11.6 0.0 collective-permute-done.4.odd_corners
  11.7 0.9 %collective-permute-done.5.even_corners = f32[4,2,2,128]{3,2,1,0:T(2,128)S(1)} collective-permute-done((f32[4,2,2,128]{3,2,1,0:T(2,128)S(1)}, f32[4,2,2,128]{3,2,1,0:T(2,128)S(1)}, u32[]{:S(2)}, u32[]{:S(2)}) %collective-permute-start.5) | collective-permute-done | bytes 8224 | tf_op jit(solution)/shard_map/ppermute | solution.py:313
  12.6 0.4 %corners.1 = (f32[4,2,4,128]{3,2,1,0:T(4,128)S(1)}, f32[32,128]{1,0:T(8,128)S(1)}) custom-call(f32[4,9]{1,0:T(4,128)S(1)} %copy-done.1, f32[4,10,8,128]{3,2,1,0:T(8,128)S(1)} %get-tuple-element.16.lines, f32[4,2,2,128]{3,2,1,0:T(2,128)S(1)} %collective-permute-done.4.odd_corners, f32[4,2,2,128]{3,2,1,0:T(2,128)S(1)} %collective-permute-done.5.even_corners, ...), custom_call_target="tpu_custom_call" | custom-call | tf_op jit(solution)/shard_map/corners/pallas_call | solution.py:382
  13.0 12.3 %all_to_all.11 = f32[32,1,128]{2,1,0:T(1,128)S(1)} all-to-all(f32[32,1,128]{2,1,0:T(1,128)S(1)} %bitcast.5), channel_id=1, replica_groups=mesh['gx'=8,'gy'=4] {'gy','gx'}, dimensions={0} | all-to-all | bytes 32768 | tf_op jit(solution)/shard_map/all_to_all | solution.py:398
  25.3 0.8 %combine.1 = (f32[4,4,16,128]{3,2,1,0:T(8,128)}, f32[4,5]{1,0:T(4,128)}) custom-call(f32[32,128]{1,0:T(8,128)S(1)} %bitcast.4, f32[4,4,16,128]{3,2,1,0:T(8,128)S(1)} %copy-done, f32[4,4,16,128]{3,2,1,0:T(8,128)S(1)} %get-tuple-element.19.image_one, f32[4,4,16,128]{3,2,1,0:T(8,128)S(1)} %get-tuple-element.20.image_two, ...), custom_call_target="tpu_custom_call" | custom-call | tf_op jit(solution)/shard_map/combine/pallas_call | solution.py:400
  (6 shorter events, 0.1 us)
Async XLA Ops:
  0.6 0.9 %copy-start = (f32[4,4,16,128]{3,2,1,0:T(8,128)S(1)}, f32[4,4,16,128]{3,2,1,0:T(8,128)}, u32[]{:S(2)}) copy-start(f32[4,4,16,128]{3,2,1,0:T(8,128)} %field.5) | copy-start | bytes 393220
  1.6 4.4 %collective-permute-start.1 = (f32[4,4,2,128]{3,2,1,0:T(2,128)S(1)}, f32[4,4,2,128]{3,2,1,0:T(2,128)S(1)}, u32[]{:S(2)}, u32[]{:S(2)}) collective-permute-start(f32[4,4,2,128]{3,2,1,0:T(2,128)S(1)} %get-tuple-element.12), channel_id=1, source_target_pairs={{0,1},{1,0},{2,3},{3,2},{4,5},{5,4},{6,7},{7,6},{8,9},{9,8},{10,11... | collective-permute-start | bytes 49160 | tf_op jit(solution)/shard_map/ppermute | solution.py:313
  2.1 8.9 %collective-permute-start = (f32[4,4,16,128]{3,2,1,0:T(8,128)S(1)}, f32[4,4,16,128]{3,2,1,0:T(8,128)S(1)}, u32[]{:S(2)}, u32[]{:S(2)}) collective-permute-start(f32[4,4,16,128]{3,2,1,0:T(8,128)S(1)} %copy-done), channel_id=1, source_target_pairs={{0,4},{1,5},{2,6},{3,7},{4,0},{5,1},{6,2},{7,3},{8,12},{9,13},{10,... | collective-permute-start | bytes 393224 | tf_op jit(solution)/shard_map/ppermute | solution.py:313
  4.6 3.2 %collective-permute-start.3 = (f32[4,4,2,128]{3,2,1,0:T(2,128)S(1)}, f32[4,4,2,128]{3,2,1,0:T(2,128)S(1)}, u32[]{:S(2)}, u32[]{:S(2)}) collective-permute-start(f32[4,4,2,128]{3,2,1,0:T(2,128)S(1)} %get-tuple-element.15), channel_id=1, source_target_pairs={{0,3},{1,2},{2,1},{3,0},{4,7},{5,6},{6,5},{7,4},{8,11},{9,10},{10,... | collective-permute-start | bytes 49160 | tf_op jit(solution)/shard_map/ppermute | solution.py:313
  5.9 5.1 %collective-permute-start.2 = (f32[4,4,16,128]{3,2,1,0:T(8,128)S(1)}, f32[4,4,16,128]{3,2,1,0:T(8,128)S(1)}, u32[]{:S(2)}, u32[]{:S(2)}) collective-permute-start(f32[4,4,16,128]{3,2,1,0:T(8,128)S(1)} %copy-done), channel_id=1, source_target_pairs={{0,1},{1,0},{2,3},{3,2},{4,8},{5,9},{6,10},{7,11},{8,4},{9,5},{10,... | collective-permute-start | bytes 393224 | tf_op jit(solution)/shard_map/ppermute | solution.py:313
  7.9 3.1 %copy-start.1 = (f32[4,9]{1,0:T(4,128)S(1)}, f32[4,9]{1,0:T(4,128)}, u32[]{:S(2)}) copy-start(f32[4,9]{1,0:T(4,128)} %rates.3) | copy-start | bytes 436
  7.9 3.8 %collective-permute-start.4 = (f32[4,2,2,128]{3,2,1,0:T(2,128)S(1)}, f32[4,2,2,128]{3,2,1,0:T(2,128)S(1)}, u32[]{:S(2)}, u32[]{:S(2)}) collective-permute-start(f32[4,2,2,128]{3,2,1,0:T(2,128)S(1)} %get-tuple-element.23), channel_id=1, source_target_pairs={{0,1},{1,0},{2,3},{3,2},{4,8},{5,9},{6,10},{7,11},{8,4},{9,5},{10,... | collective-permute-start | bytes 24584 | tf_op jit(solution)/shard_map/ppermute | solution.py:313
  8.4 4.2 %collective-permute-start.5 = (f32[4,2,2,128]{3,2,1,0:T(2,128)S(1)}, f32[4,2,2,128]{3,2,1,0:T(2,128)S(1)}, u32[]{:S(2)}, u32[]{:S(2)}) collective-permute-start(f32[4,2,2,128]{3,2,1,0:T(2,128)S(1)} %get-tuple-element.22), channel_id=1, source_target_pairs={{0,4},{1,5},{2,6},{3,7},{4,0},{5,1},{6,2},{7,3},{8,12},{9,13},{10,... | collective-permute-start | bytes 24584 | tf_op jit(solution)/shard_map/ppermute | solution.py:313

commit v17 on v14

--- a/solution.py
+++ b/solution.py
@@ -256,7 +256,9 @@
     return p00, p10, q0
 
 
-def combine_kernel(gathered, field, image_one, image_two, columns_two, propagated, entries):
+def combine_kernel(
+    gathered, field, image_one, image_two, columns_two, propagated, entries, formed, sent
+):
     members, rows, cols, depth = field.shape
     sums = jnp.broadcast_to(jnp.sum(gathered[...], axis=0, keepdims=True), (8, 128))
     g00, g01, g02, g11, g12, g22 = [
@@ -276,18 +278,23 @@
     a2 = e2
     a1 = e1 - e2 * (h00 + h11)
     a0 = e0 - e1 * h00 - e2 * (s01 - h11 * h00)
+    place_j = lax.broadcasted_iota(jnp.int32, (cols, depth), 0)
+    copies = []
+    for member in range(members):
+        b0, b1, b2 = [jnp.broadcast_to(a[member : member + 1], (cols, depth)) for a in (a0, a1, a2)]
+        for row in range(rows):
+            two = jnp.where(place_j == 0, columns_two[member, 0, row : row + 1], image_two[member, row])
+            two = jnp.where(place_j == cols - 1, columns_two[member, 1, row : row + 1], two)
+            formed[member, row] = b0 * field[member, row] + b1 * image_one[member, row] + b2 * two
+        copies.append(pltpu.make_async_copy(formed.at[member], propagated.at[member], sent.at[member]))
+        copies[-1].start()
     lane = lax.broadcasted_iota(jnp.int32, h00.shape, 1)
     table = h21
     for index, entry in enumerate((h00, h10, h01, h11)):
         table = jnp.where(lane == index, entry, table)
     entries[...] = (tau_step * table)[: entries.shape[0], : entries.shape[1]]
-    place_j = lax.broadcasted_iota(jnp.int32, (cols, depth), 0)
-    for member in range(members):
-        b0, b1, b2 = [jnp.broadcast_to(a[member : member + 1], (cols, depth)) for a in (a0, a1, a2)]
-        for row in range(rows):
-            two = jnp.where(place_j == 0, columns_two[member, 0, row : row + 1], image_two[member, row])
-            two = jnp.where(place_j == cols - 1, columns_two[member, 1, row : row + 1], two)
-            propagated[member, row] = b0 * field[member, row] + b1 * image_one[member, row] + b2 * two
+    for copy in copies:
+        copy.wait()
 
 
 def shards(density, rate_table):
@@ -402,7 +409,8 @@
         combine_kernel,
         out_shape=[block, jax.ShapeDtypeStruct((members, 5), jnp.float32)],
         in_specs=[vmem] * 5,
-        out_specs=[vmem, vmem],
+        out_specs=[pl.BlockSpec(memory_space=pl.ANY), vmem],
+        scratch_shapes=[pltpu.VMEM(density.shape, jnp.float32), pltpu.SemaphoreType.DMA((members,))],
         compiler_params=pltpu.CompilerParams(vmem_limit_bytes=8 * 2**20),
         name="combine",
     )(gathered, density, image_one, image_two, columns_two)

time: 26.2 us -> 26.8 us (1.023)
  Pallas kernels: 1.88 us -> 2.47 us
    pallas_call x1, Pallas kernels: 0.83 us -> 1.43 us  [shards(): pl.pallas_call(combine_kernel, out_shape=[block, jax.ShapeDtypeStruct((me...]
where the time goes in v17:
time: 26.8 us; the launch traced here: 26.7 us
  blocking collectives  12.3 us (46%)
  starting transfers between devices  7.83 us (29%)
  waiting for transfers between devices  3.34 us (12%)
  Pallas kernels  2.47 us (9%)
  between operations  0.7 us (3%)
    all_to_all x1, blocking collectives, shards(): gathered = lax.all_to_all(message, ('gy', 'gx'), 0, 0, tiled=True)  12.3 us
    ppermute x6, starting transfers between devices, swap(): return lax.ppermute(value, ('gx', 'gy'), pairs)  7.83 us
    ppermute x6, waiting for transfers between devices, swap(): return lax.ppermute(value, ('gx', 'gy'), pairs)  3.34 us
    pallas_call x1, Pallas kernels, shards(): pl.pallas_call(combine_kernel, out_shape=[block, jax.ShapeDtypeStruct((me...  1.43 us
    pallas_call x1, Pallas kernels, shards(): pl.pallas_call(functools.partial(images_kernel, lattice), out_shape=[bloc...  0.65 us
  transfers between devices with their start and end apart: 6, of which 3 were waited for; matrix products, arithmetic and copies ran while one was open for 0% of the time, Pallas kernels for 3%

profile of v17, /device:TPU:0, one launch (start us, length us, event | category | flops | bytes accessed | tf_op | source)
XLA Modules:
  0.0 26.7 jit_solution(15907677776673463749)
XLA Ops:
  0.6 0.0 copy-start
  0.6 3.0 %collective-permute-start = (f32[4,4,16,128]{3,2,1,0:T(8,128)}, f32[4,4,16,128]{3,2,1,0:T(8,128)S(1)}, u32[]{:S(2)}, u32[]{:S(2)}) collective-permute-start(f32[4,4,16,128]{3,2,1,0:T(8,128)} %field.5), channel_id=1, source_target_pairs={{0,4},{1,5},{2,6},{3,7},{4,0},{5,1},{6,2},{7,3},{8,12},{9,13},{10,... | collective-permute-start | bytes 393224 | tf_op jit(solution)/shard_map/ppermute | solution.py:320
  3.6 0.0 copy-done
  3.7 0.1 collective-permute-start.2
  3.7 0.9 %collective-permute-start.1 = (f32[4,4,2,128]{3,2,1,0:T(2,128)S(1)}, f32[4,4,2,128]{3,2,1,0:T(2,128)S(1)}, u32[]{:S(2)}, u32[]{:S(2)}) collective-permute-start(f32[4,4,2,128]{3,2,1,0:T(2,128)S(1)} %get-tuple-element.15), channel_id=1, source_target_pairs={{0,4},{1,2},{2,1},{3,7},{4,0},{5,6},{6,5},{7,3},{8,12},{9,10},{10,... | collective-permute-start | bytes 49160 | tf_op jit(solution)/shard_map/ppermute | solution.py:320
  4.6 0.3 %collective-permute-done.2.even_y = f32[4,4,2,128]{3,2,1,0:T(2,128)S(1)} collective-permute-done((f32[4,4,2,128]{3,2,1,0:T(2,128)S(1)}, f32[4,4,2,128]{3,2,1,0:T(2,128)S(1)}, u32[]{:S(2)}, u32[]{:S(2)}) %collective-permute-start.2) | collective-permute-done | bytes 16416 | tf_op jit(solution)/shard_map/ppermute | solution.py:320
  4.9 0.5 %collective-permute-start.3 = (f32[4,4,16,128]{3,2,1,0:T(8,128)S(1)}, f32[4,4,16,128]{3,2,1,0:T(8,128)S(1)}, u32[]{:S(2)}, u32[]{:S(2)}) collective-permute-start(f32[4,4,16,128]{3,2,1,0:T(8,128)S(1)} %copy-done), channel_id=1, source_target_pairs={{0,1},{1,0},{2,3},{3,2},{4,8},{5,9},{6,10},{7,11},{8,4},{9,5},{10,... | collective-permute-start | bytes 393224 | tf_op jit(solution)/shard_map/ppermute | solution.py:320
  5.4 2.1 %collective-permute-done.1.odd_y = f32[4,4,2,128]{3,2,1,0:T(2,128)S(1)} collective-permute-done((f32[4,4,2,128]{3,2,1,0:T(2,128)S(1)}, f32[4,4,2,128]{3,2,1,0:T(2,128)S(1)}, u32[]{:S(2)}, u32[]{:S(2)}) %collective-permute-start.1) | collective-permute-done | bytes 16416 | tf_op jit(solution)/shard_map/ppermute | solution.py:320
  7.5 0.0 collective-permute-done.even_x
  7.6 0.0 copy-start.1
  7.6 0.2 collective-permute-start.4
  7.8 3.2 %collective-permute-start.5 = (f32[4,2,2,128]{3,2,1,0:T(2,128)S(1)}, f32[4,2,2,128]{3,2,1,0:T(2,128)S(1)}, u32[]{:S(2)}, u32[]{:S(2)}) collective-permute-start(f32[4,2,2,128]{3,2,1,0:T(2,128)S(1)} %get-tuple-element.28), channel_id=1, source_target_pairs={{0,4},{1,5},{2,6},{3,7},{4,0},{5,1},{6,2},{7,3},{8,12},{9,13},{10,... | collective-permute-start | bytes 24584 | tf_op jit(solution)/shard_map/ppermute | solution.py:320
  11.0 0.0 collective-permute-done.3.odd_x
  11.0 0.0 copy-done.1
  11.0 0.7 %images.1 = (f32[4,4,16,128]{3,2,1,0:T(8,128)S(1)}, f32[4,4,16,128]{3,2,1,0:T(8,128)S(1)}, f32[4,10,8,128]{3,2,1,0:T(8,128)S(1)}, f32[48,128]{1,0:T(8,128)S(1)}) custom-call(f32[4,9]{1,0:T(4,128)S(1)} %copy-done.1, f32[4,4,16,128]{3,2,1,0:T(8,128)S(1)} %copy-done, f32[4,4,16,128]{3,2,1,0:T(8,128)S(1)} %collective-permute-done.even_x, ...), custom_call_target="tpu_custom_call" | custom-call | tf_op jit(solution)/shard_map/images/pallas_call | solution.py:372
  11.6 0.0 collective-permute-done.4.odd_corners
  11.7 0.9 %collective-permute-done.5.even_corners = f32[4,2,2,128]{3,2,1,0:T(2,128)S(1)} collective-permute-done((f32[4,2,2,128]{3,2,1,0:T(2,128)S(1)}, f32[4,2,2,128]{3,2,1,0:T(2,128)S(1)}, u32[]{:S(2)}, u32[]{:S(2)}) %collective-permute-start.5) | collective-permute-done | bytes 8224 | tf_op jit(solution)/shard_map/ppermute | solution.py:320
  12.6 0.4 %corners.1 = (f32[4,2,4,128]{3,2,1,0:T(4,128)S(1)}, f32[32,128]{1,0:T(8,128)S(1)}) custom-call(f32[4,9]{1,0:T(4,128)S(1)} %copy-done.1, f32[4,10,8,128]{3,2,1,0:T(8,128)S(1)} %get-tuple-element.22.lines, f32[4,2,2,128]{3,2,1,0:T(2,128)S(1)} %collective-permute-done.4.odd_corners, f32[4,2,2,128]{3,2,1,0:T(2,128)S(1)} %collective-permute-done.5.even_corners, ...), custom_call_target="tpu_custom_call" | custom-call | tf_op jit(solution)/shard_map/corners/pallas_call | solution.py:390
  13.0 12.3 %all_to_all.11 = f32[32,1,128]{2,1,0:T(1,128)S(1)} all-to-all(f32[32,1,128]{2,1,0:T(1,128)S(1)} %bitcast.5), channel_id=1, replica_groups=mesh['gx'=8,'gy'=4] {'gy','gx'}, dimensions={0} | all-to-all | bytes 32768 | tf_op jit(solution)/shard_map/all_to_all | solution.py:406
  25.3 1.4 %combine.1 = (f32[4,4,16,128]{3,2,1,0:T(8,128)}, f32[4,5]{1,0:T(4,128)}) custom-call(f32[32,128]{1,0:T(8,128)S(1)} %bitcast.4, f32[4,4,16,128]{3,2,1,0:T(8,128)S(1)} %copy-done, f32[4,4,16,128]{3,2,1,0:T(8,128)S(1)} %get-tuple-element.25.image_one, f32[4,4,16,128]{3,2,1,0:T(8,128)S(1)} %get-tuple-element.26.image_two, ...), custom_call_target="tpu_custom_call" | custom-call | tf_op jit(solution)/shard_map/combine/pallas_call | solution.py:408
  (6 shorter events, 0.1 us)
Async XLA Ops:
  0.6 3.0 %copy-start = (f32[4,4,16,128]{3,2,1,0:T(8,128)S(1)}, f32[4,4,16,128]{3,2,1,0:T(8,128)}, u32[]{:S(2)}) copy-start(f32[4,4,16,128]{3,2,1,0:T(8,128)} %field.5) | copy-start | bytes 393220
  0.6 6.9 %collective-permute-start = (f32[4,4,16,128]{3,2,1,0:T(8,128)}, f32[4,4,16,128]{3,2,1,0:T(8,128)S(1)}, u32[]{:S(2)}, u32[]{:S(2)}) collective-permute-start(f32[4,4,16,128]{3,2,1,0:T(8,128)} %field.5), channel_id=1, source_target_pairs={{0,4},{1,5},{2,6},{3,7},{4,0},{5,1},{6,2},{7,3},{8,12},{9,13},{10,... | collective-permute-start | bytes 393224 | tf_op jit(solution)/shard_map/ppermute | solution.py:320
  3.7 1.2 %collective-permute-start.2 = (f32[4,4,2,128]{3,2,1,0:T(2,128)S(1)}, f32[4,4,2,128]{3,2,1,0:T(2,128)S(1)}, u32[]{:S(2)}, u32[]{:S(2)}) collective-permute-start(f32[4,4,2,128]{3,2,1,0:T(2,128)S(1)} %get-tuple-element.16), channel_id=1, source_target_pairs={{0,1},{1,0},{2,3},{3,2},{4,5},{5,4},{6,7},{7,6},{8,9},{9,8},{10,11... | collective-permute-start | bytes 49160 | tf_op jit(solution)/shard_map/ppermute | solution.py:320
  3.7 3.8 %collective-permute-start.1 = (f32[4,4,2,128]{3,2,1,0:T(2,128)S(1)}, f32[4,4,2,128]{3,2,1,0:T(2,128)S(1)}, u32[]{:S(2)}, u32[]{:S(2)}) collective-permute-start(f32[4,4,2,128]{3,2,1,0:T(2,128)S(1)} %get-tuple-element.15), channel_id=1, source_target_pairs={{0,4},{1,2},{2,1},{3,7},{4,0},{5,6},{6,5},{7,3},{8,12},{9,10},{10,... | collective-permute-start | bytes 49160 | tf_op jit(solution)/shard_map/ppermute | solution.py:320
  4.9 6.1 %collective-permute-start.3 = (f32[4,4,16,128]{3,2,1,0:T(8,128)S(1)}, f32[4,4,16,128]{3,2,1,0:T(8,128)S(1)}, u32[]{:S(2)}, u32[]{:S(2)}) collective-permute-start(f32[4,4,16,128]{3,2,1,0:T(8,128)S(1)} %copy-done), channel_id=1, source_target_pairs={{0,1},{1,0},{2,3},{3,2},{4,8},{5,9},{6,10},{7,11},{8,4},{9,5},{10,... | collective-permute-start | bytes 393224 | tf_op jit(solution)/shard_map/ppermute | solution.py:320
  7.6 3.4 %copy-start.1 = (f32[4,9]{1,0:T(4,128)S(1)}, f32[4,9]{1,0:T(4,128)}, u32[]{:S(2)}) copy-start(f32[4,9]{1,0:T(4,128)} %rates.3) | copy-start | bytes 436
  7.6 4.0 %collective-permute-start.4 = (f32[4,2,2,128]{3,2,1,0:T(2,128)S(1)}, f32[4,2,2,128]{3,2,1,0:T(2,128)S(1)}, u32[]{:S(2)}, u32[]{:S(2)}) collective-permute-start(f32[4,2,2,128]{3,2,1,0:T(2,128)S(1)} %get-tuple-element.29), channel_id=1, source_target_pairs={{0,1},{1,0},{2,3},{3,2},{4,8},{5,9},{6,10},{7,11},{8,4},{9,5},{10,... | collective-permute-start | bytes 24584 | tf_op jit(solution)/shard_map/ppermute | solution.py:320
  7.8 4.8 %collective-permute-start.5 = (f32[4,2,2,128]{3,2,1,0:T(2,128)S(1)}, f32[4,2,2,128]{3,2,1,0:T(2,128)S(1)}, u32[]{:S(2)}, u32[]{:S(2)}) collective-permute-start(f32[4,2,2,128]{3,2,1,0:T(2,128)S(1)} %get-tuple-element.28), channel_id=1, source_target_pairs={{0,4},{1,5},{2,6},{3,7},{4,0},{5,1},{6,2},{7,3},{8,12},{9,13},{10,... | collective-permute-start | bytes 24584 | tf_op jit(solution)/shard_map/ppermute | solution.py:320

commit v18 on v17

--- a/solution.py
+++ b/solution.py
@@ -257,7 +257,7 @@
 
 
 def combine_kernel(
-    gathered, field, image_one, image_two, columns_two, propagated, entries, formed, sent
+    gathered, field, image_one, image_two, columns_two, propagated, entries, formed, table, sent
 ):
     members, rows, cols, depth = field.shape
     sums = jnp.broadcast_to(jnp.sum(gathered[...], axis=0, keepdims=True), (8, 128))
@@ -289,10 +289,12 @@
         copies.append(pltpu.make_async_copy(formed.at[member], propagated.at[member], sent.at[member]))
         copies[-1].start()
     lane = lax.broadcasted_iota(jnp.int32, h00.shape, 1)
-    table = h21
+    values = h21
     for index, entry in enumerate((h00, h10, h01, h11)):
-        table = jnp.where(lane == index, entry, table)
-    entries[...] = (tau_step * table)[: entries.shape[0], : entries.shape[1]]
+        values = jnp.where(lane == index, entry, values)
+    table[...] = (tau_step * values)[: table.shape[0], : table.shape[1]]
+    copies.append(pltpu.make_async_copy(table, entries, sent.at[members]))
+    copies[-1].start()
     for copy in copies:
         copy.wait()
 
@@ -409,8 +411,12 @@
         combine_kernel,
         out_shape=[block, jax.ShapeDtypeStruct((members, 5), jnp.float32)],
         in_specs=[vmem] * 5,
-        out_specs=[pl.BlockSpec(memory_space=pl.ANY), vmem],
-        scratch_shapes=[pltpu.VMEM(density.shape, jnp.float32), pltpu.SemaphoreType.DMA((members,))],
+        out_specs=[pl.BlockSpec(memory_space=pl.ANY)] * 2,
+        scratch_shapes=[
+            pltpu.VMEM(density.shape, jnp.float32),
+            pltpu.VMEM((members, 5), jnp.float32),
+            pltpu.SemaphoreType.DMA((members + 1,)),
+        ],
         compiler_params=pltpu.CompilerParams(vmem_limit_bytes=8 * 2**20),
         name="combine",
     )(gathered, density, image_one, image_two, columns_two)

time: 26.8 us -> 26.3 us (0.981)
  Pallas kernels: 2.47 us -> 1.9 us
    pallas_call x1, Pallas kernels: 1.43 us -> 0.86 us  [shards(): pl.pallas_call(combine_kernel, out_shape=[block, jax.ShapeDtypeStruct((me...]
where the time goes in v18:
time: 26.3 us; the launch traced here: 26.1 us
  blocking collectives  12.3 us (47%)
  starting transfers between devices  7.83 us (30%)
  waiting for transfers between devices  3.34 us (13%)
  Pallas kernels  1.9 us (7%)
  between operations  0.7 us (3%)
    all_to_all x1, blocking collectives, shards(): gathered = lax.all_to_all(message, ('gy', 'gx'), 0, 0, tiled=True)  12.3 us
    ppermute x6, starting transfers between devices, swap(): return lax.ppermute(value, ('gx', 'gy'), pairs)  7.83 us
    ppermute x6, waiting for transfers between devices, swap(): return lax.ppermute(value, ('gx', 'gy'), pairs)  3.34 us
    pallas_call x1, Pallas kernels, shards(): pl.pallas_call(combine_kernel, out_shape=[block, jax.ShapeDtypeStruct((me...  0.86 us
    pallas_call x1, Pallas kernels, shards(): pl.pallas_call(functools.partial(images_kernel, lattice), out_shape=[bloc...  0.65 us
  transfers between devices with their start and end apart: 6, of which 3 were waited for; matrix products, arithmetic and copies ran while one was open for 0% of the time, Pallas kernels for 3%

profile of v18, /device:TPU:0, one launch (start us, length us, event | category | flops | bytes accessed | tf_op | source)
XLA Modules:
  0.0 26.1 jit_solution(3074930689487361857)
XLA Ops:
  0.6 0.0 copy-start
  0.6 3.0 %collective-permute-start = (f32[4,4,16,128]{3,2,1,0:T(8,128)}, f32[4,4,16,128]{3,2,1,0:T(8,128)S(1)}, u32[]{:S(2)}, u32[]{:S(2)}) collective-permute-start(f32[4,4,16,128]{3,2,1,0:T(8,128)} %field.5), channel_id=1, source_target_pairs={{0,4},{1,5},{2,6},{3,7},{4,0},{5,1},{6,2},{7,3},{8,12},{9,13},{10,... | collective-permute-start | bytes 393224 | tf_op jit(solution)/shard_map/ppermute | solution.py:322
  3.6 0.0 copy-done
  3.7 0.1 collective-permute-start.2
  3.7 0.9 %collective-permute-start.1 = (f32[4,4,2,128]{3,2,1,0:T(2,128)S(1)}, f32[4,4,2,128]{3,2,1,0:T(2,128)S(1)}, u32[]{:S(2)}, u32[]{:S(2)}) collective-permute-start(f32[4,4,2,128]{3,2,1,0:T(2,128)S(1)} %get-tuple-element.15), channel_id=1, source_target_pairs={{0,4},{1,2},{2,1},{3,7},{4,0},{5,6},{6,5},{7,3},{8,12},{9,10},{10,... | collective-permute-start | bytes 49160 | tf_op jit(solution)/shard_map/ppermute | solution.py:322
  4.6 0.3 %collective-permute-done.2.even_y = f32[4,4,2,128]{3,2,1,0:T(2,128)S(1)} collective-permute-done((f32[4,4,2,128]{3,2,1,0:T(2,128)S(1)}, f32[4,4,2,128]{3,2,1,0:T(2,128)S(1)}, u32[]{:S(2)}, u32[]{:S(2)}) %collective-permute-start.2) | collective-permute-done | bytes 16416 | tf_op jit(solution)/shard_map/ppermute | solution.py:322
  4.9 0.5 %collective-permute-start.3 = (f32[4,4,16,128]{3,2,1,0:T(8,128)S(1)}, f32[4,4,16,128]{3,2,1,0:T(8,128)S(1)}, u32[]{:S(2)}, u32[]{:S(2)}) collective-permute-start(f32[4,4,16,128]{3,2,1,0:T(8,128)S(1)} %copy-done), channel_id=1, source_target_pairs={{0,1},{1,0},{2,3},{3,2},{4,8},{5,9},{6,10},{7,11},{8,4},{9,5},{10,... | collective-permute-start | bytes 393224 | tf_op jit(solution)/shard_map/ppermute | solution.py:322
  5.4 2.1 %collective-permute-done.1.odd_y = f32[4,4,2,128]{3,2,1,0:T(2,128)S(1)} collective-permute-done((f32[4,4,2,128]{3,2,1,0:T(2,128)S(1)}, f32[4,4,2,128]{3,2,1,0:T(2,128)S(1)}, u32[]{:S(2)}, u32[]{:S(2)}) %collective-permute-start.1) | collective-permute-done | bytes 16416 | tf_op jit(solution)/shard_map/ppermute | solution.py:322
  7.5 0.0 collective-permute-done.even_x
  7.6 0.0 copy-start.1
  7.6 0.2 collective-permute-start.4
  7.8 3.2 %collective-permute-start.5 = (f32[4,2,2,128]{3,2,1,0:T(2,128)S(1)}, f32[4,2,2,128]{3,2,1,0:T(2,128)S(1)}, u32[]{:S(2)}, u32[]{:S(2)}) collective-permute-start(f32[4,2,2,128]{3,2,1,0:T(2,128)S(1)} %get-tuple-element.28), channel_id=1, source_target_pairs={{0,4},{1,5},{2,6},{3,7},{4,0},{5,1},{6,2},{7,3},{8,12},{9,13},{10,... | collective-permute-start | bytes 24584 | tf_op jit(solution)/shard_map/ppermute | solution.py:322
  11.0 0.0 collective-permute-done.3.odd_x
  11.0 0.0 copy-done.1
  11.0 0.7 %images.1 = (f32[4,4,16,128]{3,2,1,0:T(8,128)S(1)}, f32[4,4,16,128]{3,2,1,0:T(8,128)S(1)}, f32[4,10,8,128]{3,2,1,0:T(8,128)S(1)}, f32[48,128]{1,0:T(8,128)S(1)}) custom-call(f32[4,9]{1,0:T(4,128)S(1)} %copy-done.1, f32[4,4,16,128]{3,2,1,0:T(8,128)S(1)} %copy-done, f32[4,4,16,128]{3,2,1,0:T(8,128)S(1)} %collective-permute-done.even_x, ...), custom_call_target="tpu_custom_call" | custom-call | tf_op jit(solution)/shard_map/images/pallas_call | solution.py:374
  11.6 0.0 collective-permute-done.4.odd_corners
  11.7 0.9 %collective-permute-done.5.even_corners = f32[4,2,2,128]{3,2,1,0:T(2,128)S(1)} collective-permute-done((f32[4,2,2,128]{3,2,1,0:T(2,128)S(1)}, f32[4,2,2,128]{3,2,1,0:T(2,128)S(1)}, u32[]{:S(2)}, u32[]{:S(2)}) %collective-permute-start.5) | collective-permute-done | bytes 8224 | tf_op jit(solution)/shard_map/ppermute | solution.py:322
  12.6 0.4 %corners.1 = (f32[4,2,4,128]{3,2,1,0:T(4,128)S(1)}, f32[32,128]{1,0:T(8,128)S(1)}) custom-call(f32[4,9]{1,0:T(4,128)S(1)} %copy-done.1, f32[4,10,8,128]{3,2,1,0:T(8,128)S(1)} %get-tuple-element.22.lines, f32[4,2,2,128]{3,2,1,0:T(2,128)S(1)} %collective-permute-done.4.odd_corners, f32[4,2,2,128]{3,2,1,0:T(2,128)S(1)} %collective-permute-done.5.even_corners, ...), custom_call_target="tpu_custom_call" | custom-call | tf_op jit(solution)/shard_map/corners/pallas_call | solution.py:392
  13.0 12.3 %all_to_all.11 = f32[32,1,128]{2,1,0:T(1,128)S(1)} all-to-all(f32[32,1,128]{2,1,0:T(1,128)S(1)} %bitcast.5), channel_id=1, replica_groups=mesh['gx'=8,'gy'=4] {'gy','gx'}, dimensions={0} | all-to-all | bytes 32768 | tf_op jit(solution)/shard_map/all_to_all | solution.py:408
  25.3 0.9 %combine.1 = (f32[4,4,16,128]{3,2,1,0:T(8,128)}, f32[4,5]{1,0:T(4,128)}) custom-call(f32[32,128]{1,0:T(8,128)S(1)} %bitcast.4, f32[4,4,16,128]{3,2,1,0:T(8,128)S(1)} %copy-done, f32[4,4,16,128]{3,2,1,0:T(8,128)S(1)} %get-tuple-element.25.image_one, f32[4,4,16,128]{3,2,1,0:T(8,128)S(1)} %get-tuple-element.26.image_two, ...), custom_call_target="tpu_custom_call" | custom-call | tf_op jit(solution)/shard_map/combine/pallas_call | solution.py:410
  (6 shorter events, 0.1 us)
Async XLA Ops:
  0.6 3.0 %copy-start = (f32[4,4,16,128]{3,2,1,0:T(8,128)S(1)}, f32[4,4,16,128]{3,2,1,0:T(8,128)}, u32[]{:S(2)}) copy-start(f32[4,4,16,128]{3,2,1,0:T(8,128)} %field.5) | copy-start | bytes 393220
  0.6 6.9 %collective-permute-start = (f32[4,4,16,128]{3,2,1,0:T(8,128)}, f32[4,4,16,128]{3,2,1,0:T(8,128)S(1)}, u32[]{:S(2)}, u32[]{:S(2)}) collective-permute-start(f32[4,4,16,128]{3,2,1,0:T(8,128)} %field.5), channel_id=1, source_target_pairs={{0,4},{1,5},{2,6},{3,7},{4,0},{5,1},{6,2},{7,3},{8,12},{9,13},{10,... | collective-permute-start | bytes 393224 | tf_op jit(solution)/shard_map/ppermute | solution.py:322
  3.7 1.2 %collective-permute-start.2 = (f32[4,4,2,128]{3,2,1,0:T(2,128)S(1)}, f32[4,4,2,128]{3,2,1,0:T(2,128)S(1)}, u32[]{:S(2)}, u32[]{:S(2)}) collective-permute-start(f32[4,4,2,128]{3,2,1,0:T(2,128)S(1)} %get-tuple-element.16), channel_id=1, source_target_pairs={{0,1},{1,0},{2,3},{3,2},{4,5},{5,4},{6,7},{7,6},{8,9},{9,8},{10,11... | collective-permute-start | bytes 49160 | tf_op jit(solution)/shard_map/ppermute | solution.py:322
  3.7 3.8 %collective-permute-start.1 = (f32[4,4,2,128]{3,2,1,0:T(2,128)S(1)}, f32[4,4,2,128]{3,2,1,0:T(2,128)S(1)}, u32[]{:S(2)}, u32[]{:S(2)}) collective-permute-start(f32[4,4,2,128]{3,2,1,0:T(2,128)S(1)} %get-tuple-element.15), channel_id=1, source_target_pairs={{0,4},{1,2},{2,1},{3,7},{4,0},{5,6},{6,5},{7,3},{8,12},{9,10},{10,... | collective-permute-start | bytes 49160 | tf_op jit(solution)/shard_map/ppermute | solution.py:322
  4.9 6.1 %collective-permute-start.3 = (f32[4,4,16,128]{3,2,1,0:T(8,128)S(1)}, f32[4,4,16,128]{3,2,1,0:T(8,128)S(1)}, u32[]{:S(2)}, u32[]{:S(2)}) collective-permute-start(f32[4,4,16,128]{3,2,1,0:T(8,128)S(1)} %copy-done), channel_id=1, source_target_pairs={{0,1},{1,0},{2,3},{3,2},{4,8},{5,9},{6,10},{7,11},{8,4},{9,5},{10,... | collective-permute-start | bytes 393224 | tf_op jit(solution)/shard_map/ppermute | solution.py:322
  7.6 3.4 %copy-start.1 = (f32[4,9]{1,0:T(4,128)S(1)}, f32[4,9]{1,0:T(4,128)}, u32[]{:S(2)}) copy-start(f32[4,9]{1,0:T(4,128)} %rates.3) | copy-start | bytes 436
  7.6 4.0 %collective-permute-start.4 = (f32[4,2,2,128]{3,2,1,0:T(2,128)S(1)}, f32[4,2,2,128]{3,2,1,0:T(2,128)S(1)}, u32[]{:S(2)}, u32[]{:S(2)}) collective-permute-start(f32[4,2,2,128]{3,2,1,0:T(2,128)S(1)} %get-tuple-element.29), channel_id=1, source_target_pairs={{0,1},{1,0},{2,3},{3,2},{4,8},{5,9},{6,10},{7,11},{8,4},{9,5},{10,... | collective-permute-start | bytes 24584 | tf_op jit(solution)/shard_map/ppermute | solution.py:322
  7.8 4.8 %collective-permute-start.5 = (f32[4,2,2,128]{3,2,1,0:T(2,128)S(1)}, f32[4,2,2,128]{3,2,1,0:T(2,128)S(1)}, u32[]{:S(2)}, u32[]{:S(2)}) collective-permute-start(f32[4,2,2,128]{3,2,1,0:T(2,128)S(1)} %get-tuple-element.28), channel_id=1, source_target_pairs={{0,4},{1,5},{2,6},{3,7},{4,0},{5,1},{6,2},{7,3},{8,12},{9,13},{10,... | collective-permute-start | bytes 24584 | tf_op jit(solution)/shard_map/ppermute | solution.py:322

commit v19 on v16

--- a/solution.py
+++ b/solution.py
@@ -350,6 +350,7 @@
 
     even_y, for_odd_x = lax.optimization_barrier((even_y, initial if rows == REACH else jnp.where(is_even, initial, last)))
     odd_x = swap("gx", size_x, 1, for_odd_x)
+    even_x, odd_y, even_y = lax.optimization_barrier((even_x, odd_y, even_y))
 
     def corners(first):
         even, odd = even_y[:, first : first + HALF], odd_y[:, first : first + HALF]

time: 26.2 us -> 26.1 us (level)
  local copies, waits for them, and re-layouts: 0.89 us -> 0.02 us
  waiting for transfers between devices: 2.47 us -> 2.86 us
  starting transfers between devices: 7.82 us -> 8.13 us
    unnamed x4, local copies, waits for them, and re-layouts: 0.88 us -> 0.01 us
    ppermute x6, waiting for transfers between devices: 2.47 us -> 2.86 us  [swap(): return lax.ppermute(value, ('gx', 'gy'), pairs)]
    ppermute x6, starting transfers between devices: 7.82 us -> 8.13 us  [swap(): return lax.ppermute(value, ('gx', 'gy'), pairs)]
  transfers between devices with their start and end apart: 6 -> 6, of which waited for: 2 -> 3; matrix products, arithmetic and copies ran while one was open for 0% -> 0% of each run, Pallas kernels for 3% -> 3%
where the time goes in v19:
time: 26.1 us; the launch traced here: 25.9 us
  blocking collectives  12.3 us (47%)
  starting transfers between devices  8.13 us (31%)
  waiting for transfers between devices  2.86 us (11%)
  Pallas kernels  1.88 us (7%)
  between operations  0.7 us (3%)
    all_to_all x1, blocking collectives, shards(): gathered = lax.all_to_all(message, ('gy', 'gx'), 0, 0, tiled=True)  12.3 us
    ppermute x6, starting transfers between devices, swap(): return lax.ppermute(value, ('gx', 'gy'), pairs)  8.13 us
    ppermute x6, waiting for transfers between devices, swap(): return lax.ppermute(value, ('gx', 'gy'), pairs)  2.86 us
    pallas_call x1, Pallas kernels, shards(): pl.pallas_call(combine_kernel, out_shape=[block, jax.ShapeDtypeStruct((me...  0.83 us
    pallas_call x1, Pallas kernels, shards(): pl.pallas_call(functools.partial(images_kernel, lattice), out_shape=[bloc...  0.65 us
  transfers between devices with their start and end apart: 6, of which 3 were waited for; matrix products, arithmetic and copies ran while one was open for 0% of the time, Pallas kernels for 3%

profile of v19, /device:TPU:0, one launch (start us, length us, event | category | flops | bytes accessed | tf_op | source)
XLA Modules:
  0.0 25.9 jit_solution(5447921737753730154)
XLA Ops:
  0.6 0.0 copy-start
  0.6 3.0 %collective-permute-start = (f32[4,4,16,128]{3,2,1,0:T(8,128)}, f32[4,4,16,128]{3,2,1,0:T(8,128)S(1)}, u32[]{:S(2)}, u32[]{:S(2)}) collective-permute-start(f32[4,4,16,128]{3,2,1,0:T(8,128)} %field.5), channel_id=1, source_target_pairs={{0,4},{1,5},{2,6},{3,7},{4,0},{5,1},{6,2},{7,3},{8,12},{9,13},{10,... | collective-permute-start | bytes 393224 | tf_op jit(solution)/shard_map/ppermute | solution.py:313
  3.6 0.0 copy-done
  3.7 0.1 collective-permute-start.2
  3.7 1.6 %collective-permute-start.1 = (f32[4,4,2,128]{3,2,1,0:T(2,128)S(1)}, f32[4,4,2,128]{3,2,1,0:T(2,128)S(1)}, u32[]{:S(2)}, u32[]{:S(2)}) collective-permute-start(f32[4,4,2,128]{3,2,1,0:T(2,128)S(1)} %get-tuple-element.15), channel_id=1, source_target_pairs={{0,3},{1,2},{2,1},{3,0},{4,7},{5,6},{6,5},{7,4},{8,11},{9,10},{10,... | collective-permute-start | bytes 49160 | tf_op jit(solution)/shard_map/ppermute | solution.py:313
  5.4 0.0 collective-permute-done.2.even_y
  5.4 0.1 collective-permute-start.3
  5.4 1.5 %collective-permute-done.1.odd_y = f32[4,4,2,128]{3,2,1,0:T(2,128)S(1)} collective-permute-done((f32[4,4,2,128]{3,2,1,0:T(2,128)S(1)}, f32[4,4,2,128]{3,2,1,0:T(2,128)S(1)}, u32[]{:S(2)}, u32[]{:S(2)}) %collective-permute-start.1) | collective-permute-done | bytes 16416 | tf_op jit(solution)/shard_map/ppermute | solution.py:313
  7.0 0.4 %collective-permute-done.even_x = f32[4,4,16,128]{3,2,1,0:T(8,128)S(1)} collective-permute-done((f32[4,4,16,128]{3,2,1,0:T(8,128)}, f32[4,4,16,128]{3,2,1,0:T(8,128)S(1)}, u32[]{:S(2)}, u32[]{:S(2)}) %collective-permute-start) | collective-permute-done | bytes 131104 | tf_op jit(solution)/shard_map/ppermute | solution.py:313
  7.4 0.0 copy-start.1
  7.4 0.2 collective-permute-start.4
  7.6 3.2 %collective-permute-start.5 = (f32[4,2,2,128]{3,2,1,0:T(2,128)S(1)}, f32[4,2,2,128]{3,2,1,0:T(2,128)S(1)}, u32[]{:S(2)}, u32[]{:S(2)}) collective-permute-start(f32[4,2,2,128]{3,2,1,0:T(2,128)S(1)} %get-tuple-element.28), channel_id=1, source_target_pairs={{0,4},{1,5},{2,6},{3,7},{4,0},{5,1},{6,2},{7,3},{8,12},{9,13},{10,... | collective-permute-start | bytes 24584 | tf_op jit(solution)/shard_map/ppermute | solution.py:313
  10.8 0.0 collective-permute-done.3.odd_x
  10.8 0.0 copy-done.1
  10.8 0.7 %images.1 = (f32[4,4,16,128]{3,2,1,0:T(8,128)S(1)}, f32[4,4,16,128]{3,2,1,0:T(8,128)S(1)}, f32[4,10,8,128]{3,2,1,0:T(8,128)S(1)}, f32[48,128]{1,0:T(8,128)S(1)}) custom-call(f32[4,9]{1,0:T(4,128)S(1)} %copy-done.1, f32[4,4,16,128]{3,2,1,0:T(8,128)S(1)} %copy-done, f32[4,4,16,128]{3,2,1,0:T(8,128)S(1)} %collective-permute-done.even_x, ...), custom_call_target="tpu_custom_call" | custom-call | tf_op jit(solution)/shard_map/images/pallas_call | solution.py:365
  11.5 0.0 collective-permute-done.4.odd_corners
  11.5 0.9 %collective-permute-done.5.even_corners = f32[4,2,2,128]{3,2,1,0:T(2,128)S(1)} collective-permute-done((f32[4,2,2,128]{3,2,1,0:T(2,128)S(1)}, f32[4,2,2,128]{3,2,1,0:T(2,128)S(1)}, u32[]{:S(2)}, u32[]{:S(2)}) %collective-permute-start.5) | collective-permute-done | bytes 8224 | tf_op jit(solution)/shard_map/ppermute | solution.py:313
  12.4 0.4 %corners.1 = (f32[4,2,4,128]{3,2,1,0:T(4,128)S(1)}, f32[32,128]{1,0:T(8,128)S(1)}) custom-call(f32[4,9]{1,0:T(4,128)S(1)} %copy-done.1, f32[4,10,8,128]{3,2,1,0:T(8,128)S(1)} %get-tuple-element.22.lines, f32[4,2,2,128]{3,2,1,0:T(2,128)S(1)} %collective-permute-done.4.odd_corners, f32[4,2,2,128]{3,2,1,0:T(2,128)S(1)} %collective-permute-done.5.even_corners, ...), custom_call_target="tpu_custom_call" | custom-call | tf_op jit(solution)/shard_map/corners/pallas_call | solution.py:383
  12.8 12.3 %all_to_all.11 = f32[32,1,128]{2,1,0:T(1,128)S(1)} all-to-all(f32[32,1,128]{2,1,0:T(1,128)S(1)} %bitcast.5), channel_id=1, replica_groups=mesh['gx'=8,'gy'=4] {'gy','gx'}, dimensions={0} | all-to-all | bytes 32768 | tf_op jit(solution)/shard_map/all_to_all | solution.py:399
  25.1 0.8 %combine.1 = (f32[4,4,16,128]{3,2,1,0:T(8,128)}, f32[4,5]{1,0:T(4,128)}) custom-call(f32[32,128]{1,0:T(8,128)S(1)} %bitcast.4, f32[4,4,16,128]{3,2,1,0:T(8,128)S(1)} %copy-done, f32[4,4,16,128]{3,2,1,0:T(8,128)S(1)} %get-tuple-element.25.image_one, f32[4,4,16,128]{3,2,1,0:T(8,128)S(1)} %get-tuple-element.26.image_two, ...), custom_call_target="tpu_custom_call" | custom-call | tf_op jit(solution)/shard_map/combine/pallas_call | solution.py:401
  (6 shorter events, 0.1 us)
Async XLA Ops:
  0.6 3.0 %copy-start = (f32[4,4,16,128]{3,2,1,0:T(8,128)S(1)}, f32[4,4,16,128]{3,2,1,0:T(8,128)}, u32[]{:S(2)}) copy-start(f32[4,4,16,128]{3,2,1,0:T(8,128)} %field.5) | copy-start | bytes 393220
  0.6 6.7 %collective-permute-start = (f32[4,4,16,128]{3,2,1,0:T(8,128)}, f32[4,4,16,128]{3,2,1,0:T(8,128)S(1)}, u32[]{:S(2)}, u32[]{:S(2)}) collective-permute-start(f32[4,4,16,128]{3,2,1,0:T(8,128)} %field.5), channel_id=1, source_target_pairs={{0,4},{1,5},{2,6},{3,7},{4,0},{5,1},{6,2},{7,3},{8,12},{9,13},{10,... | collective-permute-start | bytes 393224 | tf_op jit(solution)/shard_map/ppermute | solution.py:313
  3.7 1.7 %collective-permute-start.2 = (f32[4,4,2,128]{3,2,1,0:T(2,128)S(1)}, f32[4,4,2,128]{3,2,1,0:T(2,128)S(1)}, u32[]{:S(2)}, u32[]{:S(2)}) collective-permute-start(f32[4,4,2,128]{3,2,1,0:T(2,128)S(1)} %get-tuple-element.16), channel_id=1, source_target_pairs={{0,1},{1,0},{2,3},{3,2},{4,5},{5,4},{6,7},{7,6},{8,9},{9,8},{10,11... | collective-permute-start | bytes 49160 | tf_op jit(solution)/shard_map/ppermute | solution.py:313
  3.7 3.2 %collective-permute-start.1 = (f32[4,4,2,128]{3,2,1,0:T(2,128)S(1)}, f32[4,4,2,128]{3,2,1,0:T(2,128)S(1)}, u32[]{:S(2)}, u32[]{:S(2)}) collective-permute-start(f32[4,4,2,128]{3,2,1,0:T(2,128)S(1)} %get-tuple-element.15), channel_id=1, source_target_pairs={{0,3},{1,2},{2,1},{3,0},{4,7},{5,6},{6,5},{7,4},{8,11},{9,10},{10,... | collective-permute-start | bytes 49160 | tf_op jit(solution)/shard_map/ppermute | solution.py:313
  5.4 5.4 %collective-permute-start.3 = (f32[4,4,16,128]{3,2,1,0:T(8,128)S(1)}, f32[4,4,16,128]{3,2,1,0:T(8,128)S(1)}, u32[]{:S(2)}, u32[]{:S(2)}) collective-permute-start(f32[4,4,16,128]{3,2,1,0:T(8,128)S(1)} %copy-done), channel_id=1, source_target_pairs={{0,1},{1,0},{2,3},{3,2},{4,8},{5,9},{6,10},{7,11},{8,4},{9,5},{10,... | collective-permute-start | bytes 393224 | tf_op jit(solution)/shard_map/ppermute | solution.py:313
  7.4 3.4 %copy-start.1 = (f32[4,9]{1,0:T(4,128)S(1)}, f32[4,9]{1,0:T(4,128)}, u32[]{:S(2)}) copy-start(f32[4,9]{1,0:T(4,128)} %rates.3) | copy-start | bytes 436
  7.4 4.0 %collective-permute-start.4 = (f32[4,2,2,128]{3,2,1,0:T(2,128)S(1)}, f32[4,2,2,128]{3,2,1,0:T(2,128)S(1)}, u32[]{:S(2)}, u32[]{:S(2)}) collective-permute-start(f32[4,2,2,128]{3,2,1,0:T(2,128)S(1)} %get-tuple-element.29), channel_id=1, source_target_pairs={{0,1},{1,0},{2,3},{3,2},{4,8},{5,9},{6,10},{7,11},{8,4},{9,5},{10,... | collective-permute-start | bytes 24584 | tf_op jit(solution)/shard_map/ppermute | solution.py:313
  7.6 4.8 %collective-permute-start.5 = (f32[4,2,2,128]{3,2,1,0:T(2,128)S(1)}, f32[4,2,2,128]{3,2,1,0:T(2,128)S(1)}, u32[]{:S(2)}, u32[]{:S(2)}) collective-permute-start(f32[4,2,2,128]{3,2,1,0:T(2,128)S(1)} %get-tuple-element.28), channel_id=1, source_target_pairs={{0,4},{1,5},{2,6},{3,7},{4,0},{5,1},{6,2},{7,3},{8,12},{9,13},{10,... | collective-permute-start | bytes 24584 | tf_op jit(solution)/shard_map/ppermute | solution.py:313

commit v20 on v19

--- a/solution.py
+++ b/solution.py
@@ -396,7 +396,8 @@
         name="corners",
     )(rate_table, lines, odd_corners, even_corners, parts)
 
-    gathered = lax.all_to_all(message, ("gy", "gx"), 0, 0, tiled=True)
+    order = [0] + [i for i in range(devices - 1, 0, -1)]
+    gathered = lax.all_to_all(message, ("gx", "gy"), 0, 0, axis_index_groups=[order], tiled=True)
 
     return pl.pallas_call(
         combine_kernel,

time: 26.1 us -> 26.1 us (level)
  no operation moved by 1% of the time
where the time goes in v20:
time: 26.1 us; the launch traced here: 25.9 us
  blocking collectives  12.3 us (47%)
  starting transfers between devices  8.13 us (31%)
  waiting for transfers between devices  2.86 us (11%)
  Pallas kernels  1.88 us (7%)
  between operations  0.7 us (3%)
    all_to_all x1, blocking collectives, shards(): lax.all_to_all(message, ('gx', 'gy'), 0, 0, axis_index_groups=[order], ti...  12.3 us
    ppermute x6, starting transfers between devices, swap(): return lax.ppermute(value, ('gx', 'gy'), pairs)  8.13 us
    ppermute x6, waiting for transfers between devices, swap(): return lax.ppermute(value, ('gx', 'gy'), pairs)  2.86 us
    pallas_call x1, Pallas kernels, shards(): pl.pallas_call(combine_kernel, out_shape=[block, jax.ShapeDtypeStruct((me...  0.83 us
    pallas_call x1, Pallas kernels, shards(): pl.pallas_call(functools.partial(images_kernel, lattice), out_shape=[bloc...  0.65 us
  transfers between devices with their start and end apart: 6, of which 3 were waited for; matrix products, arithmetic and copies ran while one was open for 0% of the time, Pallas kernels for 3%

profile of v20, /device:TPU:0, one launch (start us, length us, event | category | flops | bytes accessed | tf_op | source)
XLA Modules:
  0.0 25.9 jit_solution(7157565610460967250)
XLA Ops:
  0.6 0.0 copy-start
  0.6 3.0 %collective-permute-start = (f32[4,4,16,128]{3,2,1,0:T(8,128)}, f32[4,4,16,128]{3,2,1,0:T(8,128)S(1)}, u32[]{:S(2)}, u32[]{:S(2)}) collective-permute-start(f32[4,4,16,128]{3,2,1,0:T(8,128)} %field.5), channel_id=1, source_target_pairs={{0,4},{1,5},{2,6},{3,7},{4,0},{5,1},{6,2},{7,3},{8,12},{9,13},{10,... | collective-permute-start | bytes 393224 | tf_op jit(solution)/shard_map/ppermute | solution.py:313
  3.6 0.0 copy-done
  3.7 0.1 collective-permute-start.2
  3.7 1.6 %collective-permute-start.1 = (f32[4,4,2,128]{3,2,1,0:T(2,128)S(1)}, f32[4,4,2,128]{3,2,1,0:T(2,128)S(1)}, u32[]{:S(2)}, u32[]{:S(2)}) collective-permute-start(f32[4,4,2,128]{3,2,1,0:T(2,128)S(1)} %get-tuple-element.15), channel_id=1, source_target_pairs={{0,3},{1,2},{2,1},{3,0},{4,7},{5,6},{6,5},{7,4},{8,11},{9,10},{10,... | collective-permute-start | bytes 49160 | tf_op jit(solution)/shard_map/ppermute | solution.py:313
  5.4 0.0 collective-permute-done.2.even_y
  5.4 0.1 collective-permute-start.3
  5.4 1.5 %collective-permute-done.1.odd_y = f32[4,4,2,128]{3,2,1,0:T(2,128)S(1)} collective-permute-done((f32[4,4,2,128]{3,2,1,0:T(2,128)S(1)}, f32[4,4,2,128]{3,2,1,0:T(2,128)S(1)}, u32[]{:S(2)}, u32[]{:S(2)}) %collective-permute-start.1) | collective-permute-done | bytes 16416 | tf_op jit(solution)/shard_map/ppermute | solution.py:313
  7.0 0.4 %collective-permute-done.even_x = f32[4,4,16,128]{3,2,1,0:T(8,128)S(1)} collective-permute-done((f32[4,4,16,128]{3,2,1,0:T(8,128)}, f32[4,4,16,128]{3,2,1,0:T(8,128)S(1)}, u32[]{:S(2)}, u32[]{:S(2)}) %collective-permute-start) | collective-permute-done | bytes 131104 | tf_op jit(solution)/shard_map/ppermute | solution.py:313
  7.4 0.0 copy-start.1
  7.4 0.2 collective-permute-start.4
  7.6 3.2 %collective-permute-start.5 = (f32[4,2,2,128]{3,2,1,0:T(2,128)S(1)}, f32[4,2,2,128]{3,2,1,0:T(2,128)S(1)}, u32[]{:S(2)}, u32[]{:S(2)}) collective-permute-start(f32[4,2,2,128]{3,2,1,0:T(2,128)S(1)} %get-tuple-element.28), channel_id=1, source_target_pairs={{0,4},{1,5},{2,6},{3,7},{4,0},{5,1},{6,2},{7,3},{8,12},{9,13},{10,... | collective-permute-start | bytes 24584 | tf_op jit(solution)/shard_map/ppermute | solution.py:313
  10.8 0.0 collective-permute-done.3.odd_x
  10.8 0.0 copy-done.1
  10.8 0.7 %images.1 = (f32[4,4,16,128]{3,2,1,0:T(8,128)S(1)}, f32[4,4,16,128]{3,2,1,0:T(8,128)S(1)}, f32[4,10,8,128]{3,2,1,0:T(8,128)S(1)}, f32[48,128]{1,0:T(8,128)S(1)}) custom-call(f32[4,9]{1,0:T(4,128)S(1)} %copy-done.1, f32[4,4,16,128]{3,2,1,0:T(8,128)S(1)} %copy-done, f32[4,4,16,128]{3,2,1,0:T(8,128)S(1)} %collective-permute-done.even_x, ...), custom_call_target="tpu_custom_call" | custom-call | tf_op jit(solution)/shard_map/images/pallas_call | solution.py:365
  11.5 0.0 collective-permute-done.4.odd_corners
  11.5 0.9 %collective-permute-done.5.even_corners = f32[4,2,2,128]{3,2,1,0:T(2,128)S(1)} collective-permute-done((f32[4,2,2,128]{3,2,1,0:T(2,128)S(1)}, f32[4,2,2,128]{3,2,1,0:T(2,128)S(1)}, u32[]{:S(2)}, u32[]{:S(2)}) %collective-permute-start.5) | collective-permute-done | bytes 8224 | tf_op jit(solution)/shard_map/ppermute | solution.py:313
  12.4 0.4 %corners.1 = (f32[4,2,4,128]{3,2,1,0:T(4,128)S(1)}, f32[32,128]{1,0:T(8,128)S(1)}) custom-call(f32[4,9]{1,0:T(4,128)S(1)} %copy-done.1, f32[4,10,8,128]{3,2,1,0:T(8,128)S(1)} %get-tuple-element.22.lines, f32[4,2,2,128]{3,2,1,0:T(2,128)S(1)} %collective-permute-done.4.odd_corners, f32[4,2,2,128]{3,2,1,0:T(2,128)S(1)} %collective-permute-done.5.even_corners, ...), custom_call_target="tpu_custom_call" | custom-call | tf_op jit(solution)/shard_map/corners/pallas_call | solution.py:383
  12.8 12.3 %all_to_all.11 = f32[32,1,128]{2,1,0:T(1,128)S(1)} all-to-all(f32[32,1,128]{2,1,0:T(1,128)S(1)} %bitcast.5), channel_id=1, replica_groups={{0,31,30,29,28,27,26,25,24,23,22,21,20,19,18,17,16,15,14,13,12,11,10,9,..., dimensions={0} | all-to-all | bytes 32768 | tf_op jit(solution)/shard_map/all_to_all | solution.py:400
  25.1 0.8 %combine.1 = (f32[4,4,16,128]{3,2,1,0:T(8,128)}, f32[4,5]{1,0:T(4,128)}) custom-call(f32[32,128]{1,0:T(8,128)S(1)} %bitcast.4, f32[4,4,16,128]{3,2,1,0:T(8,128)S(1)} %copy-done, f32[4,4,16,128]{3,2,1,0:T(8,128)S(1)} %get-tuple-element.25.image_one, f32[4,4,16,128]{3,2,1,0:T(8,128)S(1)} %get-tuple-element.26.image_two, ...), custom_call_target="tpu_custom_call" | custom-call | tf_op jit(solution)/shard_map/combine/pallas_call | solution.py:402
  (6 shorter events, 0.1 us)
Async XLA Ops:
  0.6 3.0 %copy-start = (f32[4,4,16,128]{3,2,1,0:T(8,128)S(1)}, f32[4,4,16,128]{3,2,1,0:T(8,128)}, u32[]{:S(2)}) copy-start(f32[4,4,16,128]{3,2,1,0:T(8,128)} %field.5) | copy-start | bytes 393220
  0.6 6.7 %collective-permute-start = (f32[4,4,16,128]{3,2,1,0:T(8,128)}, f32[4,4,16,128]{3,2,1,0:T(8,128)S(1)}, u32[]{:S(2)}, u32[]{:S(2)}) collective-permute-start(f32[4,4,16,128]{3,2,1,0:T(8,128)} %field.5), channel_id=1, source_target_pairs={{0,4},{1,5},{2,6},{3,7},{4,0},{5,1},{6,2},{7,3},{8,12},{9,13},{10,... | collective-permute-start | bytes 393224 | tf_op jit(solution)/shard_map/ppermute | solution.py:313
  3.7 1.7 %collective-permute-start.2 = (f32[4,4,2,128]{3,2,1,0:T(2,128)S(1)}, f32[4,4,2,128]{3,2,1,0:T(2,128)S(1)}, u32[]{:S(2)}, u32[]{:S(2)}) collective-permute-start(f32[4,4,2,128]{3,2,1,0:T(2,128)S(1)} %get-tuple-element.16), channel_id=1, source_target_pairs={{0,1},{1,0},{2,3},{3,2},{4,5},{5,4},{6,7},{7,6},{8,9},{9,8},{10,11... | collective-permute-start | bytes 49160 | tf_op jit(solution)/shard_map/ppermute | solution.py:313
  3.7 3.2 %collective-permute-start.1 = (f32[4,4,2,128]{3,2,1,0:T(2,128)S(1)}, f32[4,4,2,128]{3,2,1,0:T(2,128)S(1)}, u32[]{:S(2)}, u32[]{:S(2)}) collective-permute-start(f32[4,4,2,128]{3,2,1,0:T(2,128)S(1)} %get-tuple-element.15), channel_id=1, source_target_pairs={{0,3},{1,2},{2,1},{3,0},{4,7},{5,6},{6,5},{7,4},{8,11},{9,10},{10,... | collective-permute-start | bytes 49160 | tf_op jit(solution)/shard_map/ppermute | solution.py:313
  5.4 5.4 %collective-permute-start.3 = (f32[4,4,16,128]{3,2,1,0:T(8,128)S(1)}, f32[4,4,16,128]{3,2,1,0:T(8,128)S(1)}, u32[]{:S(2)}, u32[]{:S(2)}) collective-permute-start(f32[4,4,16,128]{3,2,1,0:T(8,128)S(1)} %copy-done), channel_id=1, source_target_pairs={{0,1},{1,0},{2,3},{3,2},{4,8},{5,9},{6,10},{7,11},{8,4},{9,5},{10,... | collective-permute-start | bytes 393224 | tf_op jit(solution)/shard_map/ppermute | solution.py:313
  7.4 3.4 %copy-start.1 = (f32[4,9]{1,0:T(4,128)S(1)}, f32[4,9]{1,0:T(4,128)}, u32[]{:S(2)}) copy-start(f32[4,9]{1,0:T(4,128)} %rates.3) | copy-start | bytes 436
  7.4 4.0 %collective-permute-start.4 = (f32[4,2,2,128]{3,2,1,0:T(2,128)S(1)}, f32[4,2,2,128]{3,2,1,0:T(2,128)S(1)}, u32[]{:S(2)}, u32[]{:S(2)}) collective-permute-start(f32[4,2,2,128]{3,2,1,0:T(2,128)S(1)} %get-tuple-element.29), channel_id=1, source_target_pairs={{0,1},{1,0},{2,3},{3,2},{4,8},{5,9},{6,10},{7,11},{8,4},{9,5},{10,... | collective-permute-start | bytes 24584 | tf_op jit(solution)/shard_map/ppermute | solution.py:313
  7.6 4.8 %collective-permute-start.5 = (f32[4,2,2,128]{3,2,1,0:T(2,128)S(1)}, f32[4,2,2,128]{3,2,1,0:T(2,128)S(1)}, u32[]{:S(2)}, u32[]{:S(2)}) collective-permute-start(f32[4,2,2,128]{3,2,1,0:T(2,128)S(1)} %get-tuple-element.28), channel_id=1, source_target_pairs={{0,4},{1,5},{2,6},{3,7},{4,0},{5,1},{6,2},{7,3},{8,12},{9,13},{10,... | collective-permute-start | bytes 24584 | tf_op jit(solution)/shard_map/ppermute | solution.py:313

commit v21 on v16

--- a/solution.py
+++ b/solution.py
@@ -350,6 +350,7 @@
 
     even_y, for_odd_x = lax.optimization_barrier((even_y, initial if rows == REACH else jnp.where(is_even, initial, last)))
     odd_x = swap("gx", size_x, 1, for_odd_x)
+    odd_y, even_y, even_x = lax.optimization_barrier((odd_y, even_y, even_x))
 
     def corners(first):
         even, odd = even_y[:, first : first + HALF], odd_y[:, first : first + HALF]

time: 26.2 us -> 26.1 us (level)
  local copies, waits for them, and re-layouts: 0.89 us -> 0.02 us
  waiting for transfers between devices: 2.47 us -> 2.86 us
  starting transfers between devices: 7.82 us -> 8.13 us
    unnamed x4, local copies, waits for them, and re-layouts: 0.88 us -> 0.01 us
    ppermute x6, waiting for transfers between devices: 2.47 us -> 2.86 us  [swap(): return lax.ppermute(value, ('gx', 'gy'), pairs)]
    ppermute x6, starting transfers between devices: 7.82 us -> 8.13 us  [swap(): return lax.ppermute(value, ('gx', 'gy'), pairs)]
  transfers between devices with their start and end apart: 6 -> 6, of which waited for: 2 -> 3; matrix products, arithmetic and copies ran while one was open for 0% -> 0% of each run, Pallas kernels for 3% -> 3%
where the time goes in v21:
time: 26.1 us; the launch traced here: 25.9 us
  blocking collectives  12.3 us (47%)
  starting transfers between devices  8.13 us (31%)
  waiting for transfers between devices  2.86 us (11%)
  Pallas kernels  1.88 us (7%)
  between operations  0.7 us (3%)
    all_to_all x1, blocking collectives, shards(): gathered = lax.all_to_all(message, ('gy', 'gx'), 0, 0, tiled=True)  12.3 us
    ppermute x6, starting transfers between devices, swap(): return lax.ppermute(value, ('gx', 'gy'), pairs)  8.13 us
    ppermute x6, waiting for transfers between devices, swap(): return lax.ppermute(value, ('gx', 'gy'), pairs)  2.86 us
    pallas_call x1, Pallas kernels, shards(): pl.pallas_call(combine_kernel, out_shape=[block, jax.ShapeDtypeStruct((me...  0.83 us
    pallas_call x1, Pallas kernels, shards(): pl.pallas_call(functools.partial(images_kernel, lattice), out_shape=[bloc...  0.65 us
  transfers between devices with their start and end apart: 6, of which 3 were waited for; matrix products, arithmetic and copies ran while one was open for 0% of the time, Pallas kernels for 3%

profile of v21, /device:TPU:0, one launch (start us, length us, event | category | flops | bytes accessed | tf_op | source)
XLA Modules:
  0.0 25.9 jit_solution(5447921737753730154)
XLA Ops:
  0.6 0.0 copy-start
  0.6 3.0 %collective-permute-start.2 = (f32[4,4,16,128]{3,2,1,0:T(8,128)}, f32[4,4,16,128]{3,2,1,0:T(8,128)S(1)}, u32[]{:S(2)}, u32[]{:S(2)}) collective-permute-start(f32[4,4,16,128]{3,2,1,0:T(8,128)} %field.5), channel_id=1, source_target_pairs={{0,4},{1,5},{2,6},{3,7},{4,0},{5,1},{6,2},{7,3},{8,12},{9,13},{10,... | collective-permute-start | bytes 393224 | tf_op jit(solution)/shard_map/ppermute | solution.py:313
  3.6 0.0 copy-done
  3.7 0.1 collective-permute-start.1
  3.7 1.6 %collective-permute-start = (f32[4,4,2,128]{3,2,1,0:T(2,128)S(1)}, f32[4,4,2,128]{3,2,1,0:T(2,128)S(1)}, u32[]{:S(2)}, u32[]{:S(2)}) collective-permute-start(f32[4,4,2,128]{3,2,1,0:T(2,128)S(1)} %get-tuple-element.15), channel_id=1, source_target_pairs={{0,3},{1,2},{2,1},{3,0},{4,7},{5,6},{6,5},{7,4},{8,11},{9,10},{10,... | collective-permute-start | bytes 49160 | tf_op jit(solution)/shard_map/ppermute | solution.py:313
  5.4 0.0 collective-permute-done.1.even_y
  5.4 0.1 collective-permute-start.3
  5.4 1.5 %collective-permute-done.odd_y = f32[4,4,2,128]{3,2,1,0:T(2,128)S(1)} collective-permute-done((f32[4,4,2,128]{3,2,1,0:T(2,128)S(1)}, f32[4,4,2,128]{3,2,1,0:T(2,128)S(1)}, u32[]{:S(2)}, u32[]{:S(2)}) %collective-permute-start) | collective-permute-done | bytes 16416 | tf_op jit(solution)/shard_map/ppermute | solution.py:313
  7.0 0.4 %collective-permute-done.2.even_x = f32[4,4,16,128]{3,2,1,0:T(8,128)S(1)} collective-permute-done((f32[4,4,16,128]{3,2,1,0:T(8,128)}, f32[4,4,16,128]{3,2,1,0:T(8,128)S(1)}, u32[]{:S(2)}, u32[]{:S(2)}) %collective-permute-start.2) | collective-permute-done | bytes 131104 | tf_op jit(solution)/shard_map/ppermute | solution.py:313
  7.4 0.0 copy-start.1
  7.4 0.2 collective-permute-start.4
  7.6 3.2 %collective-permute-start.5 = (f32[4,2,2,128]{3,2,1,0:T(2,128)S(1)}, f32[4,2,2,128]{3,2,1,0:T(2,128)S(1)}, u32[]{:S(2)}, u32[]{:S(2)}) collective-permute-start(f32[4,2,2,128]{3,2,1,0:T(2,128)S(1)} %get-tuple-element.28), channel_id=1, source_target_pairs={{0,4},{1,5},{2,6},{3,7},{4,0},{5,1},{6,2},{7,3},{8,12},{9,13},{10,... | collective-permute-start | bytes 24584 | tf_op jit(solution)/shard_map/ppermute | solution.py:313
  10.8 0.0 collective-permute-done.3.odd_x
  10.8 0.0 copy-done.1
  10.8 0.7 %images.1 = (f32[4,4,16,128]{3,2,1,0:T(8,128)S(1)}, f32[4,4,16,128]{3,2,1,0:T(8,128)S(1)}, f32[4,10,8,128]{3,2,1,0:T(8,128)S(1)}, f32[48,128]{1,0:T(8,128)S(1)}) custom-call(f32[4,9]{1,0:T(4,128)S(1)} %copy-done.1, f32[4,4,16,128]{3,2,1,0:T(8,128)S(1)} %copy-done, f32[4,4,16,128]{3,2,1,0:T(8,128)S(1)} %collective-permute-done.2.even_x, ...), custom_call_target="tpu_custom_call" | custom-call | tf_op jit(solution)/shard_map/images/pallas_call | solution.py:365
  11.5 0.0 collective-permute-done.4.odd_corners
  11.5 0.9 %collective-permute-done.5.even_corners = f32[4,2,2,128]{3,2,1,0:T(2,128)S(1)} collective-permute-done((f32[4,2,2,128]{3,2,1,0:T(2,128)S(1)}, f32[4,2,2,128]{3,2,1,0:T(2,128)S(1)}, u32[]{:S(2)}, u32[]{:S(2)}) %collective-permute-start.5) | collective-permute-done | bytes 8224 | tf_op jit(solution)/shard_map/ppermute | solution.py:313
  12.4 0.4 %corners.1 = (f32[4,2,4,128]{3,2,1,0:T(4,128)S(1)}, f32[32,128]{1,0:T(8,128)S(1)}) custom-call(f32[4,9]{1,0:T(4,128)S(1)} %copy-done.1, f32[4,10,8,128]{3,2,1,0:T(8,128)S(1)} %get-tuple-element.22.lines, f32[4,2,2,128]{3,2,1,0:T(2,128)S(1)} %collective-permute-done.4.odd_corners, f32[4,2,2,128]{3,2,1,0:T(2,128)S(1)} %collective-permute-done.5.even_corners, ...), custom_call_target="tpu_custom_call" | custom-call | tf_op jit(solution)/shard_map/corners/pallas_call | solution.py:383
  12.8 12.3 %all_to_all.11 = f32[32,1,128]{2,1,0:T(1,128)S(1)} all-to-all(f32[32,1,128]{2,1,0:T(1,128)S(1)} %bitcast.5), channel_id=1, replica_groups=mesh['gx'=8,'gy'=4] {'gy','gx'}, dimensions={0} | all-to-all | bytes 32768 | tf_op jit(solution)/shard_map/all_to_all | solution.py:399
  25.1 0.8 %combine.1 = (f32[4,4,16,128]{3,2,1,0:T(8,128)}, f32[4,5]{1,0:T(4,128)}) custom-call(f32[32,128]{1,0:T(8,128)S(1)} %bitcast.4, f32[4,4,16,128]{3,2,1,0:T(8,128)S(1)} %copy-done, f32[4,4,16,128]{3,2,1,0:T(8,128)S(1)} %get-tuple-element.25.image_one, f32[4,4,16,128]{3,2,1,0:T(8,128)S(1)} %get-tuple-element.26.image_two, ...), custom_call_target="tpu_custom_call" | custom-call | tf_op jit(solution)/shard_map/combine/pallas_call | solution.py:401
  (6 shorter events, 0.1 us)
Async XLA Ops:
  0.6 3.0 %copy-start = (f32[4,4,16,128]{3,2,1,0:T(8,128)S(1)}, f32[4,4,16,128]{3,2,1,0:T(8,128)}, u32[]{:S(2)}) copy-start(f32[4,4,16,128]{3,2,1,0:T(8,128)} %field.5) | copy-start | bytes 393220
  0.6 6.7 %collective-permute-start.2 = (f32[4,4,16,128]{3,2,1,0:T(8,128)}, f32[4,4,16,128]{3,2,1,0:T(8,128)S(1)}, u32[]{:S(2)}, u32[]{:S(2)}) collective-permute-start(f32[4,4,16,128]{3,2,1,0:T(8,128)} %field.5), channel_id=1, source_target_pairs={{0,4},{1,5},{2,6},{3,7},{4,0},{5,1},{6,2},{7,3},{8,12},{9,13},{10,... | collective-permute-start | bytes 393224 | tf_op jit(solution)/shard_map/ppermute | solution.py:313
  3.7 1.7 %collective-permute-start.1 = (f32[4,4,2,128]{3,2,1,0:T(2,128)S(1)}, f32[4,4,2,128]{3,2,1,0:T(2,128)S(1)}, u32[]{:S(2)}, u32[]{:S(2)}) collective-permute-start(f32[4,4,2,128]{3,2,1,0:T(2,128)S(1)} %get-tuple-element.16), channel_id=1, source_target_pairs={{0,1},{1,0},{2,3},{3,2},{4,5},{5,4},{6,7},{7,6},{8,9},{9,8},{10,11... | collective-permute-start | bytes 49160 | tf_op jit(solution)/shard_map/ppermute | solution.py:313
  3.7 3.2 %collective-permute-start = (f32[4,4,2,128]{3,2,1,0:T(2,128)S(1)}, f32[4,4,2,128]{3,2,1,0:T(2,128)S(1)}, u32[]{:S(2)}, u32[]{:S(2)}) collective-permute-start(f32[4,4,2,128]{3,2,1,0:T(2,128)S(1)} %get-tuple-element.15), channel_id=1, source_target_pairs={{0,3},{1,2},{2,1},{3,0},{4,7},{5,6},{6,5},{7,4},{8,11},{9,10},{10,... | collective-permute-start | bytes 49160 | tf_op jit(solution)/shard_map/ppermute | solution.py:313
  5.4 5.4 %collective-permute-start.3 = (f32[4,4,16,128]{3,2,1,0:T(8,128)S(1)}, f32[4,4,16,128]{3,2,1,0:T(8,128)S(1)}, u32[]{:S(2)}, u32[]{:S(2)}) collective-permute-start(f32[4,4,16,128]{3,2,1,0:T(8,128)S(1)} %copy-done), channel_id=1, source_target_pairs={{0,1},{1,0},{2,3},{3,2},{4,8},{5,9},{6,10},{7,11},{8,4},{9,5},{10,... | collective-permute-start | bytes 393224 | tf_op jit(solution)/shard_map/ppermute | solution.py:313
  7.4 3.4 %copy-start.1 = (f32[4,9]{1,0:T(4,128)S(1)}, f32[4,9]{1,0:T(4,128)}, u32[]{:S(2)}) copy-start(f32[4,9]{1,0:T(4,128)} %rates.3) | copy-start | bytes 436
  7.4 4.0 %collective-permute-start.4 = (f32[4,2,2,128]{3,2,1,0:T(2,128)S(1)}, f32[4,2,2,128]{3,2,1,0:T(2,128)S(1)}, u32[]{:S(2)}, u32[]{:S(2)}) collective-permute-start(f32[4,2,2,128]{3,2,1,0:T(2,128)S(1)} %get-tuple-element.29), channel_id=1, source_target_pairs={{0,1},{1,0},{2,3},{3,2},{4,8},{5,9},{6,10},{7,11},{8,4},{9,5},{10,... | collective-permute-start | bytes 24584 | tf_op jit(solution)/shard_map/ppermute | solution.py:313
  7.6 4.8 %collective-permute-start.5 = (f32[4,2,2,128]{3,2,1,0:T(2,128)S(1)}, f32[4,2,2,128]{3,2,1,0:T(2,128)S(1)}, u32[]{:S(2)}, u32[]{:S(2)}) collective-permute-start(f32[4,2,2,128]{3,2,1,0:T(2,128)S(1)} %get-tuple-element.28), channel_id=1, source_target_pairs={{0,4},{1,5},{2,6},{3,7},{4,0},{5,1},{6,2},{7,3},{8,12},{9,13},{10,... | collective-permute-start | bytes 24584 | tf_op jit(solution)/shard_map/ppermute | solution.py:313
